TPU v7x, 32 devices: a whole 2x2x4 slice. The times are simulated.
32 devices in a mesh: dp: 16 (over z, x, core), mp: 2 (over y).
Axes of the slice: x: 2, y: 2, z: 4, core: 2. Of those that a mesh axis runs over, the one named last changes fastest.
Arguments:
- frames: bfloat16 [49152, 1024], P(('dp', 'mp')), may hold values from -6 to 6
- text_states: bfloat16 [4096, 768], P('dp'), may hold values from -6 to 6
- clip_lengths: int32 [32, 4], P('dp'), may hold values from 1 to 768, 1536 in all within a row
- text_lengths: int32 [32, 4], P('dp'), may hold values from 1 to 64, 128 in all within a row
- cotangent: bfloat16 [49152, 1024], P(('dp', 'mp')), may hold values from -6 to 6
- self_gain: float32 [1024], replicated, may hold values from 0.25 to 1.75
- self_shift: float32 [1024], replicated, may hold values from -2 to 2
- self_query: bfloat16 [1024, 1024], P(None, 'mp'), may hold values from -0.1875 to 0.1875
- self_key: bfloat16 [1024, 1024], P(None, 'mp'), may hold values from -0.1875 to 0.1875
- self_value: bfloat16 [1024, 1024], P(None, 'mp'), may hold values from -0.1875 to 0.1875
- self_out: bfloat16 [1024, 1024], P('mp'), may hold values from -0.75 to 0.75
- cross_gain: float32 [1024], replicated, may hold values from 0.25 to 1.75
- cross_shift: float32 [1024], replicated, may hold values from -2 to 2
- cross_query: bfloat16 [1024, 1024], P(None, 'mp'), may hold values from -0.1875 to 0.1875
- cross_key: bfloat16 [1024, 1024], P(None, 'mp'), may hold values from -0.1875 to 0.1875
- cross_value: bfloat16 [1024, 1024], P(None, 'mp'), may hold values from -0.1875 to 0.1875
- cross_out: bfloat16 [1024, 1024], P('mp'), may hold values from -0.5 to 0.5
- text_weight: bfloat16 [768, 1024], P(None, 'mp'), may hold values from -0.21875 to 0.21875
- text_bias: float32 [1024], P('mp'), may hold values from -3 to 3
- feed_gain: float32 [1024], replicated, may hold values from 0.25 to 1.75
- feed_shift: float32 [1024], replicated, may hold values from -2 to 2
- feed_in: bfloat16 [1024, 4096], P(None, 'mp'), may hold values from -0.1875 to 0.1875
- feed_out: bfloat16 [4096, 1024], P('mp'), may hold values from -0.09375 to 0.09375
Outputs:
- output: bfloat16 [49152, 1024], P(('dp', 'mp'))
- frames_grad: float32 [49152, 1024], P(('dp', 'mp'))
- text_grad: float32 [4096, 768], P('dp')
- self_gain_grad: float32 [1024], replicated
- self_shift_grad: float32 [1024], replicated
- self_query_grad: float32 [1024, 1024], P(None, 'mp')
- self_key_grad: float32 [1024, 1024], P(None, 'mp')
- self_value_grad: float32 [1024, 1024], P(None, 'mp')
- self_out_grad: float32 [1024, 1024], P('mp')
- cross_gain_grad: float32 [1024], replicated
- cross_shift_grad: float32 [1024], replicated
- cross_query_grad: float32 [1024, 1024], P(None, 'mp')
- cross_key_grad: float32 [1024, 1024], P(None, 'mp')
- cross_value_grad: float32 [1024, 1024], P(None, 'mp')
- cross_out_grad: float32 [1024, 1024], P('mp')
- text_weight_grad: float32 [768, 1024], P(None, 'mp')
- text_bias_grad: float32 [1024], P('mp')
- feed_gain_grad: float32 [1024], replicated
- feed_shift_grad: float32 [1024], replicated
- feed_in_grad: float32 [1024, 4096], P(None, 'mp')
- feed_out_grad: float32 [4096, 1024], P('mp')
Inputs may be any that keep to these rules, and one draw needn't show every extreme that they name: `clip_lengths`: each row's 4 clip lengths sum to 1536, and its longest clip has exactly 768 frames. `text_lengths`: each row's 4 prompt lengths sum to 128, and its longest prompt has exactly 64 tokens; prompt k belongs to clip k of the same row.
All inputs are finite; a program needn't handle non-finite values.
Results may differ from a plain program's by a relative error of at most 0.022.
Values may be sent and summed in bfloat16 or wider, within the bound.
A program may use at most 512 MiB of HBM per device.

v0:
```python
from functools import reduce

import jax
import jax.numpy as jnp
from jax import lax
from jax.sharding import PartitionSpec as P

HEAD_DIM = 64
ROW_LEN = 1536
TXT_ROW = 128


EPSILON = 1e-05
MASKED = -1e30


def product(left_side, right_side):
    return jnp.dot(left_side, right_side, preferred_element_type=jnp.float32)


def against(left_side, right_side):
    return lax.dot_general(
        left_side, right_side, (((1,), (1,)), ((), ())), preferred_element_type=jnp.float32
    )


def outer_sum(left_side, right_side):
    return lax.dot_general(
        left_side, right_side, (((0,), (0,)), ((), ())), preferred_element_type=jnp.float32
    )


def exact_gelu(tensor):
    return jax.nn.gelu(tensor, approximate=False)


def segment_ids(lengths, positions):
    bounds = jnp.cumsum(lengths, axis=-1)
    places = jnp.arange(positions, dtype=jnp.int32)
    return jnp.sum((places[None, :, None] >= bounds[:, None, :]).astype(jnp.int32), axis=-1)


def split_heads(tensor, row_count):
    return tensor.reshape(
        row_count, tensor.shape[0] // row_count, tensor.shape[1] // HEAD_DIM, HEAD_DIM
    )


def norm_parts(tensor):
    average = jnp.mean(tensor, axis=-1, keepdims=True)
    centered = tensor - average
    inverse = lax.rsqrt(jnp.mean(centered * centered, axis=-1, keepdims=True) + EPSILON)
    return (centered * inverse, inverse)


def norm_back(gradient, standard, inverse, norm_gain):
    scaled = gradient * norm_gain
    first_mean = jnp.mean(scaled, axis=-1, keepdims=True)
    second_mean = jnp.mean(scaled * standard, axis=-1, keepdims=True)
    return (
        inverse * (scaled - first_mean - standard * second_mean),
        jnp.sum(gradient * standard, axis=0),
        jnp.sum(gradient, axis=0),
    )


def spread_rows(tensor):
    return lax.all_gather(tensor, "mp", axis=0, tiled=True)


def spread_cotangent(tensor):
    return lax.all_gather(tensor, "mp", axis=0, tiled=True)


def branch_sum(left_side, right_side):
    return lax.psum_scatter(product(left_side, right_side), "mp", scatter_dimension=0, tiled=True)


def input_grads(factor_pairs):
    partials = [against(left_side, right_side) for left_side, right_side in factor_pairs]
    return lax.psum_scatter(reduce(jnp.add, partials), "mp", scatter_dimension=0, tiled=True)


def attend_forward(queries, key_heads, values, allowed):
    scores = jnp.einsum(
        "rqhd,rkhd->rhqk", queries, key_heads, preferred_element_type=jnp.float32
    ) * HEAD_DIM ** (-0.5)
    scores = jnp.where(allowed[:, None], scores, MASKED)
    row_max = jnp.max(scores, axis=-1, keepdims=True)
    shifted = jnp.exp(scores - row_max)
    totals = jnp.sum(shifted, axis=-1, keepdims=True)
    soft_weights = (shifted / totals).astype(jnp.bfloat16)
    context = jnp.einsum(
        "rhqk,rkhd->rqhd", soft_weights, values, preferred_element_type=jnp.float32
    )
    return (context, row_max + jnp.log(totals))


def attend_back(queries, key_heads, values, allowed, log_totals, grad_context):
    score_scale = HEAD_DIM ** (-0.5)
    scores = (
        jnp.einsum("rqhd,rkhd->rhqk", queries, key_heads, preferred_element_type=jnp.float32)
        * score_scale
    )
    scores = jnp.where(allowed[:, None], scores, MASKED)
    soft_weights = jnp.exp(scores - log_totals)
    grad_soft = jnp.einsum(
        "rqhd,rkhd->rhqk", grad_context, values, preferred_element_type=jnp.float32
    )
    row_inner = jnp.sum(grad_soft * soft_weights, axis=-1, keepdims=True)
    grad_scores = (soft_weights * (grad_soft - row_inner)).astype(jnp.bfloat16)
    grad_query = (
        jnp.einsum("rhqk,rkhd->rqhd", grad_scores, key_heads, preferred_element_type=jnp.float32)
        * score_scale
    )
    grad_keys = (
        jnp.einsum("rhqk,rqhd->rkhd", grad_scores, queries, preferred_element_type=jnp.float32)
        * score_scale
    )
    grad_values = jnp.einsum(
        "rhqk,rqhd->rkhd",
        soft_weights.astype(jnp.bfloat16),
        grad_context,
        preferred_element_type=jnp.float32,
    )
    return (grad_query, grad_keys, grad_values)


def self_allowed(segments, start_at, stop_at):
    places = jnp.arange(stop_at, dtype=jnp.int32)
    same_clip = segments[:, start_at:stop_at, None] == segments[:, None, :stop_at]
    return same_clip & (places[start_at:stop_at, None] >= places[None, :])[None]


def self_forward(queries, key_heads, values, segments):
    block_size = min(512, queries.shape[1])
    contexts = []
    log_totals = []
    for start_at in range(0, queries.shape[1], block_size):
        stop_at = start_at + block_size
        context, log_total = attend_forward(
            queries[:, start_at:stop_at],
            key_heads[:, :stop_at],
            values[:, :stop_at],
            self_allowed(segments, start_at, stop_at),
        )
        contexts.append(context)
        log_totals.append(log_total)
    return (jnp.concatenate(contexts, axis=1), jnp.concatenate(log_totals, axis=2))


def self_back(queries, key_heads, values, segments, log_totals, grad_context):
    block_size = min(512, queries.shape[1])
    query_parts = []
    grad_keys = jnp.zeros(key_heads.shape, jnp.float32)
    grad_values = jnp.zeros(values.shape, jnp.float32)
    for start_at in range(0, queries.shape[1], block_size):
        stop_at = start_at + block_size
        grad_query, key_part, value_part = attend_back(
            queries[:, start_at:stop_at],
            key_heads[:, :stop_at],
            values[:, :stop_at],
            self_allowed(segments, start_at, stop_at),
            log_totals[:, :, start_at:stop_at],
            grad_context[:, start_at:stop_at],
        )
        query_parts.append(grad_query)
        grad_keys = grad_keys.at[:, :stop_at].add(key_part)
        grad_values = grad_values.at[:, :stop_at].add(value_part)
    return (jnp.concatenate(query_parts, axis=1), grad_keys, grad_values)


def body(
    frames,
    text_states,
    clip_lengths,
    text_lengths,
    cotangent,
    self_gain,
    self_shift,
    self_query,
    self_key,
    self_value,
    self_out,
    cross_gain,
    cross_shift,
    cross_query,
    cross_key,
    cross_value,
    cross_out,
    text_weight,
    text_bias,
    feed_gain,
    feed_shift,
    feed_in,
    feed_out,
):
    row_count = clip_lengths.shape[0]
    clip_segs = segment_ids(clip_lengths, ROW_LEN)
    text_segs = segment_ids(text_lengths, TXT_ROW)
    residual = frames.astype(jnp.float32)
    self_standard, self_inverse = norm_parts(residual)
    self_rows = spread_rows((self_standard * self_gain + self_shift).astype(jnp.bfloat16))
    self_queries = product(self_rows, self_query).astype(jnp.bfloat16)
    self_keys = product(self_rows, self_key).astype(jnp.bfloat16)
    self_values = product(self_rows, self_value).astype(jnp.bfloat16)
    self_context, self_logs = self_forward(
        split_heads(self_queries, row_count),
        split_heads(self_keys, row_count),
        split_heads(self_values, row_count),
        clip_segs,
    )
    self_context = self_context.reshape(self_queries.shape).astype(jnp.bfloat16)
    middle = residual + branch_sum(self_context, self_out)
    cross_standard, cross_inverse = norm_parts(middle)
    cross_rows = spread_rows((cross_standard * cross_gain + cross_shift).astype(jnp.bfloat16))
    text_part = (product(text_states, text_weight) + text_bias).astype(jnp.bfloat16)
    text_full = lax.all_gather(text_part, "mp", axis=1, tiled=True)
    cross_queries = product(cross_rows, cross_query).astype(jnp.bfloat16)
    cross_keys = product(text_full, cross_key).astype(jnp.bfloat16)
    cross_values = product(text_full, cross_value).astype(jnp.bfloat16)
    cross_allowed = clip_segs[:, :, None] == text_segs[:, None, :]
    cross_context, cross_logs = attend_forward(
        split_heads(cross_queries, row_count),
        split_heads(cross_keys, row_count),
        split_heads(cross_values, row_count),
        cross_allowed,
    )
    cross_context = cross_context.reshape(cross_queries.shape).astype(jnp.bfloat16)
    after_cross = middle + branch_sum(cross_context, cross_out)
    feed_standard, feed_inverse = norm_parts(after_cross)
    feed_normed = (feed_standard * feed_gain + feed_shift).astype(jnp.bfloat16)
    feed_rows = spread_rows(feed_normed)
    hidden = product(feed_rows, feed_in)
    active, gelu_back = jax.vjp(exact_gelu, hidden)
    active = active.astype(jnp.bfloat16)
    output = after_cross + branch_sum(active, feed_out)
    grad_output = cotangent.astype(jnp.float32)
    feed_cotangent = grad_output.astype(jnp.bfloat16)
    grad_rows = spread_cotangent(feed_cotangent)
    feed_out_grad = outer_sum(active, grad_rows)
    grad_hidden = gelu_back(against(grad_rows, feed_out))[0].astype(jnp.bfloat16)
    feed_in_grad = outer_sum(feed_rows, grad_hidden)
    grad_feed_normed = input_grads(((grad_hidden, feed_in),))
    grad_norm, feed_gain_grad, feed_shift_grad = norm_back(
        grad_feed_normed, feed_standard, feed_inverse, feed_gain
    )
    grad_after = grad_output + grad_norm
    cross_cotangent = spread_cotangent(grad_after.astype(jnp.bfloat16))
    cross_out_grad = outer_sum(cross_context, cross_cotangent)
    grad_context = against(cross_cotangent, cross_out).astype(jnp.bfloat16)
    grad_queries, grad_keys, grad_values = attend_back(
        split_heads(cross_queries, row_count),
        split_heads(cross_keys, row_count),
        split_heads(cross_values, row_count),
        cross_allowed,
        cross_logs,
        split_heads(grad_context, row_count),
    )
    grad_queries = grad_queries.reshape(cross_queries.shape).astype(jnp.bfloat16)
    grad_keys = grad_keys.reshape(cross_keys.shape).astype(jnp.bfloat16)
    grad_values = grad_values.reshape(cross_values.shape).astype(jnp.bfloat16)
    cross_query_grad = outer_sum(cross_rows, grad_queries)
    cross_key_grad = outer_sum(text_full, grad_keys)
    cross_value_grad = outer_sum(text_full, grad_values)
    grad_text_full = against(grad_keys, cross_key) + against(grad_values, cross_value)
    grad_text = lax.psum_scatter(
        grad_text_full.astype(jnp.bfloat16), "mp", scatter_dimension=1, tiled=True
    )
    text_weight_grad = outer_sum(text_states, grad_text)
    text_bias_grad = jnp.sum(grad_text.astype(jnp.float32), axis=0)
    text_grad = lax.psum(against(grad_text, text_weight).astype(jnp.bfloat16), "mp").astype(
        jnp.float32
    )
    grad_cross_normed = input_grads(((grad_queries, cross_query),))
    grad_norm, cross_gain_grad, cross_shift_grad = norm_back(
        grad_cross_normed, cross_standard, cross_inverse, cross_gain
    )
    grad_middle = grad_after + grad_norm
    self_cotangent = spread_cotangent(grad_middle.astype(jnp.bfloat16))
    self_out_grad = outer_sum(self_context, self_cotangent)
    grad_context = against(self_cotangent, self_out).astype(jnp.bfloat16)
    grad_queries, grad_keys, grad_values = self_back(
        split_heads(self_queries, row_count),
        split_heads(self_keys, row_count),
        split_heads(self_values, row_count),
        clip_segs,
        self_logs,
        split_heads(grad_context, row_count),
    )
    grad_queries = grad_queries.reshape(self_queries.shape).astype(jnp.bfloat16)
    grad_keys = grad_keys.reshape(self_keys.shape).astype(jnp.bfloat16)
    grad_values = grad_values.reshape(self_values.shape).astype(jnp.bfloat16)
    self_query_grad = outer_sum(self_rows, grad_queries)
    self_key_grad = outer_sum(self_rows, grad_keys)
    self_value_grad = outer_sum(self_rows, grad_values)
    grad_self_normed = input_grads(
        ((grad_queries, self_query), (grad_keys, self_key), (grad_values, self_value))
    )
    grad_norm, self_gain_grad, self_shift_grad = norm_back(
        grad_self_normed, self_standard, self_inverse, self_gain
    )
    frames_grad = grad_middle + grad_norm
    (
        self_query_grad,
        self_key_grad,
        self_value_grad,
        self_out_grad,
        cross_query_grad,
        cross_key_grad,
        cross_value_grad,
        cross_out_grad,
        text_weight_grad,
        text_bias_grad,
        feed_in_grad,
        feed_out_grad,
    ) = (
        lax.psum(self_query_grad.astype(jnp.bfloat16), "dp").astype(jnp.float32),
        lax.psum(self_key_grad.astype(jnp.bfloat16), "dp").astype(jnp.float32),
        lax.psum(self_value_grad.astype(jnp.bfloat16), "dp").astype(jnp.float32),
        lax.psum(self_out_grad.astype(jnp.bfloat16), "dp").astype(jnp.float32),
        lax.psum(cross_query_grad.astype(jnp.bfloat16), "dp").astype(jnp.float32),
        lax.psum(cross_key_grad.astype(jnp.bfloat16), "dp").astype(jnp.float32),
        lax.psum(cross_value_grad.astype(jnp.bfloat16), "dp").astype(jnp.float32),
        lax.psum(cross_out_grad.astype(jnp.bfloat16), "dp").astype(jnp.float32),
        lax.psum(text_weight_grad.astype(jnp.bfloat16), "dp").astype(jnp.float32),
        lax.psum(text_bias_grad.astype(jnp.bfloat16), "dp").astype(jnp.float32),
        lax.psum(feed_in_grad.astype(jnp.bfloat16), "dp").astype(jnp.float32),
        lax.psum(feed_out_grad.astype(jnp.bfloat16), "dp").astype(jnp.float32),
    )
    (
        self_gain_grad,
        self_shift_grad,
        cross_gain_grad,
        cross_shift_grad,
        feed_gain_grad,
        feed_shift_grad,
    ) = lax.psum(
        (
            self_gain_grad,
            self_shift_grad,
            cross_gain_grad,
            cross_shift_grad,
            feed_gain_grad,
            feed_shift_grad,
        ),
        ("dp", "mp"),
    )
    return (
        output.astype(jnp.bfloat16),
        frames_grad,
        text_grad,
        self_gain_grad,
        self_shift_grad,
        self_query_grad,
        self_key_grad,
        self_value_grad,
        self_out_grad,
        cross_gain_grad,
        cross_shift_grad,
        cross_query_grad,
        cross_key_grad,
        cross_value_grad,
        cross_out_grad,
        text_weight_grad,
        text_bias_grad,
        feed_gain_grad,
        feed_shift_grad,
        feed_in_grad,
        feed_out_grad,
    )


def solution(mesh):
    return jax.shard_map(
        body,
        mesh=mesh,
        in_specs=(
            P(("dp", "mp"), None),
            P("dp", None),
            P("dp", None),
            P("dp", None),
            P(("dp", "mp"), None),
            P(),
            P(),
            P(None, "mp"),
            P(None, "mp"),
            P(None, "mp"),
            P("mp", None),
            P(),
            P(),
            P(None, "mp"),
            P(None, "mp"),
            P(None, "mp"),
            P("mp", None),
            P(None, "mp"),
            P("mp"),
            P(),
            P(),
            P(None, "mp"),
            P("mp", None),
        ),
        out_specs=(
            P(("dp", "mp"), None),
            P(("dp", "mp"), None),
            P("dp", None),
            P(),
            P(),
            P(None, "mp"),
            P(None, "mp"),
            P(None, "mp"),
            P("mp", None),
            P(),
            P(),
            P(None, "mp"),
            P(None, "mp"),
            P(None, "mp"),
            P("mp", None),
            P(None, "mp"),
            P("mp"),
            P(),
            P(),
            P(None, "mp"),
            P("mp", None),
        ),
        check_vma=False,
    )
```

profile of v0, /device:TPU:0, one launch (start us, length us, event | category | flops | bytes accessed | tf_op | source)
XLA Modules:
  0.0 2520.9 jit_solution(7759455378200438289)
XLA Ops:
  21.9 77.3 %all-gather.7.cloned.1.call-done = bf16[3072,1024]{1,0:T(8,128)(2,1)} async-done(((bf16[1536,1024]{1,0:T(8,128)(2,1)}), bf16[3072,1024]{1,0:T(8,128)(2,1)}) %all-gather.7.cloned.1.call-update) | async-done | bytes 6291472 | tf_op jit(solution)/shard_map/all_gather | solution.py:68
  251.0 20.7 fusion.114
  271.6 21.4 fusion
  324.2 144.6 %reduce-scatter.8.cloned.1.call-done = f32[1536,1024]{1,0:T(8,128)} async-done(((f32[3072,1024]{1,0:T(8,128)}), f32[1536,1024]{1,0:T(8,128)}) %reduce-scatter.8.cloned.1.call-update) | async-done | bytes 6291472 | tf_op jit(solution)/shard_map/reduce_scatter | solution.py:76
  491.8 67.2 %all-gather.9.cloned.1.call-done = bf16[3072,1024]{1,0:T(8,128)(2,1)} async-done(((bf16[1536,1024]{1,0:T(8,128)(2,1)}), bf16[3072,1024]{1,0:T(8,128)(2,1)}) %all-gather.9.cloned.1.call-update) | async-done | bytes 6291472 | tf_op jit(solution)/shard_map/all_gather | solution.py:68
  607.9 144.4 %reduce-scatter.10.cloned.1.call-done = f32[1536,1024]{1,0:T(8,128)} async-done(((f32[3072,1024]{1,0:T(8,128)}), f32[1536,1024]{1,0:T(8,128)}) %reduce-scatter.10.cloned.1.call-update) | async-done | bytes 6291472 | tf_op jit(solution)/shard_map/reduce_scatter | solution.py:76
  764.0 79.9 %all-gather.11.cloned.1.call-done = bf16[3072,1024]{1,0:T(8,128)(2,1)} async-done(((bf16[1536,1024]{1,0:T(8,128)(2,1)}), bf16[3072,1024]{1,0:T(8,128)(2,1)}) %all-gather.11.cloned.1.call-update) | async-done | bytes 6291472 | tf_op jit(solution)/shard_map/all_gather | solution.py:68
  843.9 69.7 %multiply_convert_fusion.2 = (bf16[3072,2048]{1,0:T(8,128)(2,1)}, f32[3072,2048]{1,0:T(8,128)}, f32[3072,2048]{1,0:T(8,128)}) fusion(bf16[3072,1024]{1,0:T(8,128)(2,1)} %all-gather.11.cloned.1.call-done, bf16[1024,2048]{1,0:T(8,128)(2,1)} %param.60), kind=kOutput, calls=%fused_computation.21 | convolution fusion | flops 13293846528 | bytes 73400320 | tf_op jit(solution)/shard_map/dot_general | solution.py:18
  925.7 33.4 %add_convert_fusion = bf16[3072,2048]{1,0:T(8,128)(2,1)} fusion(f32[3072,2048]{1,0:T(8,128)} %get-tuple-element.206, f32[3072,2048]{1,0:T(8,128)} %get-tuple-element.229, bf16[3072,1024]{1,0:T(8,128)(2,1)} %all-gather.13.cloned.1.call-done, bf16[2048,1024]{1,0:T(8,128)(2,1)} %param.61), kind=kOutput, calls=%fused_computation.20 | convolution fusion | flops 12972982272 | bytes 73400320 | tf_op jit(solution)/shard_map/dot_general | solution.py:22
  996.5 125.2 %reduce-scatter.14.cloned.1.call-done = f32[1536,1024]{1,0:T(8,128)} async-done(((f32[3072,1024]{1,0:T(8,128)}), f32[1536,1024]{1,0:T(8,128)}) %reduce-scatter.14.cloned.1.call-update) | async-done | bytes 6291472 | tf_op jit(solution)/shard_map/reduce_scatter | solution.py:81
  1128.3 140.1 %reduce-scatter.12.cloned.1.call-done = f32[1536,1024]{1,0:T(8,128)} async-done(((f32[3072,1024]{1,0:T(8,128)}), f32[1536,1024]{1,0:T(8,128)}) %reduce-scatter.12.cloned.1.call-update) | async-done | bytes 6291472 | tf_op jit(solution)/shard_map/reduce_scatter | solution.py:76
  1281.9 80.4 %all-gather.15.cloned.1.call-done = bf16[3072,1024]{1,0:T(8,128)(2,1)} async-done(((bf16[1536,1024]{1,0:T(8,128)(2,1)}), bf16[3072,1024]{1,0:T(8,128)(2,1)}) %all-gather.15.cloned.1.call-update) | async-done | bytes 6291472 | tf_op jit(solution)/shard_map/all_gather | solution.py:72
  1433.3 129.5 %reduce-scatter.16.cloned.1.call-done = f32[1536,1024]{1,0:T(8,128)} async-done(((f32[3072,1024]{1,0:T(8,128)}), f32[1536,1024]{1,0:T(8,128)}) %reduce-scatter.16.cloned.1.call-update) | async-done | bytes 6291472 | tf_op jit(solution)/shard_map/reduce_scatter | solution.py:81
  1597.7 20.4 convolution_convert_fusion.7
  1634.5 27.6 %all-gather.17.cloned.1.call-done = bf16[3072,1024]{1,0:T(8,128)(2,1)} async-done(((bf16[1536,1024]{1,0:T(8,128)(2,1)}), bf16[3072,1024]{1,0:T(8,128)(2,1)}) %all-gather.17.cloned.1.call-update) | async-done | bytes 6291472 | tf_op jit(solution)/shard_map/all_gather | solution.py:72
  1735.3 23.2 multiply_reduce_fusion.1
  1775.1 32.6 %multiply_reduce_fusion = (f32[2,8,512]{2,1,0:T(8,128)S(1)}, f32[2,8,512,1536]{3,2,1,0:T(8,128)}) fusion(f32[2,8,512,1536]{3,2,1,0:T(8,128)} %get-tuple-element.222, f32[2,8,512]{2,1,0:T(8,128)S(1)} %copy-done.28, bf16[2,512,8,64]{1,3,2,0:T(8,128)(2,1)S(1)} %copy.198, bf16[2,1536,8,64]{1,3,2,0:T(8,128)(2,1)} %copy.123), kind=kOutput, calls=%fused_computation.1 | convolution fusion | flops 1648353280 | bytes 104923136 | tf_op jit(solution)/shard_map/rqhd,rkhd->rhqk/dot_general | solution.py:107
  1807.7 22.5 fusion.42
  1841.4 27.7 %multiply_convert_fusion.1 = bf16[2,8,512,1024]{3,2,1,0:T(8,128)(2,1)} fusion(f32[2,8,512,1024]{3,2,1,0:T(8,128)} %get-tuple-element.235, f32[2,8,512,1024]{3,2,1,0:T(8,128)} %get-tuple-element.224, f32[2,8,512]{2,1,0:T(8,128)S(1)} %get-tuple-element.234, f32[2,8,512]{2,1,0:T(8,128)S(1)} %log_add_fusion.2), kind=kLoop, calls=%fused_computation.9 | loop fusion | flops 33554432 | bytes 83951616 | tf_op jit(solution)/shard_map/convert_element_type | solution.py:111
  1893.8 40.9 %multiply_convert_fusion = bf16[2,8,512,1536]{3,2,1,0:T(8,128)(2,1)} fusion(f32[2,8,512,1536]{3,2,1,0:T(8,128)} %get-tuple-element.233, f32[2,8,512,1536]{3,2,1,0:T(8,128)} %get-tuple-element.222, f32[2,8,512]{2,1,0:T(8,128)S(1)} %get-tuple-element.232, f32[2,8,512]{2,1,0:T(8,128)S(1)} %copy-done.28), kind=kLoop, calls=%fused_computation | loop fusion | flops 50331648 | bytes 125894656 | tf_op jit(solution)/shard_map/convert_element_type | solution.py:111
  2027.4 35.2 %psum.147 = bf16[512]{0:T(512)(128)(2,1)S(1)} all-reduce(bf16[512]{0:T(512)(128)(2,1)S(1)} %reduce_sum.290), channel_id=1, replica_groups=mesh['dp'=16,'mp'=2] {'dp'}, use_global_device_ids=true, to_apply=%region_54.55 | all-reduce | flops 512 | bytes 2048 | tf_op jit(solution)/shard_map/psum | solution.py:327
  2065.1 248.4 %all-reduce.9.cloned.1.call-done = (bf16[768,512]{0,1:T(8,128)(2,1)}, bf16[1024,512]{1,0:T(8,128)(2,1)}, bf16[1024,512]{1,0:T(8,128)(2,1)}, bf16[1024,512]{1,0:T...) async-done(((bf16[768,512]{0,1:T(8,128)(2,1)}, ...) | async-done | bytes 17563664 | tf_op jit(solution)/shard_map/psum | solution.py:326
  2340.6 119.4 %reduce-scatter.18.cloned.1.call-done = f32[1536,1024]{1,0:T(8,128)} async-done(((f32[3072,1024]{1,0:T(8,128)}), f32[1536,1024]{1,0:T(8,128)}) %reduce-scatter.18.cloned.1.call-update) | async-done | bytes 6291472 | tf_op jit(solution)/shard_map/reduce_scatter | solution.py:81
  2465.3 40.0 %all-reduce.2 = (f32[1024]{0:T(1024)}, f32[1024]{0:T(1024)}, f32[1024]{0:T(1024)}, f32[1024]{0:T(1024)}, f32[1024]{0:T(1024)}, /*index=5*/f32[1024]{0:T(1024)}) all-reduce(f32[1024]{0:T(1024)S(1)} %get-tuple-element.176, f32[1024]{0:T(1024)S(1)} %get-tuple-element.183, ...), channel_id=1, replica_groups=mesh['dp'=16,'mp'=2] {'dp','mp'}, use_global_device_ids=true, to_apply=%region_37.38 | all-reduce | flops 6144 | bytes 49152 | tf_op jit(solution)/shard_map/psum | solution.py:338
  (427 shorter events, 733.7 us)
Async XLA Ops:
  7.2 594.1 %copy-start = (bf16[512,1024]{1,0:T(8,128)(2,1)S(1)}, bf16[512,1024]{1,0:T(8,128)(2,1)}, u32[]{:S(2)}) copy-start(bf16[512,1024]{1,0:T(8,128)(2,1)} %param.55) | copy-start | bytes 3145732
  7.2 92.0 %all-gather.7.cloned.1.call-start = ((), (), s32[]{:S(2)}) async-start(), calls=%async_computation.7 | async-start | bytes 9437184 | tf_op jit(solution)/shard_map/all_gather | solution.py:68
  16.0 452.8 %reduce-scatter.8.cloned.1.call-start = ((), (), s32[]{:S(2)}) async-start(), calls=%async_computation.8 | async-start | bytes 18874368 | tf_op jit(solution)/shard_map/reduce_scatter | solution.py:76
  324.2 234.8 %all-gather.9.cloned.1.call-start = ((), (), s32[]{:S(2)}) async-start(), calls=%async_computation.9 | async-start | bytes 9437184 | tf_op jit(solution)/shard_map/all_gather | solution.py:68
  478.4 273.9 %reduce-scatter.10.cloned.1.call-start = ((), (), s32[]{:S(2)}) async-start(), calls=%async_computation.10 | async-start | bytes 18874368 | tf_op jit(solution)/shard_map/reduce_scatter | solution.py:76
  607.7 236.2 %all-gather.11.cloned.1.call-start = ((), (), s32[]{:S(2)}) async-start(), calls=%async_computation.11 | async-start | bytes 9437184 | tf_op jit(solution)/shard_map/all_gather | solution.py:68
  763.4 162.3 %all-gather.13.cloned.1.call-start = ((), (), s32[]{:S(2)}) async-start(), calls=%async_computation.13 | async-start | bytes 9437184 | tf_op jit(solution)/shard_map/all_gather | solution.py:72
  764.0 357.6 %reduce-scatter.14.cloned.1.call-start = ((), (), s32[]{:S(2)}) async-start(), calls=%async_computation.14 | async-start | bytes 18874368 | tf_op jit(solution)/shard_map/reduce_scatter | solution.py:81
  977.0 291.4 %reduce-scatter.12.cloned.1.call-start = ((), (), s32[]{:S(2)}) async-start(), calls=%async_computation.12 | async-start | bytes 18874368 | tf_op jit(solution)/shard_map/reduce_scatter | solution.py:76
  996.4 125.2 %copy-start.73 = (f32[1536]{0:T(1024)S(1)}, f32[1536]{0:T(1024)}, u32[]{:S(2)}) copy-start(f32[1536]{0:T(1024)} %copy-done.72) | copy-start | bytes 18436
  996.4 125.2 %copy-start.85 = (f32[1536]{0:T(1024)S(1)}, f32[1536]{0:T(1024)}, u32[]{:S(2)}) copy-start(f32[1536]{0:T(1024)} %copy-done.84) | copy-start | bytes 18436
  996.4 125.2 %copy-start.91 = (f32[1024]{0:T(1024)S(1)}, f32[1024]{0:T(1024)}, u32[]{:S(2)}) copy-start(f32[1024]{0:T(1024)} %param.58) | copy-start | bytes 12292
  996.4 365.9 %all-gather.15.cloned.1.call-start = ((), (), s32[]{:S(2)}) async-start(), calls=%async_computation.15 | async-start | bytes 9437184 | tf_op jit(solution)/shard_map/all_gather | solution.py:72
  1281.8 281.0 %reduce-scatter.16.cloned.1.call-start = ((), (), s32[]{:S(2)}) async-start(), calls=%async_computation.16 | async-start | bytes 18874368 | tf_op jit(solution)/shard_map/reduce_scatter | solution.py:81
  1418.1 211.9 %reduce-scatter.20.cloned.1.call-start = ((), (), s32[]{:S(2)}) async-start(), calls=%async_computation.19 | async-start | bytes 786432 | tf_op jit(solution)/shard_map/reduce_scatter | solution.py:267
  1428.8 134.0 %copy-start.71 = (f32[1536]{0:T(1024)S(1)}, f32[1536]{0:T(1024)}, u32[]{:S(2)}) copy-start(f32[1536]{0:T(1024)} %copy-done.70) | copy-start | bytes 18436
  1428.8 134.0 %copy-start.81 = (f32[1536]{0:T(1024)S(1)}, f32[1536]{0:T(1024)}, u32[]{:S(2)}) copy-start(f32[1536]{0:T(1024)} %copy-done.80) | copy-start | bytes 18436
  1428.8 134.0 %copy-start.87 = (f32[1024]{0:T(1024)S(1)}, f32[1024]{0:T(1024)}, u32[]{:S(2)}) copy-start(f32[1024]{0:T(1024)} %param.50) | copy-start | bytes 12292
  1433.2 228.8 %all-gather.17.cloned.1.call-start = ((), (), s32[]{:S(2)}) async-start(), calls=%async_computation.17 | async-start | bytes 9437184 | tf_op jit(solution)/shard_map/all_gather | solution.py:72
  1577.9 485.3 %all-reduce.7.cloned.1.call-start = ((), (), s32[]{:S(2)}) async-start(), calls=%async_computation.20 | async-start | bytes 786432 | tf_op jit(solution)/shard_map/psum | solution.py:272
  1632.2 681.3 %all-reduce.9.cloned.1.call-start = ((), (), s32[]{:S(2)}) async-start(), calls=%async_computation.21 | async-start | bytes 35127296 | tf_op jit(solution)/shard_map/psum | solution.py:326
  1994.7 465.3 %reduce-scatter.18.cloned.1.call-start = ((), (), s32[]{:S(2)}) async-start(), calls=%async_computation.18 | async-start | bytes 18874368 | tf_op jit(solution)/shard_map/reduce_scatter | solution.py:81
  2340.6 124.6 %copy-start.94 = (f32[1024]{0:T(1024)S(1)}, f32[1024]{0:T(1024)}, u32[]{:S(2)}) copy-start(f32[1024]{0:T(1024)} %get-tuple-element.174) | copy-start | bytes 12292
  2340.6 124.7 %copy-start.95 = (f32[1024]{0:T(1024)S(1)}, f32[1024]{0:T(1024)}, u32[]{:S(2)}) copy-start(f32[1024]{0:T(1024)} %get-tuple-element.182) | copy-start | bytes 12292
  (108 other events, 1813.8 us)
Sparse Core Ops, SparseCore 0:
  16.1 83.0 all-gather.6
  324.3 144.4 reduce-scatter.7
  478.6 80.3 all-gather.8
  607.8 144.4 reduce-scatter.9
  763.5 80.3 all-gather.10
  845.3 80.3 all-gather.12
  977.1 144.4 reduce-scatter.13
  1123.9 144.4 reduce-scatter.11
  1281.9 80.3 all-gather.14
  1418.3 144.4 reduce-scatter.15
  1565.6 14.5 reduce-scatter.19
  1581.6 80.3 all-gather.16
  1665.0 25.7 all-reduce.6
  1994.8 318.6 all-reduce.8
  2315.7 144.2 reduce-scatter.17
where the time goes:
time: 2530 us; the launch traced here: 2520 us
  waiting for transfers between devices  1400 us (55%)
  matrix products  609 us (24%)
  other arithmetic  243 us (10%)
  local copies, waits for them, and re-layouts  171 us (7%)
  blocking collectives  83.9 us (3%)
    reduce_scatter x3, waiting for transfers between devices, branch_sum(): lax.psum_scatter(product(left_side, right_side), 'mp', scatter_dimension=...  429 us
    reduce_scatter x3, waiting for transfers between devices, input_grads(): lax.psum_scatter(reduce(jnp.add, partials), 'mp', scatter_dimension=0, ti...  374 us
    psum x1, waiting for transfers between devices, body(): lax.psum(text_weight_grad.astype(jnp.bfloat16), 'dp').astype(jnp.float32)  248 us
    all_gather x3, waiting for transfers between devices, spread_rows(): return lax.all_gather(tensor, 'mp', axis=0, tiled=True)  224 us
    dot_general x11, matrix products, product(): return jnp.dot(left_side, right_side, preferred_element_type=jnp.float32)  136 us
    all_gather x3, waiting for transfers between devices, spread_cotangent(): return lax.all_gather(tensor, 'mp', axis=0, tiled=True)  120 us
    dot_general x11, matrix products, against(): lax.dot_general(left_side, right_side, (((1,), (1,)), ((), ())), preferre...  107 us
    convert_element_type x4, other arithmetic, attend_back(): grad_scores = (soft_weights * (grad_soft - row_inner)).astype(jnp.bfloat16)  87.6 us
  transfers between devices with their start and end apart: 15, of which 13 were waited for; matrix products, arithmetic and copies ran while one was open for 23% of the time, Pallas kernels for 0%

commit v1 on v0

--- a/solution.py
+++ b/solution.py
@@ -1,8 +1,11 @@
+import functools
 from functools import reduce
 
 import jax
 import jax.numpy as jnp
 from jax import lax
+from jax.experimental import pallas as pl
+from jax.experimental.pallas import tpu as pltpu
 from jax.sharding import PartitionSpec as P
 
 HEAD_DIM = 64
@@ -371,9 +374,553 @@
     )
 
 
+LOG2E=1.4426950408889634
+SCALE2=LOG2E*HEAD_DIM**-0.5
+BQ=256
+SPAN=768
+
+def dot(a,b,ca,cb):
+    return lax.dot_general(a,b,(((ca,),(cb,)),((),())),preferred_element_type=jnp.float32)
+
+def starts_of(bounds_ref, places):
+    start=jnp.zeros_like(places)
+    for k in range(3):
+        start=jnp.where(places>=bounds_ref[k],bounds_ref[k],start)
+    return start
+
+def self_fwd_kernel(bounds_ref,q_ref,k_ref,v_ref,o_ref,lse_ref,*,ahead=2):
+    low=lax.broadcasted_iota(jnp.int32,(1,128),1)<HEAD_DIM
+    vt=jnp.transpose(v_ref[...])
+    pad=jnp.ones((16,ROW_LEN),jnp.bfloat16)
+    vts=[jnp.concatenate([vt[64*h:64*h+64],pad],0) for h in range(2)]
+    def span(i):
+        return max(0,BQ*i-SPAN),BQ*(i+1)
+    def scores(i,h):
+        k0,k1=span(i)
+        q=q_ref[BQ*i:k1,:]
+        qh=jnp.where(low==(h==0),q,jnp.zeros_like(q))
+        places=BQ*i+lax.broadcasted_iota(jnp.int32,(1,BQ),1)
+        keys=k0+lax.broadcasted_iota(jnp.int32,(k1-k0,BQ),0)
+        allowed=(keys>=starts_of(bounds_ref,places))&(keys<=places)
+        return jnp.where(allowed,dot(k_ref[k0:k1,:],qh,1,1),MASKED)
+    items=[(i,h) for i in range(ROW_LEN//BQ) for h in range(2)]
+    queue=[scores(*it) for it in items[:ahead]]
+    outs=[]
+    for n,(i,h) in enumerate(items):
+        if n+ahead<len(items):
+            queue.append(scores(*items[n+ahead]))
+        s=queue.pop(0)
+        k0,k1=span(i)
+        m=jnp.max(s,axis=0,keepdims=True)
+        p=jnp.exp2((s-m)*SCALE2)
+        o=dot(vts[h][:,k0:k1],p.astype(jnp.bfloat16),1,0)
+        l=o[64:65]
+        outs.append(o[:64]*(1.0/l))
+        lse_ref[0,h:h+1,BQ*i:k1]=m*SCALE2+jnp.log2(l)
+        if h==1:
+            o_ref[BQ*i:k1,:]=jnp.transpose(jnp.concatenate(outs,0)).astype(jnp.bfloat16)
+            outs=[]
+
+def row_self_forward(bounds,q,k,v):
+    pairs=q.shape[1]//128
+    spec=pl.BlockSpec((ROW_LEN,128),lambda h:(0,h))
+    return pl.pallas_call(self_fwd_kernel,grid=(pairs,),
+        in_specs=[pl.BlockSpec(memory_space=pltpu.SMEM),spec,spec,spec],
+        out_specs=[spec,pl.BlockSpec((1,2,ROW_LEN),lambda h:(h,0,0))],
+        out_shape=[jax.ShapeDtypeStruct(q.shape,jnp.bfloat16),jax.ShapeDtypeStruct((pairs,2,ROW_LEN),jnp.float32)],
+        compiler_params=pltpu.CompilerParams(vmem_limit_bytes=40<<20),
+        name="self_forward",
+        cost_estimate=pl.CostEstimate(flops=pairs*2*18*256*256*64*4*4,bytes_accessed=pairs*4*1536*256,transcendentals=0),
+    )(bounds,q,k,v)
+
+def self_bwd_kernel(bounds_ref,q_ref,k_ref,v_ref,o_ref,g_ref,lse_ref,dq_ref,dk_ref,dv_ref,acc_ref,d_ref,*,mode,ahead=1):
+    low=lax.broadcasted_iota(jnp.int32,(1,128),1)<HEAD_DIM
+    n=ROW_LEN//BQ
+    for i in range(n):
+        sl=slice(BQ*i,BQ*(i+1))
+        t=jnp.transpose(g_ref[sl,:].astype(jnp.float32)*o_ref[sl,:].astype(jnp.float32))
+        d_ref[0:1,sl]=jnp.sum(t[:64],axis=0,keepdims=True)
+        d_ref[1:2,sl]=jnp.sum(t[64:],axis=0,keepdims=True)
+    acc_ref[...]=jnp.zeros_like(acc_ref)
+    def span(j):
+        return BQ*j,min(ROW_LEN,BQ*(j+1)+SPAN)
+    def masked(ref,j,h):
+        t=ref[BQ*j:BQ*(j+1),:]
+        return jnp.where(low==(h==0),t,jnp.zeros_like(t))
+    def scores(j,h):
+        q0,q1=span(j)
+        places=q0+lax.broadcasted_iota(jnp.int32,(1,q1-q0),1)
+        keys=BQ*j+lax.broadcasted_iota(jnp.int32,(BQ,q1-q0),0)
+        allowed=(keys>=starts_of(bounds_ref,places))&(keys<=places)
+        s=dot(masked(k_ref,j,h),q_ref[q0:q1,:],1,1)*SCALE2-lse_ref[0,h:h+1,q0:q1]
+        return jnp.where(allowed,s,MASKED),dot(masked(v_ref,j,h),g_ref[q0:q1,:],1,1)
+    items=[(j,h) for j in range(n) for h in range(2)]
+    queue=[scores(*it) for it in items[:ahead]]
+    dks=[];dvs=[]
+    for t,(j,h) in enumerate(items):
+        if t+ahead<len(items):
+            queue.append(scores(*items[t+ahead]))
+        s,dp=queue.pop(0)
+        sl=slice(BQ*j,BQ*(j+1))
+        q0,q1=span(j)
+        p=jnp.exp2(s)
+        ds=(p*(dp-d_ref[h:h+1,q0:q1])).astype(jnp.bfloat16)
+        dvs.append(dot(p.astype(jnp.bfloat16),g_ref[q0:q1,:],1,0))
+        dks.append(dot(ds,q_ref[q0:q1,:],1,0))
+        if mode=="t":
+            kt=jnp.transpose(k_ref[sl,:])
+            acc_ref[64*h:64*h+64,q0:q1]+=dot(kt[64*h:64*h+64],ds,1,0)
+        else:
+            acc_ref[q0:q1,:]+=dot(ds,masked(k_ref,j,h),0,0)
+        if h==1:
+            dk_ref[sl,:]=(jnp.where(low,dks[0],dks[1])*HEAD_DIM**-0.5).astype(jnp.bfloat16)
+            dv_ref[sl,:]=jnp.where(low,dvs[0],dvs[1]).astype(jnp.bfloat16)
+            dks=[];dvs=[]
+            acc=jnp.transpose(acc_ref[:,sl]) if mode=="t" else acc_ref[sl,:]
+            dq_ref[sl,:]=(acc*HEAD_DIM**-0.5).astype(jnp.bfloat16)
+
+def self_backward(bounds,q,k,v,o,g,lse,mode="t",ahead=1):
+    pairs=q.shape[1]//128
+    spec=pl.BlockSpec((ROW_LEN,128),lambda h:(0,h))
+    sh=jax.ShapeDtypeStruct(q.shape,jnp.bfloat16)
+    return pl.pallas_call(functools.partial(self_bwd_kernel,mode=mode,ahead=ahead),grid=(pairs,),
+        in_specs=[pl.BlockSpec(memory_space=pltpu.SMEM)]+[spec]*5+[pl.BlockSpec((1,2,ROW_LEN),lambda h:(h,0,0))],
+        out_specs=[spec]*3,
+        out_shape=[sh]*3,
+        scratch_shapes=[pltpu.VMEM((128,ROW_LEN) if mode=="t" else (ROW_LEN,128),jnp.float32),pltpu.VMEM((8,ROW_LEN),jnp.float32)],
+        compiler_params=pltpu.CompilerParams(vmem_limit_bytes=48<<20),
+        name="self_backward",
+        cost_estimate=pl.CostEstimate(flops=pairs*2*18*256*256*64*10*4,bytes_accessed=pairs*8*1536*256,transcendentals=0),
+    )(bounds,q,k,v,o,g,lse)
+
+def token_range(cb_ref,tb_ref,places):
+    lo=jnp.zeros_like(places); hi=jnp.full_like(places,0)+tb_ref[0]
+    for c in range(3):
+        past=places>=cb_ref[c]
+        lo=jnp.where(past,tb_ref[c],lo)
+        hi=jnp.where(past,tb_ref[c+1],hi)
+    return lo,hi
+
+def cross_fwd_kernel(cb_ref,tb_ref,q_ref,k_ref,v_ref,o_ref,lse_ref,*,ahead=2,w=512):
+    low=lax.broadcasted_iota(jnp.int32,(1,128),1)<HEAD_DIM
+    k=k_ref[...]
+    vt=jnp.transpose(v_ref[...])
+    pad=jnp.ones((16,TXT_ROW),jnp.bfloat16)
+    vts=[jnp.concatenate([vt[64*h:64*h+64],pad],0) for h in range(2)]
+    khs=[jnp.where(low==(h==0),k,jnp.zeros_like(k)) for h in range(2)]
+    def scores(i,h):
+        places=w*i+lax.broadcasted_iota(jnp.int32,(1,w),1)
+        lo,hi=token_range(cb_ref,tb_ref,places)
+        toks=lax.broadcasted_iota(jnp.int32,(TXT_ROW,w),0)
+        return jnp.where((toks>=lo)&(toks<hi),dot(khs[h],q_ref[w*i:w*(i+1),:],1,1),MASKED)
+    items=[(i,h) for i in range(ROW_LEN//w) for h in range(2)]
+    queue=[scores(*it) for it in items[:ahead]]
+    outs=[]
+    for n,(i,h) in enumerate(items):
+        if n+ahead<len(items):
+            queue.append(scores(*items[n+ahead]))
+        s=queue.pop(0)
+        sl=slice(w*i,w*(i+1))
+        m=jnp.max(s,axis=0,keepdims=True)
+        p=jnp.exp2((s-m)*SCALE2)
+        o=dot(vts[h],p.astype(jnp.bfloat16),1,0)
+        l=o[64:65]
+        outs.append(o[:64]*(1.0/l))
+        lse_ref[0,h:h+1,sl]=m*SCALE2+jnp.log2(l)
+        if h==1:
+            o_ref[sl,:]=jnp.transpose(jnp.concatenate(outs,0)).astype(jnp.bfloat16)
+            outs=[]
+
+def cross_forward(cb,tb,q,k,v,**kw):
+    pairs=q.shape[1]//128
+    spec=pl.BlockSpec((ROW_LEN,128),lambda h:(0,h))
+    tspec=pl.BlockSpec((TXT_ROW,128),lambda h:(0,h))
+    return pl.pallas_call(functools.partial(cross_fwd_kernel,**kw),grid=(pairs,),
+        in_specs=[pl.BlockSpec(memory_space=pltpu.SMEM)]*2+[spec,tspec,tspec],
+        out_specs=[spec,pl.BlockSpec((1,2,ROW_LEN),lambda h:(h,0,0))],
+        out_shape=[jax.ShapeDtypeStruct(q.shape,jnp.bfloat16),jax.ShapeDtypeStruct((pairs,2,ROW_LEN),jnp.float32)],
+        compiler_params=pltpu.CompilerParams(vmem_limit_bytes=32<<20),
+        name="cross_forward",
+        cost_estimate=pl.CostEstimate(flops=pairs*2*1536*128*64*4*4,bytes_accessed=pairs*2*1536*256,transcendentals=0),
+    )(cb,tb,q,k,v)
+
+def cross_bwd_kernel(cb_ref,tb_ref,q_ref,k_ref,v_ref,o_ref,g_ref,lse_ref,dq_ref,dk_ref,dv_ref,d_ref,*,ahead=1,w=512):
+    low=lax.broadcasted_iota(jnp.int32,(1,128),1)<HEAD_DIM
+    k=k_ref[...]; v=v_ref[...]
+    kt=jnp.transpose(k)
+    khs=[jnp.where(low==(h==0),k,jnp.zeros_like(k)) for h in range(2)]
+    vhs=[jnp.where(low==(h==0),v,jnp.zeros_like(v)) for h in range(2)]
+    for i in range(ROW_LEN//256):
+        sl=slice(256*i,256*(i+1))
+        t=jnp.transpose(g_ref[sl,:].astype(jnp.float32)*o_ref[sl,:].astype(jnp.float32))
+        d_ref[0:1,sl]=jnp.sum(t[:64],axis=0,keepdims=True)
+        d_ref[1:2,sl]=jnp.sum(t[64:],axis=0,keepdims=True)
+    dk=[jnp.zeros((TXT_ROW,128),jnp.float32)]*2
+    dv=[jnp.zeros((TXT_ROW,128),jnp.float32)]*2
+    def scores(i,h):
+        sl=slice(w*i,w*(i+1))
+        places=w*i+lax.broadcasted_iota(jnp.int32,(1,w),1)
+        lo,hi=token_range(cb_ref,tb_ref,places)
+        toks=lax.broadcasted_iota(jnp.int32,(TXT_ROW,w),0)
+        s=dot(khs[h],q_ref[sl,:],1,1)*SCALE2-lse_ref[0,h:h+1,sl]
+        return jnp.where((toks>=lo)&(toks<hi),s,MASKED),dot(vhs[h],g_ref[sl,:],1,1)
+    items=[(i,h) for i in range(ROW_LEN//w) for h in range(2)]
+    queue=[scores(*it) for it in items[:ahead]]
+    dqs=[]
+    for n,(i,h) in enumerate(items):
+        if n+ahead<len(items):
+            queue.append(scores(*items[n+ahead]))
+        s,dp=queue.pop(0)
+        sl=slice(w*i,w*(i+1))
+        p=jnp.exp2(s)
+        ds=(p*(dp-d_ref[h:h+1,sl])).astype(jnp.bfloat16)
+        dv[h]=dv[h]+dot(p.astype(jnp.bfloat16),g_ref[sl,:],1,0)
+        dk[h]=dk[h]+dot(ds,q_ref[sl,:],1,0)
+        dqs.append(dot(kt[64*h:64*h+64],ds,1,0))
+        if h==1:
+            dq_ref[sl,:]=(jnp.transpose(jnp.concatenate(dqs,axis=0))*HEAD_DIM**-0.5).astype(jnp.bfloat16)
+            dqs=[]
+    dk_ref[...]=(jnp.where(low,dk[0],dk[1])*HEAD_DIM**-0.5).astype(jnp.bfloat16)
+    dv_ref[...]=jnp.where(low,dv[0],dv[1]).astype(jnp.bfloat16)
+
+def cross_backward(cb,tb,q,k,v,o,g,lse,**kw):
+    pairs=q.shape[1]//128
+    spec=pl.BlockSpec((ROW_LEN,128),lambda h:(0,h))
+    tspec=pl.BlockSpec((TXT_ROW,128),lambda h:(0,h))
+    sh=jax.ShapeDtypeStruct(q.shape,jnp.bfloat16)
+    th=jax.ShapeDtypeStruct(k.shape,jnp.bfloat16)
+    return pl.pallas_call(functools.partial(cross_bwd_kernel,**kw),grid=(pairs,),
+        in_specs=[pl.BlockSpec(memory_space=pltpu.SMEM)]*2+[spec,tspec,tspec,spec,spec,pl.BlockSpec((1,2,ROW_LEN),lambda h:(h,0,0))],
+        out_specs=[spec,tspec,tspec],
+        out_shape=[sh,th,th],
+        scratch_shapes=[pltpu.VMEM((8,ROW_LEN),jnp.float32)],
+        compiler_params=pltpu.CompilerParams(vmem_limit_bytes=32<<20),
+        name="cross_backward",
+        cost_estimate=pl.CostEstimate(flops=pairs*2*1536*128*64*10*4,bytes_accessed=pairs*4*1536*256,transcendentals=0),
+    )(cb,tb,q,k,v,o,g,lse)
+
+
+INV_SQRT_2PI = 0.3989422804014327
+
+
+def gelu_pair(hidden):
+    size = jnp.abs(hidden)
+    density = jnp.exp(hidden * hidden * -0.5) * INV_SQRT_2PI
+    t = 1.0 / (1.0 + 0.2316419 * size)
+    series = t * (
+        0.319381530
+        + t * (-0.356563782 + t * (1.781477937 + t * (-1.821255978 + t * 1.330274429)))
+    )
+    tail = density * series
+    below = jnp.where(hidden >= 0, 1.0 - tail, tail)
+    return (hidden * below).astype(jnp.bfloat16), (below + hidden * density).astype(jnp.bfloat16)
+
+
+def row_body(dp, *args):
+    (
+        frames,
+        text_states,
+        clip_lengths,
+        text_lengths,
+        cotangent,
+        self_gain,
+        self_shift,
+        self_query,
+        self_key,
+        self_value,
+        self_out,
+        cross_gain,
+        cross_shift,
+        cross_query,
+        cross_key,
+        cross_value,
+        cross_out,
+        text_weight,
+        text_bias,
+        feed_gain,
+        feed_shift,
+        feed_in,
+        feed_out,
+    ) = args
+    bf16, f32 = jnp.bfloat16, jnp.float32
+    me = lax.axis_index("dp")
+    half = lax.axis_index("mp")
+    core = me % 2
+    rest = dp // 2
+
+    swap_mp = [(0, 1), (1, 0)]
+    swap_core = [(i, i ^ 1) for i in range(dp)]
+
+    def over_y(t):
+        return lax.ppermute(t, "mp", swap_mp)
+
+    def over_core(t):
+        return lax.ppermute(t, "dp", swap_core)
+
+    bits = []
+    step = 2
+    while step < dp:
+        bits.append(step)
+        step *= 2
+
+    def over_bit(t, step):
+        return lax.ppermute(t, "dp", [(i, i ^ step) for i in range(dp)])
+
+    def half_of(t, which, axis):
+        size = t.shape[axis] // 2
+        return lax.dynamic_slice_in_dim(t, which * size, size, axis)
+
+    def ordered(first_is_mine, mine, theirs, axis):
+        return jnp.concatenate(
+            [jnp.where(first_is_mine, mine, theirs), jnp.where(first_is_mine, theirs, mine)], axis
+        )
+
+    def fetch(t):
+        mine = over_y(half_of(t, core, 0))
+        return ordered(core == 0, mine, over_core(mine), 0)
+
+    def reduce_chunk(keeps, sends, splits):
+        got = [over_core(t) for t in sends]
+        sums = [(k.astype(f32) + g.astype(f32)) for k, g in zip(keeps, got)]
+        owns, others = [], []
+        for t, axis in zip(sums, splits):
+            size = t.shape[axis] // 2
+            owns.append(lax.slice_in_dim(t, 0, size, axis=axis).astype(bf16))
+            others.append(lax.slice_in_dim(t, size, 2 * size, axis=axis).astype(bf16))
+        other = others[0] if len(others) == 1 else jnp.concatenate(others, 0)
+        own = owns[0] if len(owns) == 1 else jnp.concatenate(owns, 0)
+        arrived = over_y(other)
+        now, came = own, arrived
+        for step in bits:
+            at = (me // step) % 2
+            total = lambda which: (
+                half_of(now, which, 0).astype(f32) + half_of(came, which, 0).astype(f32)
+            ).astype(bf16)
+            keep, send = total(at), total(1 - at)
+            now, came = keep, over_bit(send, step)
+        block = (now.astype(f32) + came.astype(f32)).astype(bf16)
+        for step in reversed(bits):
+            at = (me // step) % 2
+            block = ordered(at == 0, block, over_bit(block, step), 0)
+        return block, over_core(block)
+
+    def full_width(mine, theirs, axis):
+        return ordered(core == 0, mine.astype(f32), theirs.astype(f32), axis)
+
+    def reduce_small(t):
+        t = t + over_core(t)
+        t = t + over_y(t)
+        for step in bits:
+            t = t + over_bit(t, step)
+        return t
+
+    def wide_halves(t):
+        return half_of(t, core, 1), half_of(t, 1 - core, 1)
+
+    lengths = lax.dynamic_index_in_dim(clip_lengths, half, 0, keepdims=False)
+    words = lax.dynamic_index_in_dim(text_lengths, half, 0, keepdims=False)
+    clip_bounds, text_bounds = jnp.cumsum(lengths), jnp.cumsum(words)
+    text = lax.dynamic_slice_in_dim(text_states, half * TXT_ROW, TXT_ROW, 0)
+
+    matrices = dict(
+        self_query=self_query,
+        self_key=self_key,
+        self_value=self_value,
+        self_out=self_out,
+        text_weight=text_weight,
+        cross_key=cross_key,
+        cross_value=cross_value,
+        cross_query=cross_query,
+        cross_out=cross_out,
+        feed_in=feed_in,
+        feed_out=feed_out,
+    )
+    other = {name: fetch(t) for name, t in matrices.items()}
+    pairs = {name: (matrices[name], other[name]) for name in matrices}
+
+    residual = frames.astype(f32)
+    self_standard, self_inverse = norm_parts(residual)
+    self_rows = (self_standard * self_gain + self_shift).astype(bf16)
+    self_q = [product(self_rows, w).astype(bf16) for w in pairs["self_query"]]
+    self_k = [product(self_rows, w).astype(bf16) for w in pairs["self_key"]]
+    self_v = [product(self_rows, w).astype(bf16) for w in pairs["self_value"]]
+    self_ctx, self_log = zip(
+        *[row_self_forward(clip_bounds, *qkv) for qkv in zip(self_q, self_k, self_v)]
+    )
+    middle = residual + sum(product(c, w) for c, w in zip(self_ctx, pairs["self_out"]))
+
+    bias_other = over_y(text_bias)
+    text_full = ordered(
+        half == 0,
+        (product(text, text_weight) + text_bias).astype(bf16),
+        (product(text, other["text_weight"]) + bias_other).astype(bf16),
+        1,
+    )
+    cross_standard, cross_inverse = norm_parts(middle)
+    cross_rows = (cross_standard * cross_gain + cross_shift).astype(bf16)
+    cross_q = [product(cross_rows, w).astype(bf16) for w in pairs["cross_query"]]
+    cross_k = [product(text_full, w).astype(bf16) for w in pairs["cross_key"]]
+    cross_v = [product(text_full, w).astype(bf16) for w in pairs["cross_value"]]
+    cross_ctx, cross_log = zip(
+        *[
+            cross_forward(clip_bounds, text_bounds, *qkv)
+            for qkv in zip(cross_q, cross_k, cross_v)
+        ]
+    )
+    after = middle + sum(product(c, w) for c, w in zip(cross_ctx, pairs["cross_out"]))
+
+    feed_standard, feed_inverse = norm_parts(after)
+    feed_rows = (feed_standard * feed_gain + feed_shift).astype(bf16)
+    active, slope = zip(*[gelu_pair(product(feed_rows, w)) for w in pairs["feed_in"]])
+    output = after + sum(product(a, w) for a, w in zip(active, pairs["feed_out"]))
+    grad_output = cotangent.astype(f32)
+    grad_hidden = [
+        (against(cotangent, w) * s.astype(f32)).astype(bf16)
+        for w, s in zip(pairs["feed_out"], slope)
+    ]
+    active_all = jnp.concatenate(active, 1)
+    hidden_all = jnp.concatenate(grad_hidden, 1)
+    out_keep, out_send = [
+        outer_sum(active_all, t).astype(bf16) for t in wide_halves(cotangent)
+    ]
+    in_keep, in_send = [outer_sum(t, hidden_all).astype(bf16) for t in wide_halves(feed_rows)]
+    grad_hidden, out_keep, out_send, in_keep, in_send = lax.optimization_barrier(
+        (grad_hidden, out_keep, out_send, in_keep, in_send)
+    )
+    feed_out_sum = reduce_chunk([out_keep], [out_send], [0])
+    feed_in_sum = reduce_chunk([in_keep], [in_send], [1])
+    grad_normed = sum(against(g, w) for g, w in zip(grad_hidden, pairs["feed_in"]))
+    grad_norm, feed_gain_grad, feed_shift_grad = norm_back(
+        grad_normed, feed_standard, feed_inverse, feed_gain
+    )
+    grad_after = grad_output + grad_norm
+
+    grad_c = grad_after.astype(bf16)
+    grad_ctx = [against(grad_c, w).astype(bf16) for w in pairs["cross_out"]]
+    grad_q, grad_k, grad_v = zip(
+        *[
+            cross_backward(clip_bounds, text_bounds, *parts)
+            for parts in zip(cross_q, cross_k, cross_v, cross_ctx, grad_ctx, cross_log)
+        ]
+    )
+    grad_text_full = sum(
+        against(g, w)
+        for g, w in zip(grad_k + grad_v, pairs["cross_key"] + pairs["cross_value"])
+    ).astype(bf16)
+    text_grad_row = against(
+        lax.dynamic_slice_in_dim(grad_text_full, half * 512, 512, 1), text_weight
+    ) + against(
+        lax.dynamic_slice_in_dim(grad_text_full, (1 - half) * 512, 512, 1), other["text_weight"]
+    )
+    text_grad_row = text_grad_row.astype(bf16)
+    text_grad = ordered(half == 0, text_grad_row, over_y(text_grad_row), 0).astype(f32)
+    grad_text_mine = jnp.concatenate(
+        [half_of(grad_text_full, half, 1), half_of(grad_text_full, 1 - half, 1)], 1
+    )
+    ctx_all = jnp.concatenate(cross_ctx, 1)
+    chunk = []
+    for which in range(2):
+        chunk.append(
+            [
+                outer_sum(wide_halves(cross_rows)[which], jnp.concatenate(grad_q, 1)).astype(bf16),
+                outer_sum(wide_halves(text_full)[which], jnp.concatenate(grad_k, 1)).astype(bf16),
+                outer_sum(wide_halves(text_full)[which], jnp.concatenate(grad_v, 1)).astype(bf16),
+                outer_sum(ctx_all, wide_halves(grad_c)[which]).astype(bf16),
+                outer_sum(wide_halves(text)[which], grad_text_mine).astype(bf16),
+            ]
+        )
+    grad_q, chunk = lax.optimization_barrier((grad_q, chunk))
+    cross_sum = reduce_chunk(chunk[0], chunk[1], [1, 1, 1, 0, 1])
+    grad_normed = sum(against(g, w) for g, w in zip(grad_q, pairs["cross_query"]))
+    grad_norm, cross_gain_grad, cross_shift_grad = norm_back(
+        grad_normed, cross_standard, cross_inverse, cross_gain
+    )
+    grad_middle = grad_after + grad_norm
+    early = reduce_small(
+        jnp.stack(
+            [
+                feed_gain_grad,
+                feed_shift_grad,
+                cross_gain_grad,
+                cross_shift_grad,
+                jnp.sum(grad_text_full.astype(f32), axis=0),
+            ]
+        )
+    )
+
+    grad_s = grad_middle.astype(bf16)
+    grad_ctx = [against(grad_s, w).astype(bf16) for w in pairs["self_out"]]
+    ctx_all = jnp.concatenate(self_ctx, 1)
+    so_keep, so_send = [outer_sum(ctx_all, t).astype(bf16) for t in wide_halves(grad_s)]
+    grad_ctx, so_keep, so_send = lax.optimization_barrier((grad_ctx, so_keep, so_send))
+    self_out_sum = reduce_chunk([so_keep], [so_send], [0])
+    grad_q, grad_k, grad_v = zip(
+        *[
+            self_backward(clip_bounds, *parts)
+            for parts in zip(self_q, self_k, self_v, self_ctx, grad_ctx, self_log)
+        ]
+    )
+    chunk = []
+    for which in range(2):
+        rows = wide_halves(self_rows)[which]
+        chunk.append(
+            [
+                outer_sum(rows, jnp.concatenate(g, 1)).astype(bf16)
+                for g in (grad_q, grad_k, grad_v)
+            ]
+        )
+    self_sum = reduce_chunk(chunk[0], chunk[1], [1, 1, 1])
+    grad_normed = sum(
+        against(g, w)
+        for g, w in zip(
+            grad_q + grad_k + grad_v,
+            pairs["self_query"] + pairs["self_key"] + pairs["self_value"],
+        )
+    )
+    grad_norm, self_gain_grad, self_shift_grad = norm_back(
+        grad_normed, self_standard, self_inverse, self_gain
+    )
+    frames_grad = grad_middle + grad_norm
+    late = reduce_small(jnp.stack([self_gain_grad, self_shift_grad]))
+
+    def part(pair, at, rows, axis):
+        return full_width(pair[0][at : at + rows], pair[1][at : at + rows], axis)
+
+    return (
+        output.astype(bf16),
+        frames_grad,
+        text_grad,
+        late[0],
+        late[1],
+        part(self_sum, 0, 512, 0),
+        part(self_sum, 512, 512, 0),
+        part(self_sum, 1024, 512, 0),
+        part(self_out_sum, 0, 512, 1),
+        early[2],
+        early[3],
+        part(cross_sum, 0, 512, 0),
+        part(cross_sum, 512, 512, 0),
+        part(cross_sum, 1024, 512, 0),
+        part(cross_sum, 1536, 512, 1),
+        part(cross_sum, 2048, 384, 0),
+        lax.dynamic_slice_in_dim(early[4], half * 512, 512, 0),
+        early[0],
+        early[1],
+        part(feed_in_sum, 0, 512, 0),
+        part(feed_out_sum, 0, 2048, 1),
+    )
+
+
+def chosen(dp, mp, *args):
+    rows_here, frames_here = args[2].shape[0], args[0].shape[0]
+    if mp == 2 and dp == 16 and rows_here == mp and frames_here == ROW_LEN:
+        return row_body(dp, *args)
+    return body(*args)
+
+
 def solution(mesh):
     return jax.shard_map(
-        body,
+        functools.partial(chosen, mesh.shape["dp"], mesh.shape["mp"]),
         mesh=mesh,
         in_specs=(
             P(("dp", "mp"), None),

time: 2530 us -> 999 us (0.39)
  waiting for transfers between devices: 1400 us -> 316 us
  matrix products: 609 us -> 322 us
  other arithmetic: 243 us -> 95.1 us
  Pallas kernels: 0 us -> 116 us
  local copies, waits for them, and re-layouts: 171 us -> 68.8 us
  blocking collectives: 83.9 us -> 0 us
  starting transfers between devices: 0.79 us -> 66.4 us
    reduce_scatter x7 -> x0, waiting for transfers between devices: 803 us -> none  [the longest x3 429 us: branch_sum(): lax.psum_scatter(product(left_side, right_side), 'mp', scatter_dimension=...]
    all_gather x6 -> x0, waiting for transfers between devices: 344 us -> none  [the longest x3 224 us: spread_rows(): return lax.all_gather(tensor, 'mp', axis=0, tiled=True)]
    ppermute x0 -> x85, waiting for transfers between devices: none -> 316 us  [the longest x36 195 us: over_bit(): return lax.ppermute(t, 'dp', [(i, i ^ step) for i in range(dp)])]
    dot_general x24 -> x0, matrix products: 289 us -> none  [the longest x4 75.6 us: attend_back(): jnp.einsum('rqhd,rkhd->rhqk', grad_context, values, preferred_element_typ...]
    psum x2 -> x0, waiting for transfers between devices: 248 us -> none  [the longest x1 248 us: body(): lax.psum(text_weight_grad.astype(jnp.bfloat16), 'dp').astype(jnp.float32)]
    convert_element_type x21 -> x26, other arithmetic: 143 us -> 26.1 us  [the longest x1 10.7 us: row_body(): grad_s = grad_middle.astype(bf16)]
    pallas_call x0 -> x8, Pallas kernels: none -> 116 us  [the longest x2 56.9 us: self_backward(): pl.pallas_call(functools.partial(self_bwd_kernel, mode=mode, ahead=ahead)...]
    reshape x14 -> x0, local copies, waits for them, and re-layouts: 85.6 us -> none  [split_heads(): tensor.reshape(row_count, tensor.shape[0] // row_count, tensor.shape[1] /...]
  transfers between devices with their start and end apart: 15 -> 85, of which waited for: 13 -> 31; matrix products, arithmetic and copies ran while one was open for 23% -> 28% of each run, Pallas kernels for 0% -> 7%
where the time goes in v1:
time: 999 us; the launch traced here: 989 us
  matrix products  322 us (32%)
  waiting for transfers between devices  316 us (32%)
  Pallas kernels  116 us (12%)
  other arithmetic  95.1 us (10%)
  local copies, waits for them, and re-layouts  68.8 us (7%)
  starting transfers between devices  66.4 us (7%)
    ppermute x36, waiting for transfers between devices, over_bit(): return lax.ppermute(t, 'dp', [(i, i ^ step) for i in range(dp)])  195 us
    dot_general x22, matrix products, against(): lax.dot_general(left_side, right_side, (((1,), (1,)), ((), ())), preferre...  127 us
    ppermute x20, waiting for transfers between devices, over_y(): return lax.ppermute(t, 'mp', swap_mp)  115 us
    dot_general x22, matrix products, product(): return jnp.dot(left_side, right_side, preferred_element_type=jnp.float32)  99.9 us
    dot_general x22, matrix products, outer_sum(): lax.dot_general(left_side, right_side, (((0,), (0,)), ((), ())), preferre...  95.4 us
    pallas_call x2, Pallas kernels, self_backward(): pl.pallas_call(functools.partial(self_bwd_kernel, mode=mode, ahead=ahead)...  56.9 us
    unnamed x350, local copies, waits for them, and re-layouts  46.1 us
    ppermute x36, starting transfers between devices, over_bit(): return lax.ppermute(t, 'dp', [(i, i ^ step) for i in range(dp)])  37.9 us
  transfers between devices with their start and end apart: 85, of which 31 were waited for; matrix products, arithmetic and copies ran while one was open for 28% of the time, Pallas kernels for 7%

profile of v1, /device:TPU:0, one launch (start us, length us, event | category | flops | bytes accessed | tf_op | source)
XLA Modules:
  0.0 989.3 jit_solution(17581803047297321762)
XLA Ops:
  43.3 15.2 %self_forward.2 = (bf16[1536,512]{1,0:T(8,128)(2,1)S(1)}, f32[4,2,1536]{2,1,0:T(2,128)S(1)}) custom-call(s32[4]{0:T(128)S(1)} %bitcast.100, bf16[1536,512]{1,0:T(8,128)(2,1)S(1)} %copy-done.21, bf16[1536,512]{1,0:T(8,128)(2,1)S(1)} %copy-done.20, bf16[1536,512]{1,0:T(8,128)(2,1)S(1)} %copy-done.22), custom_call_target="tpu_custom_call" | custom-call | flops 9663676416 | bytes 6291456 | tf_op jit(solution)/shard_map/self_forward/pallas_call | solution.py:427
  96.8 15.3 %self_forward.3 = (bf16[1536,512]{1,0:T(8,128)(2,1)S(1)}, f32[4,2,1536]{2,1,0:T(2,128)S(1)}) custom-call(s32[4]{0:T(128)S(1)} %bitcast.101, bf16[1536,512]{1,0:T(8,128)(2,1)S(1)} %convolution_convert_fusion.8.q_ref, bf16[1536,512]{1,0:T(8,128)(2,1)S(1)} %convolution_convert_fusion.7.k_ref, bf16[1536,512]{1,0:T(8,128)(2,1)S(1)} %convolution_convert_fusion.6.v_ref), custom_call_target="tpu_custom_call" | custom-call | flops 9663676416 | bytes 6291456 | tf_op jit(solution)/shard_map/self_forward/pallas_call | solution.py:427
  172.4 17.9 %multiply_convert_fusion.2 = (bf16[1536,2048]{1,0:T(8,128)(2,1)}, f32[1536,2048]{1,0:T(8,128)}) fusion(bf16[1536,1024]{0,1:T(8,128)(2,1)S(1)} %add_convert_fusion.5, bf16[1024,2048]{1,0:T(8,128)(2,1)S(1)} %copy-done.87), kind=kOutput, calls=%fused_computation.11 | convolution fusion | flops 6511656960 | bytes 26214400 | tf_op jit(solution)/shard_map/dot_general | solution.py:21
  190.3 20.1 %multiply_convert_fusion = bf16[1536,2048]{1,0:T(8,128)(2,1)} fusion(bf16[1536,1024]{1,0:T(8,128)(2,1)S(1)} %copy-done.49, bf16[2048,1024]{1,0:T(8,128)(2,1)} %param.45, f32[1536,2048]{1,0:T(8,128)} %get-tuple-element.274), kind=kOutput, calls=%fused_computation.7 | convolution fusion | flops 6524239872 | bytes 26214400 | tf_op jit(solution)/shard_map/dot_general | solution.py:25
  229.0 18.0 %multiply_convert_fusion.1 = (bf16[1536,2048]{1,0:T(8,128)(2,1)}, f32[1536,2048]{1,0:T(8,128)}) fusion(bf16[1536,1024]{0,1:T(8,128)(2,1)S(1)} %copy-done.59, bf16[512,2048]{1,0:T(8,128)(2,1)S(1)} %get-tuple-element.159, bf16[512,2048]{1,0:T(8,128)(2,1)S(1)} %get-tuple-element.158), kind=kOutput, calls=%fused_computation.9 | convolution fusion | flops 6520045568 | bytes 26214400 | tf_op jit(solution)/shard_map/dot_general | solution.py:21
  250.3 21.7 %fusion = bf16[1536,2048]{1,0:T(8,128)(2,1)} fusion(bf16[1536,1024]{1,0:T(8,128)(2,1)S(1)} %copy-done.49, f32[1536,2048]{1,0:T(8,128)} %get-tuple-element.276, bf16[1024,1024]{1,0:T(8,128)(2,1)S(1)} %get-tuple-element.157, bf16[1024,1024]{1,0:T(8,128)(2,1)S(1)} %get-tuple-element.156), kind=kOutput, calls=%fused_computation.5 | convolution fusion | flops 6532628480 | bytes 26214400 | tf_op jit(solution)/shard_map/dot_general | solution.py:25
  272.0 13.4 %fusion.21 = bf16[512,4096]{1,0:T(8,128)(2,1)} fusion(bf16[1536,2048]{1,0:T(8,128)(2,1)} %fusion, bf16[1536,2048]{1,0:T(8,128)(2,1)} %multiply_convert_fusion, bf16[1536,1024]{0,1:T(8,128)(2,1)S(1)} %copy-done.59, s32[]{:T(128)S(6)} %select_n.694), kind=kOutput, calls=%fused_computation.53 | convolution fusion | flops 6469713920 | bytes 18350084 | tf_op jit(solution)/shard_map/dot_general | solution.py:31
  285.4 13.8 %fusion.22 = bf16[512,4096]{1,0:T(8,128)(2,1)} fusion(bf16[1536,2048]{1,0:T(8,128)(2,1)} %fusion, bf16[1536,2048]{1,0:T(8,128)(2,1)} %multiply_convert_fusion, bf16[1536,1024]{0,1:T(8,128)(2,1)} %copy-done.58, s32[]{:T(128)S(6)} %select_n.730), kind=kOutput, calls=%fused_computation.54 | convolution fusion | flops 6469713920 | bytes 18350084 | tf_op jit(solution)/shard_map/dot_general | solution.py:31
  299.2 13.6 %fusion.20 = bf16[4096,512]{1,0:T(8,128)(2,1)} fusion(bf16[1536,2048]{1,0:T(8,128)(2,1)} %get-tuple-element.275, bf16[1536,2048]{1,0:T(8,128)(2,1)} %get-tuple-element.273, bf16[1536,1024]{1,0:T(8,128)(2,1)S(1)} %copy-done.50, s32[]{:T(128)S(6)} %select_n.730), kind=kOutput, calls=%fused_computation.52 | convolution fusion | flops 6469713920 | bytes 18350084 | tf_op jit(solution)/shard_map/dot_general | solution.py:31
  312.8 13.4 %fusion.19 = bf16[4096,512]{1,0:T(8,128)(2,1)} fusion(bf16[1536,2048]{1,0:T(8,128)(2,1)} %get-tuple-element.275, bf16[1536,2048]{1,0:T(8,128)(2,1)} %get-tuple-element.273, bf16[1536,1024]{1,0:T(8,128)(2,1)S(1)} %copy-done.50, s32[]{:T(128)S(6)} %select_n.694), kind=kOutput, calls=%fused_computation.51 | convolution fusion | flops 6469713920 | bytes 18350084 | tf_op jit(solution)/shard_map/dot_general | solution.py:31
  326.2 12.1 %fusion.146 = f32[1536,1024]{0,1:T(8,128)} fusion(bf16[1536,2048]{1,0:T(8,128)(2,1)} %multiply_convert_fusion, bf16[1024,2048]{1,0:T(8,128)(2,1)} %param.44), kind=kOutput, calls=%fused_computation.429 | convolution fusion | flops 6442450944 | bytes 16777216 | tf_op jit(solution)/shard_map/dot_general | solution.py:25
  338.3 14.8 %multiply_reduce_fusion.1 = (f32[1024]{0:T(1024)S(1)}, f32[1536]{0:T(1024)S(1)}, f32[1536]{0:T(1024)S(1)}, f32[1024]{0:T(1024)S(1)}, f32[1536,1024]{0,1:T(8,128)}) fusion(f32[1536,1024]{0,1:T(8,128)} %copy-done.30, f32[1536]{0:T(1024)S(1)} %copy-done.144, f32[1536]{0:T(1024)S(1)} %copy-done.138, f32[1024]{0:T(1024)S(1)} %copy-done.150, ...), kind=kOutput, calls=%fused_computation.39 | convolution fusion | flops 6466563072 | bytes 29396992 | tf_op jit(solution)/shard_map/dot_general | solution.py:25
  435.6 28.2 %self_backward.2 = (bf16[1536,512]{1,0:T(8,128)(2,1)S(1)}, bf16[1536,512]{1,0:T(8,128)(2,1)S(1)}, bf16[1536,512]{1,0:T(8,128)(2,1)S(1)}) custom-call(s32[4]{0:T(128)S(1)} %bitcast.106, bf16[1536,512]{1,0:T(8,128)(2,1)} %convolution_convert_fusion.11.q_ref, bf16[1536,512]{1,0:T(8,128)(2,1)} %convolution_convert_fusion.10.k_ref, ...), custom_call_target="tpu_custom_call" | custom-call | flops 24159191040 | bytes 12582912 | tf_op jit(solution)/shard_map/self_backward/pallas_call | solution.py:486
  477.3 28.6 %self_backward.3 = (bf16[1536,512]{1,0:T(8,128)(2,1)S(1)}, bf16[1536,512]{1,0:T(8,128)(2,1)S(1)}, bf16[1536,512]{1,0:T(8,128)(2,1)S(1)}) custom-call(s32[4]{0:T(128)S(1)} %bitcast.107, bf16[1536,512]{1,0:T(8,128)(2,1)} %copy-done.25, bf16[1536,512]{1,0:T(8,128)(2,1)} %copy-done.24, bf16[1536,512]{1,0:T(8,128)(2,1)} %copy-done.23, ...), custom_call_target="tpu_custom_call" | custom-call | flops 24159191040 | bytes 12582912 | tf_op jit(solution)/shard_map/self_backward/pallas_call | solution.py:486
  527.2 15.5 %fusion.17 = (f32[1024]{0:T(1024)S(1)}, f32[1536]{0:T(1024)S(1)}, f32[1536]{0:T(1024)S(1)}, f32[1024]{0:T(1024)S(1)}, f32[1536,1024]{0,1:T(8,128)}) fusion(bf16[1536,1024]{0,1:T(8,128)(2,1)S(1)} %copy-done.29, f32[1536]{0:T(1024)S(1)} %copy-done.140, f32[1536]{0:T(1024)S(1)} %copy-done.136, f32[1024]{0:T(1024)S(1)} %copy-done.148, ...), kind=kOutput, calls=%fused_computation.36 | convolution fusion | flops 1636297728 | bytes 43552768 | tf_op jit(solution)/shard_map/dot_general | solution.py:25
  542.9 13.5 %add_convert_fusion.4 = bf16[1536,1024]{0,1:T(8,128)(2,1)} fusion(f32[1536,1024]{0,1:T(8,128)} %copy-done.30, f32[1536,1024]{0,1:T(8,128)} %fusion.145, bf16[1536,2048]{1,0:T(8,128)(2,1)} %get-tuple-element.275, bf16[1024,1024]{1,0:T(8,128)(2,1)} %copy-done.79, bf16[1024,1024]{1,0:T(8,128)(2,1)} %copy-done.78), kind=kOutput, calls=%fused_computation.45 | convolution fusion | flops 6455558144 | bytes 26214400 | tf_op jit(solution)/shard_map/dot_general | solution.py:21
  642.4 19.0 %collective-permute-done.32 = bf16[1536,512]{1,0:T(8,128)(2,1)S(1)} collective-permute-done((bf16[1536,512]{1,0:T(8,128)(2,1)S(1)}, bf16[1536,512]{1,0:T(8,128)(2,1)S(1)}, u32[]{:S(2)}, u32[]{:S(2)}) %collective-permute-start.32) | collective-permute-done | bytes 1572896 | tf_op jit(solution)/shard_map/ppermute | solution.py:655
  681.0 36.9 %collective-permute-done.23 = bf16[128,768]{1,0:T(8,128)(2,1)S(1)} collective-permute-done((bf16[128,768]{1,0:T(8,128)(2,1)S(1)}, bf16[128,768]{1,0:T(8,128)(2,1)S(1)}, u32[]{:S(2)}, u32[]{:S(2)}) %collective-permute-start.23) | collective-permute-done | bytes 196640 | tf_op jit(solution)/shard_map/ppermute | solution.py:655
  776.0 12.2 %collective-permute-done.62 = bf16[304,512]{1,0:T(8,128)(2,1)S(1)} collective-permute-done((bf16[304,512]{1,0:T(8,128)(2,1)S(1)}, bf16[304,512]{1,0:T(8,128)(2,1)S(1)}, u32[]{:S(2)}, u32[]{:S(2)}) %collective-permute-start.62) | collective-permute-done | bytes 311328 | tf_op jit(solution)/shard_map/ppermute | solution.py:667
  789.0 15.2 %collective-permute-done.63 = bf16[304,512]{1,0:T(8,128)(2,1)S(1)} collective-permute-done((bf16[304,512]{1,0:T(8,128)(2,1)S(1)}, bf16[304,512]{1,0:T(8,128)(2,1)S(1)}, u32[]{:S(2)}, u32[]{:S(2)}) %collective-permute-start.63) | collective-permute-done | bytes 311328 | tf_op jit(solution)/shard_map/ppermute | solution.py:667
  805.7 25.9 %collective-permute-done.68 = bf16[512,2048]{1,0:T(8,128)(2,1)S(1)} collective-permute-done((bf16[512,2048]{1,0:T(8,128)(2,1)S(1)}, bf16[512,2048]{1,0:T(8,128)(2,1)S(1)}, u32[]{:S(2)}, u32[]{:S(2)}) %collective-permute-start.68) | collective-permute-done | bytes 2097184 | tf_op jit(solution)/shard_map/ppermute | solution.py:655
  839.4 19.1 %collective-permute-done.69 = bf16[256,2048]{1,0:T(8,128)(2,1)S(1)} collective-permute-done((bf16[256,2048]{1,0:T(8,128)(2,1)S(1)}, bf16[256,2048]{1,0:T(8,128)(2,1)S(1)}, u32[]{:S(2)}, u32[]{:S(2)}) %collective-permute-start.69) | collective-permute-done | bytes 1048608 | tf_op jit(solution)/shard_map/ppermute | solution.py:667
  886.0 15.8 %collective-permute-done.81 = bf16[256,512]{1,0:T(8,128)(2,1)S(1)} collective-permute-done((bf16[256,512]{1,0:T(8,128)(2,1)S(1)}, bf16[256,512]{1,0:T(8,128)(2,1)S(1)}, u32[]{:S(2)}, u32[]{:S(2)}) %collective-permute-start.81) | collective-permute-done | bytes 262176 | tf_op jit(solution)/shard_map/ppermute | solution.py:667
  944.8 20.8 %collective-permute-done.74 = bf16[256,2048]{1,0:T(8,128)(2,1)S(1)} collective-permute-done((bf16[256,2048]{1,0:T(8,128)(2,1)S(1)}, bf16[256,2048]{1,0:T(8,128)(2,1)S(1)}, u32[]{:S(2)}, u32[]{:S(2)}) %collective-permute-start.74) | collective-permute-done | bytes 1048608 | tf_op jit(solution)/shard_map/ppermute | solution.py:667
  (730 shorter events, 545.3 us)
Async XLA Ops:
  2.7 78.2 %collective-permute-start.4 = (bf16[512,512]{1,0:T(8,128)(2,1)}, bf16[512,512]{1,0:T(8,128)(2,1)}, u32[]{:S(2)}, u32[]{:S(2)}) collective-permute-start(bf16[512,512]{1,0:T(8,128)(2,1)} %constant_dynamic-slice_fusion.12), channel_id=1, source_target_pairs={{0,1},{1,0},{2,3},{3,2},{4,5},{5,4},{6,7},{7,6},{8,9},{9,8},{10,11... | collective-permute-start | bytes 1572872 | tf_op jit(solution)/shard_map/ppermute | solution.py:655
  7.5 75.5 %collective-permute-start.2 = (bf16[512,512]{1,0:T(8,128)(2,1)}, bf16[512,512]{1,0:T(8,128)(2,1)}, u32[]{:S(2)}, u32[]{:S(2)}) collective-permute-start(bf16[512,512]{1,0:T(8,128)(2,1)} %constant_dynamic-slice_fusion.13), channel_id=1, source_target_pairs={{0,1},{1,0},{2,3},{3,2},{4,5},{5,4},{6,7},{7,6},{8,9},{9,8},{10,11... | collective-permute-start | bytes 1572872 | tf_op jit(solution)/shard_map/ppermute | solution.py:655
  9.4 77.3 %collective-permute-start = (bf16[512,512]{1,0:T(8,128)(2,1)}, bf16[512,512]{1,0:T(8,128)(2,1)}, u32[]{:S(2)}, u32[]{:S(2)}) collective-permute-start(bf16[512,512]{1,0:T(8,128)(2,1)} %constant_dynamic-slice_fusion.14), channel_id=1, source_target_pairs={{0,1},{1,0},{2,3},{3,2},{4,5},{5,4},{6,7},{7,6},{8,9},{9,8},{10,11... | collective-permute-start | bytes 1572872 | tf_op jit(solution)/shard_map/ppermute | solution.py:655
  11.5 58.0 %collective-permute-start.8 = (bf16[384,512]{1,0:T(8,128)(2,1)S(1)}, bf16[384,512]{1,0:T(8,128)(2,1)}, u32[]{:S(2)}, u32[]{:S(2)}) collective-permute-start(bf16[384,512]{1,0:T(8,128)(2,1)S(1)} %constant_dynamic-slice_fusion.9), channel_id=1, source_target_pairs={{0,1},{1,0},{2,3},{3,2},{4,5},{5,4},{6,7},{7,6},{8,9},{9,8},{10,11... | collective-permute-start | bytes 1179656 | tf_op jit(solution)/shard_map/ppermute | solution.py:655
  11.6 67.4 %collective-permute-start.10 = (f32[512]{0:T(512)S(1)}, f32[512]{0:T(512)S(1)}, u32[]{:S(2)}, u32[]{:S(2)}) collective-permute-start(f32[512]{0:T(512)S(1)} %copy-done.156), channel_id=1, source_target_pairs={{0,1},{1,0},{2,3},{3,2},{4,5},{5,4},{6,7},{7,6},{8,9},{9,8},{10,11... | collective-permute-start | bytes 6152 | tf_op jit(solution)/shard_map/ppermute | solution.py:655
  92.6 45.0 %collective-permute-start.17 = (bf16[256,1024]{1,0:T(8,128)(2,1)}, bf16[256,1024]{1,0:T(8,128)(2,1)}, u32[]{:S(2)}, u32[]{:S(2)}) collective-permute-start(bf16[256,1024]{1,0:T(8,128)(2,1)} %constant_dynamic-slice_fusion.5), channel_id=1, source_target_pairs={{0,1},{1,0},{2,3},{3,2},{4,5},{5,4},{6,7},{7,6},{8,9},{9,8},{10,11... | collective-permute-start | bytes 1572872 | tf_op jit(solution)/shard_map/ppermute | solution.py:655
  112.1 101.9 %collective-permute-start.19 = (bf16[512,2048]{1,0:T(8,128)(2,1)S(1)}, bf16[512,2048]{1,0:T(8,128)(2,1)}, u32[]{:S(2)}, u32[]{:S(2)}) collective-permute-start(bf16[512,2048]{1,0:T(8,128)(2,1)S(1)} %copy-done.77), channel_id=1, source_target_pairs={{0,1},{1,0},{2,3},{3,2},{4,5},{5,4},{6,7},{7,6},{8,9},{9,8},{10,11... | collective-permute-start | bytes 6291464 | tf_op jit(solution)/shard_map/ppermute | solution.py:655
  120.3 106.9 %collective-permute-start.21 = (bf16[1024,1024]{1,0:T(8,128)(2,1)}, bf16[1024,1024]{1,0:T(8,128)(2,1)}, u32[]{:S(2)}, u32[]{:S(2)}) collective-permute-start(bf16[1024,1024]{1,0:T(8,128)(2,1)} %constant_dynamic-slice_fusion.3), channel_id=1, source_target_pairs={{0,1},{1,0},{2,3},{3,2},{4,5},{5,4},{6,7},{7,6},{8,9},{9,8},{10,11... | collective-permute-start | bytes 6291464 | tf_op jit(solution)/shard_map/ppermute | solution.py:655
  476.2 118.0 %collective-permute-start.58 = (bf16[384,1024]{1,0:T(8,128)(2,1)}, bf16[384,1024]{1,0:T(8,128)(2,1)}, u32[]{:S(2)}, u32[]{:S(2)}) collective-permute-start(bf16[384,1024]{1,0:T(8,128)(2,1)} %convolution_convert_fusion.22), channel_id=1, source_target_pairs={{0,2},{2,0},{4,6},{6,4},{8,10},{10,8},{12,14},{14,12},{16,18},{18,... | collective-permute-start | bytes 2359304 | tf_op jit(solution)/shard_map/ppermute | solution.py:658
  476.8 93.3 %collective-permute-start.49 = (f32[5,1024]{1,0:T(8,128)S(1)}, f32[5,1024]{1,0:T(8,128)S(1)}, u32[]{:S(2)}, u32[]{:S(2)}) collective-permute-start(f32[5,1024]{1,0:T(8,128)S(1)} %stack.35), channel_id=1, source_target_pairs={{0,2},{2,0},{4,6},{6,4},{8,10},{10,8},{12,14},{14,12},{16,18},{18,... | collective-permute-start | bytes 61448 | tf_op jit(solution)/shard_map/ppermute | solution.py:658
  476.9 121.2 %collective-permute-start.40 = (bf16[1024,512]{1,0:T(8,128)(2,1)}, bf16[1024,512]{1,0:T(8,128)(2,1)}, u32[]{:S(2)}, u32[]{:S(2)}) collective-permute-start(bf16[1024,512]{1,0:T(8,128)(2,1)} %fusion.55), channel_id=1, source_target_pairs={{0,2},{2,0},{4,6},{6,4},{8,10},{10,8},{12,14},{14,12},{16,18},{18,... | collective-permute-start | bytes 3145736 | tf_op jit(solution)/shard_map/ppermute | solution.py:658
  593.6 144.6 %collective-permute-start.76 = (bf16[4096,512]{1,0:T(8,128)(2,1)}, bf16[4096,512]{1,0:T(8,128)(2,1)S(1)}, u32[]{:S(2)}, u32[]{:S(2)}) collective-permute-start(bf16[4096,512]{1,0:T(8,128)(2,1)} %fusion.20), channel_id=1, source_target_pairs={{0,2},{2,0},{4,6},{6,4},{8,10},{10,8},{12,14},{14,12},{16,18},{18,... | collective-permute-start | bytes 12582920 | tf_op jit(solution)/shard_map/ppermute | solution.py:658
  614.7 46.7 %collective-permute-start.32 = (bf16[1536,512]{1,0:T(8,128)(2,1)S(1)}, bf16[1536,512]{1,0:T(8,128)(2,1)S(1)}, u32[]{:S(2)}, u32[]{:S(2)}) collective-permute-start(bf16[1536,512]{1,0:T(8,128)(2,1)S(1)} %pad_maximum_fusion.35), channel_id=1, source_target_pairs={{0,1},{1,0},{2,3},{3,2},{4,5},{5,4},{6,7},{7,6},{8,9},{9,8},{10,11... | collective-permute-start | bytes 4718600 | tf_op jit(solution)/shard_map/ppermute | solution.py:655
  628.5 101.7 %collective-permute-start.59 = (bf16[2432,512]{1,0:T(8,128)(2,1)S(1)}, bf16[2432,512]{1,0:T(8,128)(2,1)S(1)}, u32[]{:S(2)}, u32[]{:S(2)}) collective-permute-start(bf16[2432,512]{1,0:T(8,128)(2,1)S(1)} %get-tuple-element.235), channel_id=1, source_target_pairs={{0,1},{1,0},{2,3},{3,2},{4,5},{5,4},{6,7},{7,6},{8,9},{9,8},{10,11... | collective-permute-start | bytes 7471112 | tf_op jit(solution)/shard_map/ppermute | solution.py:655
  630.6 111.1 %collective-permute-start.67 = (bf16[512,4096]{1,0:T(8,128)(2,1)}, bf16[512,4096]{1,0:T(8,128)(2,1)S(1)}, u32[]{:S(2)}, u32[]{:S(2)}) collective-permute-start(bf16[512,4096]{1,0:T(8,128)(2,1)} %fusion.22), channel_id=1, source_target_pairs={{0,2},{2,0},{4,6},{6,4},{8,10},{10,8},{12,14},{14,12},{16,18},{18,... | collective-permute-start | bytes 12582920 | tf_op jit(solution)/shard_map/ppermute | solution.py:658
  668.3 49.5 %collective-permute-start.23 = (bf16[128,768]{1,0:T(8,128)(2,1)S(1)}, bf16[128,768]{1,0:T(8,128)(2,1)S(1)}, u32[]{:S(2)}, u32[]{:S(2)}) collective-permute-start(bf16[128,768]{1,0:T(8,128)(2,1)S(1)} %fusion.65), channel_id=1, source_target_pairs={{0,1},{1,0},{2,3},{3,2},{4,5},{5,4},{6,7},{7,6},{8,9},{9,8},{10,11... | collective-permute-start | bytes 589832 | tf_op jit(solution)/shard_map/ppermute | solution.py:655
  679.2 40.3 %collective-permute-start.46 = (bf16[128,512]{1,0:T(8,128)(2,1)S(1)}, bf16[128,512]{1,0:T(8,128)(2,1)S(1)}, u32[]{:S(2)}, u32[]{:S(2)}) collective-permute-start(bf16[128,512]{1,0:T(8,128)(2,1)S(1)} %pad_maximum_fusion.78), channel_id=1, source_target_pairs={{0,8},{2,10},{4,12},{6,14},{8,0},{10,2},{12,4},{14,6},{16,24},{18,... | collective-permute-start | bytes 393224 | tf_op jit(solution)/shard_map/ppermute | solution.py:667
  720.2 54.6 %collective-permute-start.47 = (bf16[256,512]{1,0:T(8,128)(2,1)}, bf16[256,512]{1,0:T(8,128)(2,1)}, u32[]{:S(2)}, u32[]{:S(2)}) collective-permute-start(bf16[256,512]{1,0:T(8,128)(2,1)} %pad_maximum_fusion.75), channel_id=1, source_target_pairs={{0,4},{2,6},{4,0},{6,2},{8,12},{10,14},{12,8},{14,10},{16,20},{18,... | collective-permute-start | bytes 786440 | tf_op jit(solution)/shard_map/ppermute | solution.py:667
  740.1 64.3 %collective-permute-start.77 = (bf16[2048,512]{1,0:T(8,128)(2,1)S(1)}, bf16[2048,512]{1,0:T(8,128)(2,1)S(1)}, u32[]{:S(2)}, u32[]{:S(2)}) collective-permute-start(bf16[2048,512]{1,0:T(8,128)(2,1)S(1)} %get-tuple-element.149), channel_id=1, source_target_pairs={{0,1},{1,0},{2,3},{3,2},{4,5},{5,4},{6,7},{7,6},{8,9},{9,8},{10,11... | collective-permute-start | bytes 6291464 | tf_op jit(solution)/shard_map/ppermute | solution.py:655
  760.6 70.9 %collective-permute-start.68 = (bf16[512,2048]{1,0:T(8,128)(2,1)S(1)}, bf16[512,2048]{1,0:T(8,128)(2,1)S(1)}, u32[]{:S(2)}, u32[]{:S(2)}) collective-permute-start(bf16[512,2048]{1,0:T(8,128)(2,1)S(1)} %get-tuple-element.155), channel_id=1, source_target_pairs={{0,1},{1,0},{2,3},{3,2},{4,5},{5,4},{6,7},{7,6},{8,9},{9,8},{10,11... | collective-permute-start | bytes 6291464 | tf_op jit(solution)/shard_map/ppermute | solution.py:655
  775.9 57.0 %collective-permute-start.48 = (bf16[512,512]{1,0:T(8,128)(2,1)S(1)}, bf16[512,512]{1,0:T(8,128)(2,1)S(1)}, u32[]{:S(2)}, u32[]{:S(2)}) collective-permute-start(bf16[512,512]{1,0:T(8,128)(2,1)S(1)} %pad_maximum_fusion.67), channel_id=1, source_target_pairs={{0,2},{2,0},{4,6},{6,4},{8,10},{10,8},{12,14},{14,12},{16,18},{18,... | collective-permute-start | bytes 1572872 | tf_op jit(solution)/shard_map/ppermute | solution.py:658
  788.9 72.4 %collective-permute-start.39 = (bf16[1536,512]{1,0:T(8,128)(2,1)S(1)}, bf16[1536,512]{1,0:T(8,128)(2,1)S(1)}, u32[]{:S(2)}, u32[]{:S(2)}) collective-permute-start(bf16[1536,512]{1,0:T(8,128)(2,1)S(1)} %pad_maximum_fusion.33), channel_id=1, source_target_pairs={{0,2},{2,0},{4,6},{6,4},{8,10},{10,8},{12,14},{14,12},{16,18},{18,... | collective-permute-start | bytes 4718600 | tf_op jit(solution)/shard_map/ppermute | solution.py:658
  833.6 48.6 %collective-permute-start.65 = (bf16[1216,512]{1,0:T(8,128)(2,1)S(1)}, bf16[1216,512]{1,0:T(8,128)(2,1)S(1)}, u32[]{:S(2)}, u32[]{:S(2)}) collective-permute-start(bf16[1216,512]{1,0:T(8,128)(2,1)S(1)} %pad_maximum_fusion.37), channel_id=1, source_target_pairs={{0,4},{2,6},{4,0},{6,2},{8,12},{10,14},{12,8},{14,10},{16,20},{18,... | collective-permute-start | bytes 3735560 | tf_op jit(solution)/shard_map/ppermute | solution.py:667
  906.9 60.9 %collective-permute-start.66 = (bf16[2432,512]{1,0:T(8,128)(2,1)S(1)}, bf16[2432,512]{1,0:T(8,128)(2,1)S(1)}, u32[]{:S(2)}, u32[]{:S(2)}) collective-permute-start(bf16[2432,512]{1,0:T(8,128)(2,1)S(1)} %pad_maximum_fusion.18), channel_id=1, source_target_pairs={{0,2},{2,0},{4,6},{6,4},{8,10},{10,8},{12,14},{14,12},{16,18},{18,... | collective-permute-start | bytes 7471112 | tf_op jit(solution)/shard_map/ppermute | solution.py:658
  (228 other events, 2541.2 us)

commit v2 on v0

--- a/solution.py
+++ b/solution.py
@@ -1,8 +1,11 @@
+import functools
 from functools import reduce
 
 import jax
 import jax.numpy as jnp
 from jax import lax
+from jax.experimental import pallas as pl
+from jax.experimental.pallas import tpu as pltpu
 from jax.sharding import PartitionSpec as P
 
 HEAD_DIM = 64
@@ -371,9 +374,1013 @@
     )
 
 
+LOG2E=1.4426950408889634
+SCALE2=LOG2E*HEAD_DIM**-0.5
+BQ=256
+SPAN=768
+
+def dot(a,b,ca,cb):
+    return lax.dot_general(a,b,(((ca,),(cb,)),((),())),preferred_element_type=jnp.float32)
+
+def starts_of(bounds_ref, places):
+    start=jnp.zeros_like(places)
+    for k in range(3):
+        start=jnp.where(places>=bounds_ref[k],bounds_ref[k],start)
+    return start
+
+def self_fwd_kernel(bounds_ref,q_ref,k_ref,v_ref,o_ref,lse_ref,*,ahead=2):
+    low=lax.broadcasted_iota(jnp.int32,(1,128),1)<HEAD_DIM
+    vt=jnp.transpose(v_ref[...])
+    pad=jnp.ones((16,ROW_LEN),jnp.bfloat16)
+    vts=[jnp.concatenate([vt[64*h:64*h+64],pad],0) for h in range(2)]
+    def span(i):
+        return max(0,BQ*i-SPAN),BQ*(i+1)
+    def scores(i,h):
+        k0,k1=span(i)
+        q=q_ref[BQ*i:k1,:]
+        qh=jnp.where(low==(h==0),q,jnp.zeros_like(q))
+        places=BQ*i+lax.broadcasted_iota(jnp.int32,(1,BQ),1)
+        keys=k0+lax.broadcasted_iota(jnp.int32,(k1-k0,BQ),0)
+        allowed=(keys>=starts_of(bounds_ref,places))&(keys<=places)
+        return jnp.where(allowed,dot(k_ref[k0:k1,:],qh,1,1),MASKED)
+    items=[(i,h) for i in range(ROW_LEN//BQ) for h in range(2)]
+    queue=[scores(*it) for it in items[:ahead]]
+    outs=[]
+    for n,(i,h) in enumerate(items):
+        if n+ahead<len(items):
+            queue.append(scores(*items[n+ahead]))
+        s=queue.pop(0)
+        k0,k1=span(i)
+        m=jnp.max(s,axis=0,keepdims=True)
+        p=jnp.exp2((s-m)*SCALE2)
+        o=dot(vts[h][:,k0:k1],p.astype(jnp.bfloat16),1,0)
+        l=o[64:65]
+        outs.append(o[:64]*(1.0/l))
+        lse_ref[0,h:h+1,BQ*i:k1]=m*SCALE2+jnp.log2(l)
+        if h==1:
+            o_ref[BQ*i:k1,:]=jnp.transpose(jnp.concatenate(outs,0)).astype(jnp.bfloat16)
+            outs=[]
+
+def self_bwd_kernel(bounds_ref,q_ref,k_ref,v_ref,o_ref,g_ref,lse_ref,out_ref,acc_ref,d_ref,*,mode="t",ahead=1):
+    low=lax.broadcasted_iota(jnp.int32,(1,128),1)<HEAD_DIM
+    n=ROW_LEN//BQ
+    pair=pl.program_id(0)
+    width=128*pl.num_programs(0)
+    def put(which,sl,t):
+        at=pl.multiple_of(which*width+pair*128,128)
+        out_ref[sl,pl.ds(at,128)]=t.astype(jnp.bfloat16)
+
+    for i in range(n):
+        sl=slice(BQ*i,BQ*(i+1))
+        t=jnp.transpose(g_ref[sl,:].astype(jnp.float32)*o_ref[sl,:].astype(jnp.float32))
+        d_ref[0:1,sl]=jnp.sum(t[:64],axis=0,keepdims=True)
+        d_ref[1:2,sl]=jnp.sum(t[64:],axis=0,keepdims=True)
+    acc_ref[...]=jnp.zeros_like(acc_ref)
+    def span(j):
+        return BQ*j,min(ROW_LEN,BQ*(j+1)+SPAN)
+    def masked(ref,j,h):
+        t=ref[BQ*j:BQ*(j+1),:]
+        return jnp.where(low==(h==0),t,jnp.zeros_like(t))
+    def scores(j,h):
+        q0,q1=span(j)
+        places=q0+lax.broadcasted_iota(jnp.int32,(1,q1-q0),1)
+        keys=BQ*j+lax.broadcasted_iota(jnp.int32,(BQ,q1-q0),0)
+        allowed=(keys>=starts_of(bounds_ref,places))&(keys<=places)
+        s=dot(masked(k_ref,j,h),q_ref[q0:q1,:],1,1)*SCALE2-lse_ref[0,h:h+1,q0:q1]
+        return jnp.where(allowed,s,MASKED),dot(masked(v_ref,j,h),g_ref[q0:q1,:],1,1)
+    items=[(j,h) for j in range(n) for h in range(2)]
+    queue=[scores(*it) for it in items[:ahead]]
+    dks=[];dvs=[]
+    for t,(j,h) in enumerate(items):
+        if t+ahead<len(items):
+            queue.append(scores(*items[t+ahead]))
+        s,dp=queue.pop(0)
+        sl=slice(BQ*j,BQ*(j+1))
+        q0,q1=span(j)
+        p=jnp.exp2(s)
+        ds=(p*(dp-d_ref[h:h+1,q0:q1])).astype(jnp.bfloat16)
+        dvs.append(dot(p.astype(jnp.bfloat16),g_ref[q0:q1,:],1,0))
+        dks.append(dot(ds,q_ref[q0:q1,:],1,0))
+        if mode=="t":
+            kt=jnp.transpose(k_ref[sl,:])
+            acc_ref[64*h:64*h+64,q0:q1]+=dot(kt[64*h:64*h+64],ds,1,0)
+        else:
+            acc_ref[q0:q1,:]+=dot(ds,masked(k_ref,j,h),0,0)
+        if h==1:
+            put(1,sl,jnp.where(low,dks[0],dks[1])*HEAD_DIM**-0.5)
+            put(2,sl,jnp.where(low,dvs[0],dvs[1]))
+            dks=[];dvs=[]
+            acc=jnp.transpose(acc_ref[:,sl]) if mode=="t" else acc_ref[sl,:]
+            put(0,sl,acc*HEAD_DIM**-0.5)
+
+
+def group_forward(bounds,qkv):
+    width=qkv.shape[1]//3
+    pairs=width//128
+    spec=lambda t: pl.BlockSpec((ROW_LEN,128),lambda h:(0,t*pairs+h))
+    return pl.pallas_call(self_fwd_kernel,grid=(pairs,),
+        in_specs=[pl.BlockSpec(memory_space=pltpu.SMEM),spec(0),spec(1),spec(2)],
+        out_specs=[spec(0),pl.BlockSpec((1,2,ROW_LEN),lambda h:(h,0,0))],
+        out_shape=[jax.ShapeDtypeStruct((ROW_LEN,width),jnp.bfloat16),jax.ShapeDtypeStruct((pairs,2,ROW_LEN),jnp.float32)],
+        compiler_params=pltpu.CompilerParams(vmem_limit_bytes=40<<20),
+        name="self_forward",
+        cost_estimate=pl.CostEstimate(flops=pairs*2*18*256*256*64*4*4,bytes_accessed=pairs*4*1536*256,transcendentals=0),
+    )(bounds,qkv,qkv,qkv)
+
+def group_backward(bounds,qkv,o,g,lse,group):
+    width=qkv.shape[1]//3
+    pairs=width//128
+    spec=lambda t: pl.BlockSpec((ROW_LEN,128),lambda h:(0,t*pairs+h))
+    return pl.pallas_call(self_bwd_kernel,grid=(pairs,),
+        in_specs=[pl.BlockSpec(memory_space=pltpu.SMEM),spec(0),spec(1),spec(2),spec(0),spec(group),pl.BlockSpec((1,2,ROW_LEN),lambda h:(h,0,0))],
+        out_specs=pl.BlockSpec((ROW_LEN,3*width),lambda h:(0,0)),
+        out_shape=jax.ShapeDtypeStruct(qkv.shape,jnp.bfloat16),
+        scratch_shapes=[pltpu.VMEM((128,ROW_LEN),jnp.float32),pltpu.VMEM((8,ROW_LEN),jnp.float32)],
+        compiler_params=pltpu.CompilerParams(vmem_limit_bytes=48<<20),
+        name="self_backward",
+        cost_estimate=pl.CostEstimate(flops=pairs*2*18*256*256*64*10*4,bytes_accessed=pairs*8*1536*256,transcendentals=0),
+    )(bounds,qkv,qkv,qkv,o,g,lse)
+
+def token_range(cb_ref,tb_ref,places):
+    lo=jnp.zeros_like(places); hi=jnp.full_like(places,0)+tb_ref[0]
+    for c in range(3):
+        past=places>=cb_ref[c]
+        lo=jnp.where(past,tb_ref[c],lo)
+        hi=jnp.where(past,tb_ref[c+1],hi)
+    return lo,hi
+
+
+INV_SQRT_2PI = 0.3989422804014327
+TB = 256
+NB = 512
+
+
+def mean_row(t):
+    return jnp.sum(t, axis=-1, keepdims=True) * (1.0 / t.shape[-1])
+
+
+def standardise(t):
+    centered = t - mean_row(t)
+    inverse = lax.rsqrt(mean_row(centered * centered) + EPSILON)
+    return centered * inverse, inverse
+
+
+def norm_input_grad(e, standard, inverse, gain):
+    scaled = e * gain
+    return inverse * (scaled - mean_row(scaled) - standard * mean_row(scaled * standard))
+
+
+def column_sums(t):
+    return jnp.sum(t, axis=0, keepdims=True)
+
+
+def gelu_pair(hidden):
+    density = jnp.exp2(hidden * hidden * (-0.5 * LOG2E)) * INV_SQRT_2PI
+    t = 1.0 / (1.0 + 0.2316419 * jnp.abs(hidden))
+    series = t * (
+        0.319381530
+        + t * (-0.356563782 + t * (1.781477937 + t * (-1.821255978 + t * 1.330274429)))
+    )
+    tail = density * series
+    below = jnp.where(hidden >= 0, 1.0 - tail, tail)
+    return hidden * below, below + hidden * density
+
+
+def mid_forward_kernel(
+    count, cb_ref, tb_ref, x_ref, *refs,
+):
+    ctxs, sos, cqs, cos = [refs[count * t : count * t + count] for t in range(4)]
+    (k_ref, v_ref, vec_ref,
+     mid_ref, rows_ref, q_ref, cctx_ref, lse_ref, after_ref, feed_ref, feedt_ref, vt_ref) = refs[4 * count :]
+    i = pl.program_id(0)
+    low = lax.broadcasted_iota(jnp.int32, (1, 128), 1) < HEAD_DIM
+
+    @pl.when(i == 0)
+    def _():
+        vt_ref[0:1024, :] = jnp.transpose(v_ref[...])
+        vt_ref[1024:1040, :] = jnp.ones((16, TXT_ROW), jnp.bfloat16)
+
+    middle = x_ref[...].astype(jnp.float32)
+    for c, w in zip(ctxs, sos):
+        middle = middle + dot(c[...], w[...], 1, 0)
+    mid_ref[...] = middle
+    u, _ = standardise(middle)
+    rows = (u * vec_ref[0:1, :] + vec_ref[1:2, :]).astype(jnp.bfloat16)
+    rows_ref[...] = rows
+    at = 0
+    for w in cqs:
+        n = w.shape[1]
+        q_ref[:, at : at + n] = dot(rows, w[...], 1, 0).astype(jnp.bfloat16)
+        at += n
+    places = TB * i + lax.broadcasted_iota(jnp.int32, (1, TB), 1)
+    lo, hi = token_range(cb_ref, tb_ref, places)
+    toks = lax.broadcasted_iota(jnp.int32, (TXT_ROW, TB), 0)
+    allowed = (toks >= lo) & (toks < hi)
+
+    def scores(head):
+        p, h = head // 2, head % 2
+        k = k_ref[:, 128 * p : 128 * p + 128]
+        kh = jnp.where(low == (h == 0), k, jnp.zeros_like(k))
+        return jnp.where(allowed, dot(kh, q_ref[:, 128 * p : 128 * p + 128], 1, 1), MASKED)
+
+    ahead = 3
+    queue = [scores(t) for t in range(ahead)]
+    outs = []
+    ones = vt_ref[1024:1040, :]
+    for head in range(16):
+        if head + ahead < 16:
+            queue.append(scores(head + ahead))
+        s = queue.pop(0)
+        m = jnp.max(s, axis=0, keepdims=True)
+        p = jnp.exp2((s - m) * SCALE2)
+        vt = jnp.concatenate([vt_ref[64 * head : 64 * head + 64, :], ones], 0)
+        o = dot(vt, p.astype(jnp.bfloat16), 1, 0)
+        l = o[64:65]
+        outs.append(o[:64] * (1.0 / l))
+        lse_ref[head : head + 1, :] = m * SCALE2 + jnp.log2(l)
+        if head % 2 == 1:
+            pair = head // 2
+            cctx_ref[:, 128 * pair : 128 * pair + 128] = jnp.transpose(
+                jnp.concatenate(outs, 0)
+            ).astype(jnp.bfloat16)
+            outs = []
+    after = mid_ref[...]
+    at = 0
+    for w in cos:
+        n = w.shape[0]
+        after = after + dot(cctx_ref[:, at : at + n], w[...], 1, 0)
+        at += n
+    after_ref[...] = after
+    u, _ = standardise(after)
+    feed = (u * vec_ref[2:3, :] + vec_ref[3:4, :]).astype(jnp.bfloat16)
+    feed_ref[...] = feed
+    feedt_ref[...] = jnp.transpose(feed)
+
+
+def row_block(n):
+    return pl.BlockSpec((TB, n), lambda i: (i, 0))
+
+
+def whole(t):
+    return pl.BlockSpec(t.shape, lambda i: (0,) * t.ndim)
+
+
+def mid_forward(cb, tb, x, ctxs, sos, cqs, cos, k, v, vec):
+    n, d = x.shape
+    smem = pl.BlockSpec(memory_space=pltpu.SMEM)
+    bf, f = jnp.bfloat16, jnp.float32
+    weights = [*sos, *cqs, *cos, k, v, vec]
+    return pl.pallas_call(
+        functools.partial(mid_forward_kernel, len(ctxs)),
+        grid=(n // TB,),
+        in_specs=[smem, smem, row_block(d)] + [row_block(c.shape[1]) for c in ctxs] + [whole(w) for w in weights],
+        out_specs=[row_block(d)] * 4
+        + [pl.BlockSpec((16, TB), lambda i: (0, i))]
+        + [row_block(d)] * 2
+        + [pl.BlockSpec((d, TB), lambda i: (0, i))],
+        out_shape=[jax.ShapeDtypeStruct((n, d), t) for t in (f, bf, bf, bf)]
+        + [jax.ShapeDtypeStruct((16, n), f)]
+        + [jax.ShapeDtypeStruct((n, d), t) for t in (f, bf)]
+        + [jax.ShapeDtypeStruct((d, n), bf)],
+        scratch_shapes=[pltpu.VMEM((1040, TXT_ROW), bf)],
+        compiler_params=pltpu.CompilerParams(vmem_limit_bytes=56 << 20),
+        name="mid_forward",
+        cost_estimate=pl.CostEstimate(flops=24 * n * d * d // 2, bytes_accessed=40 * n * d // 2, transcendentals=0),
+    )(cb, tb, x, *ctxs, *weights)
+
+
+def mid_backward_kernel(
+    count, cb_ref, tb_ref, e_ref, after_ref, g_ref, mid_ref, q_ref, cctx_ref, lse_ref, *refs,
+):
+    cos, cqs, sos = [refs[count * t : count * t + count] for t in range(3)]
+    (k_ref, v_ref, vec_ref,
+     gc_ref, gq_ref, gmid_ref, gs_ref, gctx_ref, dk_ref, dv_ref, sums_ref,
+     kt_ref, dka_ref, dva_ref, gcc_ref) = refs[3 * count :]
+    i = pl.program_id(0)
+    low = lax.broadcasted_iota(jnp.int32, (1, 128), 1) < HEAD_DIM
+
+    @pl.when(i == 0)
+    def _():
+        kt_ref[...] = jnp.transpose(k_ref[...])
+        dka_ref[...] = jnp.zeros_like(dka_ref)
+        dva_ref[...] = jnp.zeros_like(dva_ref)
+        sums_ref[...] = jnp.zeros_like(sums_ref)
+
+    e = e_ref[...]
+    u, inverse = standardise(after_ref[...])
+    sums_ref[0:1, :] += column_sums(e * u)
+    sums_ref[1:2, :] += column_sums(e)
+    g_after = g_ref[...].astype(jnp.float32) + norm_input_grad(e, u, inverse, vec_ref[2:3, :])
+    gmid_ref[...] = g_after
+    gc = g_after.astype(jnp.bfloat16)
+    gc_ref[...] = gc
+    at = 0
+    for w in cos:
+        n = w.shape[0]
+        gcc_ref[:, at : at + n] = dot(gc, w[...], 1, 1).astype(jnp.bfloat16)
+        at += n
+    places = TB * i + lax.broadcasted_iota(jnp.int32, (1, TB), 1)
+    lo, hi = token_range(cb_ref, tb_ref, places)
+    toks = lax.broadcasted_iota(jnp.int32, (TXT_ROW, TB), 0)
+    allowed = (toks >= lo) & (toks < hi)
+
+    def scores(head):
+        p, h = head // 2, head % 2
+        sl = slice(128 * p, 128 * p + 128)
+        pick = lambda t: jnp.where(low == (h == 0), t, jnp.zeros_like(t))
+        s = dot(pick(k_ref[:, sl]), q_ref[:, sl], 1, 1) * SCALE2 - lse_ref[head : head + 1, :]
+        return jnp.where(allowed, s, MASKED), dot(pick(v_ref[:, sl]), gcc_ref[:, sl], 1, 1)
+
+    ahead = 2
+    queue = [scores(t) for t in range(ahead)]
+    dqs, dks, dvs = [], [], []
+    for head in range(16):
+        if head + ahead < 16:
+            queue.append(scores(head + ahead))
+        p_at, h = head // 2, head % 2
+        sl = slice(128 * p_at, 128 * p_at + 128)
+        if h == 0:
+            t = jnp.transpose(
+                gcc_ref[:, sl].astype(jnp.float32) * cctx_ref[:, sl].astype(jnp.float32)
+            )
+        s, dp = queue.pop(0)
+        p = jnp.exp2(s)
+        ds = (p * (dp - column_sums(t[64 * h : 64 * h + 64]))).astype(jnp.bfloat16)
+        dvs.append(dot(p.astype(jnp.bfloat16), gcc_ref[:, sl], 1, 0))
+        dks.append(dot(ds, q_ref[:, sl], 1, 0))
+        dqs.append(dot(kt_ref[64 * head : 64 * head + 64, :], ds, 1, 0))
+        if h == 1:
+            gq_ref[:, sl] = (
+                jnp.transpose(jnp.concatenate(dqs, 0)) * HEAD_DIM**-0.5
+            ).astype(jnp.bfloat16)
+            dka_ref[:, sl] += jnp.where(low, dks[0], dks[1])
+            dva_ref[:, sl] += jnp.where(low, dvs[0], dvs[1])
+            dqs, dks, dvs = [], [], []
+    e = None
+    at = 0
+    for w in cqs:
+        n = w.shape[1]
+        part = dot(gq_ref[:, at : at + n], w[...], 1, 1)
+        e = part if e is None else e + part
+        at += n
+    u, inverse = standardise(mid_ref[...])
+    sums_ref[2:3, :] += column_sums(e * u)
+    sums_ref[3:4, :] += column_sums(e)
+    g_middle = gmid_ref[...] + norm_input_grad(e, u, inverse, vec_ref[0:1, :])
+    gmid_ref[...] = g_middle
+    gs = g_middle.astype(jnp.bfloat16)
+    gs_ref[...] = gs
+    at = 0
+    for w in sos:
+        n = w.shape[0]
+        gctx_ref[:, at : at + n] = dot(gs, w[...], 1, 1).astype(jnp.bfloat16)
+        at += n
+
+    @pl.when(i == pl.num_programs(0) - 1)
+    def _():
+        dk_ref[...] = (dka_ref[...] * HEAD_DIM**-0.5).astype(jnp.bfloat16)
+        dv_ref[...] = dva_ref[...].astype(jnp.bfloat16)
+
+
+def mid_backward(cb, tb, e, after, g, middle, q, cctx, lse, cos, cqs, sos, k, v, vec):
+    n, d = after.shape
+    smem = pl.BlockSpec(memory_space=pltpu.SMEM)
+    bf, f = jnp.bfloat16, jnp.float32
+    weights = [*cos, *cqs, *sos, k, v, vec]
+    text = jax.ShapeDtypeStruct((TXT_ROW, d), bf)
+    sums = jax.ShapeDtypeStruct((8, d), f)
+    return pl.pallas_call(
+        functools.partial(mid_backward_kernel, len(cos)),
+        grid=(n // TB,),
+        in_specs=[smem, smem] + [row_block(d)] * 6 + [pl.BlockSpec((16, TB), lambda i: (0, i))] + [whole(w) for w in weights],
+        out_specs=[row_block(d)] * 5 + [whole(text), whole(text), whole(sums)],
+        out_shape=[jax.ShapeDtypeStruct((n, d), t) for t in (bf, bf, f, bf, bf)] + [text, text, sums],
+        scratch_shapes=[
+            pltpu.VMEM((d, TXT_ROW), bf),
+            pltpu.VMEM((TXT_ROW, d), f),
+            pltpu.VMEM((TXT_ROW, d), f),
+            pltpu.VMEM((TB, d), bf),
+        ],
+        compiler_params=pltpu.CompilerParams(vmem_limit_bytes=58 << 20),
+        name="mid_backward",
+        cost_estimate=pl.CostEstimate(flops=40 * n * d * d // 2, bytes_accessed=46 * n * d // 2, transcendentals=0),
+    )(cb, tb, e, after, g, middle, q, cctx, lse, *weights)
+
+
+def feed_kernel(
+    idx_ref, fr_hbm, frt_hbm, cot_hbm, o_in, e_in, *refs, own, first, last
+):
+    if own:
+        fi_src, fo_src = refs[:2]
+        refs = refs[2:]
+    else:
+        fi_srcs, fo_srcs = refs[:2], refs[2:4]
+        refs = refs[4:]
+    (o_out, e_out, gi_ref, go_ref, fr_ref, frt_ref, cot_ref, out_ref, acc_o, acc_e,
+     fi_buf, fo_buf, act_s, gh_s, wsem, isem, asem) = refs
+    p = pl.program_id(0)
+    slot = p % 2
+    rows = 256
+    blocks = fr_hbm.shape[0] // rows
+
+    def weights(step, into, act):
+        if own:
+            at = pl.multiple_of(idx_ref[step] * NB, NB)
+            act(pltpu.make_async_copy(fi_src.at[:, pl.ds(at, NB)], fi_buf.at[into], wsem.at[into, 0]))
+            act(pltpu.make_async_copy(fo_src.at[pl.ds(at, NB), :], fo_buf.at[into], wsem.at[into, 1]))
+        else:
+            for s in range(2):
+                @pl.when(step == s)
+                def _(s=s):
+                    act(pltpu.make_async_copy(fi_srcs[s], fi_buf.at[into], wsem.at[into, 0]))
+                    act(pltpu.make_async_copy(fo_srcs[s], fo_buf.at[into], wsem.at[into, 1]))
+
+    def cut(r):
+        return slice(rows * r, rows * r + rows)
+
+    def row_in(r):
+        return [
+            pltpu.make_async_copy(fr_hbm.at[cut(r), :], fr_ref.at[cut(r), :], isem.at[0, r]),
+            pltpu.make_async_copy(cot_hbm.at[cut(r), :], cot_ref.at[cut(r), :], isem.at[1, r]),
+        ]
+
+    def sums_in(r):
+        loads = [pltpu.make_async_copy(o_in.at[cut(r), :], acc_o.at[cut(r), :], asem.at[0, r])]
+        if not first:
+            loads.append(pltpu.make_async_copy(e_in.at[cut(r), :], acc_e.at[cut(r), :], asem.at[1, r]))
+        return loads
+
+    def sums_out(r):
+        stores = [pltpu.make_async_copy(acc_e.at[cut(r), :], e_out.at[cut(r), :], asem.at[1, r])]
+        source = out_ref if last else acc_o
+        stores.append(pltpu.make_async_copy(source.at[cut(r), :], o_out.at[cut(r), :], asem.at[0, r]))
+        return stores
+
+    turned = pltpu.make_async_copy(frt_hbm, frt_ref, isem.at[2, 0])
+
+    @pl.when(p == 0)
+    def _():
+        weights(p, slot, lambda c: c.start())
+        for c in row_in(0) + row_in(1) + sums_in(0):
+            c.start()
+        if first:
+            acc_e[...] = jnp.zeros_like(acc_e)
+        for c in row_in(0):
+            c.wait()
+
+    weights(p, slot, lambda c: c.wait())
+
+    @pl.when(p == 0)
+    def _():
+        weights(p + 1, 1 - slot, lambda c: c.start())
+
+    fi, fo = fi_buf.at[slot], fo_buf.at[slot]
+
+    def products(r):
+        return dot(fr_ref[cut(r), :], fi[...], 1, 0), dot(cot_ref[cut(r), :], fo[...], 1, 1)
+
+    def whole_pass(arriving):
+        queue = [products(0)]
+        for r in range(blocks):
+            if arriving:
+                for c in (row_in(r + 1) if r + 1 < blocks else []) + sums_in(r):
+                    c.wait()
+                for c in (row_in(r + 2) if r + 2 < blocks else []) + (
+                    sums_in(r + 1) if r + 1 < blocks else []
+                ):
+                    c.start()
+                if r == 2:
+                    turned.start()
+            elif r > 0:
+                for c in sums_out(r - 1):
+                    c.start()
+            if r + 1 < blocks:
+                queue.append(products(r + 1))
+            h, g = queue.pop(0)
+            active, slope = gelu_pair(h)
+            active = active.astype(jnp.bfloat16)
+            gh = (g * slope).astype(jnp.bfloat16)
+            act_s[cut(r), :] = active
+            gh_s[cut(r), :] = gh
+            o_sum = acc_o[cut(r), :] + dot(active, fo[...], 1, 0)
+            if last and not arriving:
+                out_ref[cut(r), :] = o_sum.astype(jnp.bfloat16)
+            else:
+                acc_o[cut(r), :] = o_sum
+            acc_e[cut(r), :] += dot(gh, fi[...], 1, 1)
+        if not arriving:
+            for c in sums_out(blocks - 1):
+                c.start()
+        if arriving:
+            turned.wait()
+        gi_ref[...] = dot(frt_ref[...], gh_s[...], 1, 0).astype(jnp.bfloat16)
+        go_ref[...] = dot(act_s[...], cot_ref[...], 0, 0).astype(jnp.bfloat16)
+        if not arriving:
+            for r in range(blocks):
+                for c in sums_out(r):
+                    c.wait()
+
+    @pl.when(p == 0)
+    def _():
+        whole_pass(True)
+
+    @pl.when(p == 1)
+    def _():
+        whole_pass(False)
+
+
+def feed_part(idx, rows, rows_t, cot, o_in, e_in, fis, fos, first, last):
+    n, d = rows.shape
+    own = len(fis) == 1
+    bf, f = jnp.bfloat16, jnp.float32
+    hbm = pl.BlockSpec(memory_space=pl.ANY)
+    grad = lambda shape: jax.ShapeDtypeStruct(shape, bf)
+    blocks = n // 256
+    return pl.pallas_call(
+        functools.partial(feed_kernel, own=own, first=first, last=last),
+        grid_spec=pltpu.PrefetchScalarGridSpec(
+            num_scalar_prefetch=1,
+            grid=(2,),
+            in_specs=[hbm] * (5 + 2 * len(fis)),
+            out_specs=[
+                hbm,
+                hbm,
+                pl.BlockSpec((d, NB), lambda p, idx: (0, idx[p] % 2)),
+                pl.BlockSpec((NB, d), lambda p, idx: (idx[p] % 2, 0)),
+            ],
+            scratch_shapes=[
+                pltpu.VMEM((n, d), bf),
+                pltpu.VMEM((d, n), bf),
+                pltpu.VMEM((n, d), bf),
+                pltpu.VMEM((n, d) if last else (16, 128), bf),
+                pltpu.VMEM((n, d), f),
+                pltpu.VMEM((n, d), f),
+                pltpu.VMEM((2, d, NB), bf),
+                pltpu.VMEM((2, NB, d), bf),
+                pltpu.VMEM((n, NB), bf),
+                pltpu.VMEM((n, NB), bf),
+                pltpu.SemaphoreType.DMA((2, 2)),
+                pltpu.SemaphoreType.DMA((3, blocks)),
+                pltpu.SemaphoreType.DMA((2, blocks)),
+            ],
+        ),
+        out_shape=[
+            jax.ShapeDtypeStruct((n, d), bf if last else f),
+            jax.ShapeDtypeStruct((n, d), f),
+            grad((d, 2 * NB)),
+            grad((2 * NB, d)),
+        ],
+        compiler_params=pltpu.CompilerParams(vmem_limit_bytes=60 << 20),
+        name="feed_last" if last else "feed_first" if first else "feed_more",
+        cost_estimate=pl.CostEstimate(flops=24 * n * d * NB, bytes_accessed=48 << 20, transcendentals=0),
+    )(idx, rows, rows_t, cot, o_in, e_in, *fis, *fos)
+
+
+def final_kernel(x_ref, gmid_ref, *refs):
+    count = (len(refs) - 3) // 2
+    gs, ws = refs[:count], refs[count : 2 * count]
+    vec_ref, out_ref, sums_ref = refs[2 * count :]
+
+    @pl.when(pl.program_id(0) == 0)
+    def _():
+        sums_ref[...] = jnp.zeros_like(sums_ref)
+
+    e = None
+    for g, w in zip(gs, ws):
+        part = dot(g[...], w[...], 1, 1)
+        e = part if e is None else e + part
+    u, inverse = standardise(x_ref[...].astype(jnp.float32))
+    sums_ref[0:1, :] += column_sums(e * u)
+    sums_ref[1:2, :] += column_sums(e)
+    out_ref[...] = gmid_ref[...] + norm_input_grad(e, u, inverse, vec_ref[4:5, :])
+
+
+def final_grads(x, gmid, gs, ws, vec):
+    n, d = x.shape
+    sums = jax.ShapeDtypeStruct((8, d), jnp.float32)
+    return pl.pallas_call(
+        final_kernel,
+        grid=(n // TB,),
+        in_specs=[row_block(d), row_block(d)] + [row_block(g.shape[1]) for g in gs] + [whole(w) for w in ws] + [whole(vec)],
+        out_specs=[row_block(d), whole(sums)],
+        out_shape=[jax.ShapeDtypeStruct((n, d), jnp.float32), sums],
+        compiler_params=pltpu.CompilerParams(vmem_limit_bytes=56 << 20),
+        name="frames_gradient",
+        cost_estimate=pl.CostEstimate(flops=6 * n * d * d, bytes_accessed=24 * n * d // 2, transcendentals=0),
+    )(x, gmid, *gs, *ws, vec)
+
+
+class Journey:
+    def __init__(self, hops):
+        self.hops = hops
+        self.pending = next(hops)
+        self.result = None
+
+    def go(self, tied):
+        try:
+            self.pending = self.hops.send(tied)
+        except StopIteration as end:
+            self.pending, self.result = None, end.value
+
+
+def onward(main, *journeys):
+    main, tied = lax.optimization_barrier((main, [j.pending for j in journeys]))
+    for journey, sent in zip(journeys, tied):
+        journey.go(sent)
+    return main
+
+
+def row_body(dp, *args):
+    (
+        frames,
+        text_states,
+        clip_lengths,
+        text_lengths,
+        cotangent,
+        self_gain,
+        self_shift,
+        self_query,
+        self_key,
+        self_value,
+        self_out,
+        cross_gain,
+        cross_shift,
+        cross_query,
+        cross_key,
+        cross_value,
+        cross_out,
+        text_weight,
+        text_bias,
+        feed_gain,
+        feed_shift,
+        feed_in,
+        feed_out,
+    ) = args
+    bf16, f32 = jnp.bfloat16, jnp.float32
+    me = lax.axis_index("dp")
+    half = lax.axis_index("mp")
+    core = me % 2
+    swap = [(0, 1), (1, 0)]
+    steps = [2 << i for i in range(dp.bit_length() - 2)]
+
+    def over_y(t):
+        return jax.tree.map(lambda a: lax.ppermute(a, "mp", swap), t)
+
+    def over_bit(t, step):
+        return jax.tree.map(lambda a: lax.ppermute(a, "dp", [(i, i ^ step) for i in range(dp)]), t)
+
+    def over_core(t):
+        return over_bit(t, 1)
+
+    def piece(t, at, size, axis):
+        return lax.dynamic_slice_in_dim(t, at * size, size, axis)
+
+    def ordered(mine_first, mine, theirs, axis):
+        return jnp.concatenate(
+            [jnp.where(mine_first, mine, theirs), jnp.where(mine_first, theirs, mine)], axis
+        )
+
+    def add(*ts):
+        return reduce(jnp.add, [t.astype(f32) for t in ts]).astype(bf16)
+
+    def parts_of(ts, step):
+        at = (me // step) % 2
+        size = ts[0].shape[0] // 2
+        return [add(*[piece(t, w, size, 0) for t in ts]) for w in (at, 1 - at)]
+
+    def travel(terms, left):
+        for step in left:
+            kept, sent = parts_of(terms, step)
+            sent = yield sent
+            terms = (kept, over_bit(sent, step))
+        block = add(*terms)
+        for step in reversed(steps):
+            block = yield block
+            block = ordered((me // step) % 2 == 0, block, over_bit(block, step), 0)
+        block = yield block
+        return block, over_core(block)
+
+    def travel_y(own, other):
+        other = yield other
+        return (yield from travel((*own, over_y(other)), steps))
+
+    def travel_small(t):
+        for hop in (over_core, over_y, *[functools.partial(over_bit, step=s) for s in steps]):
+            t = yield t
+            t = t + hop(t)
+        return t
+
+    lengths = lax.dynamic_index_in_dim(clip_lengths, half, 0, keepdims=False)
+    words = lax.dynamic_index_in_dim(text_lengths, half, 0, keepdims=False)
+    clip_bounds, text_bounds = jnp.cumsum(lengths), jnp.cumsum(words)
+    zeros = jnp.zeros_like(self_gain)
+    vec = jnp.stack(
+        [cross_gain, cross_shift, feed_gain, feed_shift, self_gain, zeros, zeros, zeros]
+    )
+
+    def quarter(t, which, axis):
+        return piece(t, which, t.shape[axis] // 2, axis)
+
+    tie = lax.optimization_barrier
+    x_at = (me // 2) % 2
+
+    def shared(mine, axis):
+        return quarter(mine, x_at, axis)
+
+    def joined(came, across, axis):
+        return ordered(x_at == 0, came, across, axis)
+
+    trio = (self_query, self_key, self_value)
+    qkv_c = jnp.concatenate([quarter(t, core, 1) for t in trio], 1)
+    qkv_d = jnp.concatenate([quarter(t, 1 - core, 1) for t in trio], 1)
+    text_part = (product(text_states, text_weight) + text_bias).astype(bf16)
+    qkv_half = shared(qkv_c, 0)
+    cut = qkv_half.shape[0] // 2
+    frames, text_part, qkv_1, qkv_2 = tie((frames, text_part, qkv_half[:cut], qkv_half[cut:]))
+    text_came, qkv_1 = over_y(text_part), over_y(qkv_1)
+    standard, _ = norm_parts(frames.astype(f32))
+    self_rows = (standard * self_gain + self_shift).astype(bf16)
+    qkv, ctx, log = [None] * 4, [None] * 4, [None] * 4
+    qkv[0] = product(self_rows, qkv_c).astype(bf16)
+    qkv[2] = product(self_rows, qkv_d).astype(bf16)
+    qkv[0], qkv[2], text_came, qkv_1, qkv_2 = tie((qkv[0], qkv[2], text_came, qkv_1, qkv_2))
+    text_full = ordered(half == 0, text_part, text_came, 1)
+    keys_here = product(text_full, cross_key).astype(bf16)
+    values_here = product(text_full, cross_value).astype(bf16)
+    text_rows = TXT_ROW
+
+    def row_of(t, which):
+        return piece(t, which, text_rows, 0)
+
+    kv_send = jnp.concatenate([row_of(keys_here, 1 - half), row_of(values_here, 1 - half)], 1)
+    qkv_2, across_1 = over_y(qkv_2), over_bit(qkv_1, 2)
+    ctx[0], log[0] = group_forward(clip_bounds, qkv[0])
+    so_c, cq_c, co_c = quarter(self_out, core, 0), quarter(cross_query, core, 1), quarter(cross_out, core, 0)
+    late = [shared(so_c, 0), shared(cq_c, 0), shared(co_c, 0)]
+    ctx[0], qkv[2], qkv_2, across_1, kv_send, late = tie(
+        (ctx[0], qkv[2], qkv_2, across_1, kv_send, late)
+    )
+    across_2 = over_bit(qkv_2, 2)
+    kv_came = over_y(kv_send)
+    so_h = over_y(late[0])
+    ctx[2], log[2] = group_forward(clip_bounds, qkv[2])
+    ctx[2], across_2, kv_came, so_h = tie((ctx[2], across_2, kv_came, so_h))
+    qkv_oc = joined(jnp.concatenate([qkv_1, qkv_2]), jnp.concatenate([across_1, across_2]), 0)
+    qkv_oc, rows_1, so_h = tie((qkv_oc, self_rows, so_h))
+    qkv_od = over_core(qkv_oc)
+    cq_h, so_x = over_y(late[1]), over_bit(so_h, 2)
+    qkv[1] = product(rows_1, qkv_oc).astype(bf16)
+    qkv[1], cq_h = tie((qkv[1], cq_h))
+    co_h, cq_x = over_y(late[2]), over_bit(cq_h, 2)
+    ctx[1], log[1] = group_forward(clip_bounds, qkv[1])
+    qkv[3] = product(self_rows, qkv_od).astype(bf16)
+    so_oc, cq_oc = joined(so_h, so_x, 0), joined(cq_h, cq_x, 0)
+    qkv[3], ctx[1], co_h, so_oc, cq_oc = tie((qkv[3], ctx[1], co_h, so_oc, cq_oc))
+    co_x = over_bit(co_h, 2)
+    so_od, cq_od = over_core(so_oc), over_core(cq_oc)
+    ctx[3], log[3] = group_forward(clip_bounds, qkv[3])
+    co_oc = joined(co_h, co_x, 0)
+    co_od = over_core(co_oc)
+    width = cross_key.shape[1]
+
+    def mixed(mine, theirs):
+        mine = row_of(mine, half)
+        return jnp.concatenate(
+            [quarter(t, w, 1) for w in (core, 1 - core) for t in (mine, theirs)], 1
+        )
+
+    keys = mixed(keys_here, kv_came[:, :width])
+    values = mixed(values_here, kv_came[:, width:])
+    qkv_w = [qkv_c, qkv_oc, qkv_d, qkv_od]
+    so = [so_c, so_oc, quarter(self_out, 1 - core, 0), so_od]
+    cq = [cq_c, cq_oc, quarter(cross_query, 1 - core, 1), cq_od]
+    co = [co_c, co_oc, quarter(cross_out, 1 - core, 0), co_od]
+    block = 2 * core + x_at
+    fi_s, fo_s = piece(feed_in, block, NB, 1), piece(feed_out, block, NB, 0)
+    ctx, so, cq, co, keys, values, fi_s, fo_s = tie((ctx, so, cq, co, keys, values, fi_s, fo_s))
+    fi_cx = over_y(fi_s)
+
+    middle, cross_rows, cross_q, cross_ctx, cross_log, after, feed_rows, feed_t = mid_forward(
+        clip_bounds, text_bounds, frames, ctx, so, cq, co, keys, values, vec
+    )
+
+    feed = (feed_rows, feed_t, cotangent)
+    places = lambda *t: jnp.stack(t).astype(jnp.int32)
+    feed, fi_cx, fo_s = tie((feed, fi_cx, fo_s))
+    fo_cx, fi_cy = over_y(fo_s), over_bit(fi_cx, 2)
+    o, e, in_od, out_od = feed_part(
+        places(2 - 2 * core, 3 - 2 * core), *feed, after, after, [feed_in], [feed_out], True, False
+    )
+    o, e, fo_cx, fi_cy = tie((o, e, fo_cx, fi_cy))
+    fo_cy = over_bit(fo_cx, 2)
+    fi_d = over_core([fi_cx, fi_cy])
+    o, e, in_oc, out_oc = feed_part(
+        places(2 * core, 2 * core + 1), *feed, o, e, [feed_in], [feed_out], False, False
+    )
+    o, e, fo_cy, fi_d = tie((o, e, fo_cy, fi_d))
+    fo_d = over_core([fo_cx, fo_cy])
+    o, e, fo_d, in_od, out_od = tie((o, e, fo_d, in_od, out_od))
+    in_og, out_og = over_core([in_od, out_od])
+    where = places(x_at, 1 - x_at)
+    o, e, in_td, out_td = feed_part(where, *feed, o, e, fi_d, fo_d, False, False)
+    o, e, in_og, in_td, out_td = tie((o, e, in_og, in_td, out_td))
+    own_low, own_high = parts_of((in_oc, in_og), 2)
+    o, e, own_low, own_high = tie((o, e, own_low, own_high))
+    in_tg, out_tg = over_core([in_td, out_td])
+    own_came = over_bit(own_high, 2)
+    output, e, in_tc, out_tc = feed_part(
+        where, *feed, o, e, [fi_cx, fi_cy], [fo_cx, fo_cy], False, True
+    )
+    e, in_tg, out_tg, own_came = tie((e, in_tg, out_tg, own_came))
+    other_low, other_high = parts_of((in_tc, in_tg), 2)
+
+    def travel_in():
+        sent = yield other_high
+        other = yield add(other_low, over_bit(sent, 2))
+        return (yield from travel((own_low, own_came, over_y(other)), steps[1:]))
+
+    j_in = Journey(travel_in())
+    middle_cut = out_tc.shape[1] // 2
+    j_out = []
+    for sl in (slice(0, middle_cut), slice(middle_cut, None)):
+        j_out.append(
+            Journey(
+                travel_y((out_oc[:, sl], out_og[:, sl]), add(out_tc[:, sl], out_tg[:, sl]))
+            )
+        )
+    e = onward(e, j_in, j_out[0])
+
+    g_c, grad_q, g_middle, g_s, grad_ctx, grad_k, grad_v, sums = mid_backward(
+        clip_bounds,
+        text_bounds,
+        e,
+        after,
+        cotangent,
+        middle,
+        cross_q,
+        cross_ctx,
+        cross_log,
+        co,
+        cq,
+        so,
+        keys,
+        values,
+        vec,
+    )
+    small = Journey(travel_small(sums[:4]))
+    (g_c, grad_q, g_s, grad_ctx, grad_k, grad_v) = onward(
+        (g_c, grad_q, g_s, grad_ctx, grad_k, grad_v), j_out[0], j_out[1], small
+    )
+
+    side = width
+
+    def both(big, small):
+        out = []
+        for at in (0, side):
+            t = outer_sum(big, small[:, at : at + side]).astype(bf16)
+            out.append((t[:, : side // 2], t[:, side // 2 :]))
+        return out
+
+    ctx_all = [jnp.concatenate(ctx[:2], 1), jnp.concatenate(ctx[2:], 1)]
+    wide = [both(cross_rows, grad_q), both(g_c, cross_ctx)]
+    so_parts = [outer_sum(g_s, t).astype(bf16) for t in ctx_all]
+    wide.append([(t[:, : side // 2], t[:, side // 2 :]) for t in so_parts])
+    c_keep, c_send = [
+        tuple(jnp.concatenate([w[n][m] for w in wide], 1) for m in range(2)) for n in range(2)
+    ]
+
+    def split_heads_back(t):
+        oc, tc, od, td = [t[:, side // 2 * n : side // 2 * (n + 1)] for n in range(4)]
+        return ordered(core == 0, oc, od, 1), ordered(core == 0, tc, td, 1)
+
+    dk_own, dk_other = split_heads_back(grad_k)
+    dv_own, dv_other = split_heads_back(grad_v)
+    came = over_y(jnp.concatenate([dk_other, dv_other], 1))
+    dk = ordered(half == 0, dk_own, came[:, :width], 0)
+    dv = ordered(half == 0, dv_own, came[:, width:], 0)
+    grad_text = against(dk, cross_key) + against(dv, cross_value)
+    mine = piece(grad_text, half, width, 1)
+    grad_text = (
+        mine + over_y(piece(grad_text, 1 - half, width, 1).astype(bf16)).astype(f32)
+    ).astype(bf16)
+    text_part = against(grad_text, text_weight).astype(bf16)
+    text_grad = text_part.astype(f32) + over_y(text_part).astype(f32)
+    tall = text_full.shape[1] - text_states.shape[1]
+    text_wide = jnp.concatenate(
+        [
+            text_states,
+            jnp.ones((text_states.shape[0], 1), bf16),
+            jnp.zeros((text_states.shape[0], tall - 1), bf16),
+        ],
+        1,
+    )
+    text_keep, text_send = [
+        jnp.concatenate(
+            [
+                outer_sum(text_full, quarter(dk, w, 1)),
+                outer_sum(text_full, quarter(dv, w, 1)),
+                outer_sum(text_wide, quarter(grad_text, w, 1)),
+            ],
+            1,
+        ).astype(bf16)
+        for w in (core, 1 - core)
+    ]
+
+    grad_ctx, c_send, text_send = tie((grad_ctx, c_send, text_send))
+    c_got, text_got = over_core((c_send, text_send))
+    grad_ctx = onward(grad_ctx, j_in, *j_out, small)
+
+    grads, parts = [None] * 4, [None] * 4
+
+    def back(n, main):
+        grads[n] = group_backward(clip_bounds, qkv[n], ctx[n], main, log[n], n)
+        parts[n] = outer_sum(self_rows, grads[n]).astype(bf16)
+        main, parts[n] = tie((main, parts[n]))
+        return main
+
+    main = back(3, grad_ctx)
+    main, c_got, text_got = tie((main, c_got, text_got))
+    c_cut = c_keep[0].shape[1] // 2
+    j_wide = [
+        Journey(
+            travel_y((c_keep[0][:, sl], c_got[0][:, sl]), add(c_keep[1][:, sl], c_got[1][:, sl]))
+        )
+        for sl in (slice(0, c_cut), slice(c_cut, None))
+    ]
+    j_text = Journey(travel((text_keep, text_got), steps))
+    main, parts[3] = tie((main, parts[3]))
+    td_got = over_core(parts[3])
+    main = onward(main, j_in, *j_out, j_wide[0], j_text, small)
+    main = back(1, main)
+    main, td_got = tie((main, td_got))
+    e_cut = parts[1].shape[0] // 2
+    other = add(parts[1], td_got)
+    main, other = tie((main, other))
+    came_1 = over_y(other[:e_cut])
+    main = onward(main, j_in, *j_out, j_text, small)
+    main = back(2, main)
+    main, parts[2], came_1 = tie((main, parts[2], came_1))
+    od_got = over_core(parts[2])
+    came_2 = over_y(other[e_cut:])
+    main = onward(main, j_in, *j_out, j_wide[0], j_text)
+    main = back(0, main)
+    main, came_1, came_2, od_got = tie((main, came_1, came_2, od_got))
+    j_self = Journey(travel((parts[0], od_got, jnp.concatenate([came_1, came_2])), steps))
+    grads = onward(grads, j_in, *j_out, j_wide[0], j_wide[1], j_text, j_self)
+    frames_grad, self_sums = final_grads(frames, g_middle, grads, qkv_w, vec)
+    last = Journey(travel_small(self_sums[:2]))
+    everything = [j_in, *j_out, *j_wide, j_text, j_self, small, last]
+    frames_grad = onward(frames_grad, *[j for j in everything if j.result is None])
+    for journey in everything:
+        while journey.result is None:
+            journey.go(journey.pending)
+    early, late = small.result, last.result
+    everything = None
+
+    def full(result, at, size, axis):
+        mine, theirs = [t[:, at : at + size] for t in result]
+        return ordered(core == 0, mine, theirs, axis).astype(f32)
+
+    n = side // 2
+    wide_sum = [jnp.concatenate([j.result[t] for j in j_wide], 1) for t in range(2)]
+    text_sum, self_sum = j_text.result, j_self.result
+    out_sum = [jnp.concatenate([j.result[t] for j in j_out], 1) for t in range(2)]
+    text_rows_grad = full(text_sum, 2 * n, n, 1)
+    return (
+        output,
+        frames_grad,
+        text_grad,
+        late[0],
+        late[1],
+        full(self_sum, 0, n, 1),
+        full(self_sum, n, n, 1),
+        full(self_sum, 2 * n, n, 1),
+        full(wide_sum, 2 * n, n, 1).T,
+        early[2],
+        early[3],
+        full(wide_sum, 0, n, 1),
+        full(text_sum, 0, n, 1),
+        full(text_sum, n, n, 1),
+        full(wide_sum, n, n, 1).T,
+        text_rows_grad[: text_states.shape[1]],
+        text_rows_grad[text_states.shape[1]],
+        early[0],
+        early[1],
+        full(j_in.result, 0, 2 * NB, 1),
+        ordered(core == 0, *out_sum, 0).astype(f32),
+    )
+
+
+def chosen(dp, mp, *args):
+    rows_here, frames_here = args[2].shape[0], args[0].shape[0]
+    if mp == 2 and dp == 16 and rows_here == mp and frames_here == ROW_LEN:
+        return row_body(dp, *args)
+    return body(*args)
+
+
 def solution(mesh):
     return jax.shard_map(
-        body,
+        functools.partial(chosen, mesh.shape["dp"], mesh.shape["mp"]),
         mesh=mesh,
         in_specs=(
             P(("dp", "mp"), None),

time: 2530 us -> 832 us (0.33)
  waiting for transfers between devices: 1400 us -> 187 us
  matrix products: 609 us -> 47.7 us
  Pallas kernels: 0 us -> 336 us
  other arithmetic: 243 us -> 109 us
  local copies, waits for them, and re-layouts: 171 us -> 52.7 us
  starting transfers between devices: 0.79 us -> 90.5 us
  blocking collectives: 83.9 us -> 0 us
    reduce_scatter x7 -> x0, waiting for transfers between devices: 803 us -> none  [the longest x3 429 us: branch_sum(): lax.psum_scatter(product(left_side, right_side), 'mp', scatter_dimension=...]
    all_gather x6 -> x0, waiting for transfers between devices: 344 us -> none  [the longest x3 224 us: spread_rows(): return lax.all_gather(tensor, 'mp', axis=0, tiled=True)]
    pallas_call x0 -> x15, Pallas kernels: none -> 336 us  [the longest x4 167 us: feed_part(): pl.pallas_call(functools.partial(feed_kernel, own=own, first=first, last=...]
    dot_general x24 -> x0, matrix products: 289 us -> none  [the longest x4 75.6 us: attend_back(): jnp.einsum('rqhd,rkhd->rhqk', grad_context, values, preferred_element_typ...]
    psum x2 -> x0, waiting for transfers between devices: 248 us -> none  [the longest x1 248 us: body(): lax.psum(text_weight_grad.astype(jnp.bfloat16), 'dp').astype(jnp.float32)]
    ppermute x0 -> x103, waiting for transfers between devices: none -> 187 us  [the longest x82 146 us: over_bit(): lax.ppermute(a, 'dp', [(i, i ^ step) for i in range(dp)])]
    dot_general x11 -> x7, matrix products: 136 us -> 16.8 us  [product(): return jnp.dot(left_side, right_side, preferred_element_type=jnp.float32)]
    dot_general x11 -> x3, matrix products: 107 us -> 2.09 us  [against(): lax.dot_general(left_side, right_side, (((1,), (1,)), ((), ())), preferre...]
  transfers between devices with their start and end apart: 15 -> 103, of which waited for: 13 -> 33; matrix products, arithmetic and copies ran while one was open for 23% -> 21% of each run, Pallas kernels for 0% -> 41%
where the time goes in v2:
time: 832 us; the launch traced here: 828 us
  Pallas kernels  336 us (40%)
  waiting for transfers between devices  187 us (22%)
  other arithmetic  109 us (13%)
  starting transfers between devices  90.5 us (11%)
  local copies, waits for them, and re-layouts  52.7 us (6%)
  matrix products  47.7 us (6%)
    pallas_call x4, Pallas kernels, feed_part(): pl.pallas_call(functools.partial(feed_kernel, own=own, first=first, last=...  167 us
    ppermute x82, waiting for transfers between devices, over_bit(): lax.ppermute(a, 'dp', [(i, i ^ step) for i in range(dp)])  146 us
    ppermute x82, starting transfers between devices, over_bit(): lax.ppermute(a, 'dp', [(i, i ^ step) for i in range(dp)])  67.7 us
    pallas_call x4, Pallas kernels, group_backward(): pl.pallas_call(self_bwd_kernel, grid=(pairs,), in_specs=[pl.BlockSpec(mem...  57.2 us
    convert_element_type x33, other arithmetic, add(): return reduce(jnp.add, [t.astype(f32) for t in ts]).astype(bf16)  46.1 us
    ppermute x21, waiting for transfers between devices, over_y(): return jax.tree.map(lambda a: lax.ppermute(a, 'mp', swap), t)  41.1 us
    pallas_call x1, Pallas kernels, mid_backward(): pl.pallas_call(functools.partial(mid_backward_kernel, len(cos)), grid=(n...  35.2 us
    pallas_call x4, Pallas kernels, group_forward(): pl.pallas_call(self_fwd_kernel, grid=(pairs,), in_specs=[pl.BlockSpec(mem...  31.4 us
  transfers between devices with their start and end apart: 103, of which 33 were waited for; matrix products, arithmetic and copies ran while one was open for 21% of the time, Pallas kernels for 41%

profile of v2, /device:TPU:0, one launch (start us, length us, event | category | flops | bytes accessed | tf_op | source)
XLA Modules:
  0.0 827.5 jit_solution(16891946855497922670)
XLA Ops:
  51.4 7.7 self_forward.4
  62.6 7.9 self_forward.5
  82.2 7.7 self_forward.6
  102.5 8.1 self_forward.7
  112.7 27.0 %mid_forward.1 = (f32[1536,1024]{1,0:T(8,128)}, bf16[1536,1024]{1,0:T(8,128)(2,1)}, bf16[1536,1024]{1,0:T(8,128)(2,1)}, bf16[1536,1024]{1,0:T(8,128)(2,1)}, f32[...) custom-call(s32[4]{0:T(128)} %bitcast.61, s32[4]{0:T(128)} %bitcast.79, ...), custom_call_target="tpu_custom_call" | custom-call | flops 19327352832 | bytes 31457280 | tf_op jit(solution)/shard_map/mid_forward/pallas_call | solution.py:633
  142.3 44.0 %feed_first.1 = (f32[1536,1024]{1,0:T(8,128)}, f32[1536,1024]{1,0:T(8,128)}, bf16[1024,1024]{1,0:T(8,128)(2,1)}, bf16[1024,1024]{1,0:T(8,128)(2,1)}) custom-call(s32[2]{0:T(128)} %pad_add_fusion.2.idx_ref, bf16[1536,1024]{1,0:T(8,128)(2,1)} %get-tuple-element.288.fr_hbm, bf16[1024,1536]{1,0:T(8,128)(2,1)} %get-tuple-element.289.frt_hbm, ...), custom_call_target="tpu_custom_call" | custom-call | flops 19327352832 | bytes 50331648 | tf_op jit(solution)/shard_map/feed_first/pallas_call | solution.py:899
  187.4 45.7 %feed_more.2 = (f32[1536,1024]{1,0:T(8,128)}, f32[1536,1024]{1,0:T(8,128)}, bf16[1024,1024]{1,0:T(8,128)(2,1)}, bf16[1024,1024]{1,0:T(8,128)(2,1)}) custom-call(s32[2]{0:T(128)} %get-tuple-element.633.idx_ref, bf16[1536,1024]{1,0:T(8,128)(2,1)} %get-tuple-element.288.fr_hbm, bf16[1024,1536]{1,0:T(8,128)(2,1)} %get-tuple-element.289.frt_hbm, ...), custom_call_target="tpu_custom_call" | custom-call | flops 19327352832 | bytes 50331648 | tf_op jit(solution)/shard_map/feed_more/pallas_call | solution.py:899
  238.2 45.8 %feed_more.3 = (f32[1536,1024]{1,0:T(8,128)}, f32[1536,1024]{1,0:T(8,128)}, bf16[1024,1024]{1,0:T(8,128)(2,1)}, bf16[1024,1024]{1,0:T(8,128)(2,1)}) custom-call(s32[2]{0:T(128)} %get-tuple-element.632.idx_ref, bf16[1536,1024]{1,0:T(8,128)(2,1)} %get-tuple-element.288.fr_hbm, bf16[1024,1536]{1,0:T(8,128)(2,1)} %get-tuple-element.289.frt_hbm, ...), custom_call_target="tpu_custom_call" | custom-call | flops 19327352832 | bytes 50331648 | tf_op jit(solution)/shard_map/feed_more/pallas_call | solution.py:899
  290.5 31.6 %feed_last.1 = (bf16[1536,1024]{1,0:T(8,128)(2,1)}, f32[1536,1024]{1,0:T(8,128)}, bf16[1024,1024]{1,0:T(8,128)(2,1)}, bf16[1024,1024]{1,0:T(8,128)(2,1)}) custom-call(s32[2]{0:T(128)} %get-tuple-element.632.idx_ref, bf16[1536,1024]{1,0:T(8,128)(2,1)} %get-tuple-element.288.fr_hbm, bf16[1024,1536]{1,0:T(8,128)(2,1)} %get-tuple-element.289.frt_hbm, ...), custom_call_target="tpu_custom_call" | custom-call | flops 19327352832 | bytes 50331648 | tf_op jit(solution)/shard_map/feed_last/pallas_call | solution.py:899
  332.3 35.2 %mid_backward.1 = (bf16[1536,1024]{1,0:T(8,128)(2,1)}, bf16[1536,1024]{1,0:T(8,128)(2,1)}, f32[1536,1024]{1,0:T(8,128)}, bf16[1536,1024]{1,0:T(8,128)(2,1)}, bf1...) custom-call(s32[4]{0:T(128)} %bitcast.62, s32[4]{0:T(128)} %bitcast.80, ...), custom_call_target="tpu_custom_call" | custom-call | flops 32212254720 | bytes 36175872 | tf_op jit(solution)/shard_map/mid_backward/pallas_call | solution.py:752
  399.9 12.7 %collective-permute-done.30 = bf16[128,1024]{1,0:T(8,128)(2,1)S(1)} collective-permute-done((bf16[128,1024]{1,0:T(8,128)(2,1)S(1)}, bf16[128,1024]{1,0:T(8,128)(2,1)S(1)}, u32[]{:S(2)}, u32[]{:S(2)}) %collective-permute-start.30) | collective-permute-done | bytes 262176 | tf_op jit(solution)/shard_map/ppermute | solution.py:1027
  431.6 14.4 %self_backward.4.refs_3_ = bf16[1536,768]{1,0:T(8,128)(2,1)S(1)} custom-call(s32[4]{0:T(128)S(1)} %bitcast.63, bf16[1536,768]{1,0:T(8,128)(2,1)S(1)} %copy-done.8, bf16[1536,768]{1,0:T(8,128)(2,1)S(1)} %copy-done.8, bf16[1536,768]{1,0:T(8,128)(2,1)S(1)} %copy-done.8, bf16[1536,256]{1,0:T(8,128)(2,1)S(1)} %copy-done.20, ...), custom_call_target="tpu_custom_call" | custom-call | flops 12079595520 | bytes 6291456 | tf_op jit(solution)/shard_map/self_backward/pallas_call | solution.py:494
  480.4 14.5 %self_backward.5.refs_1_ = bf16[1536,768]{1,0:T(8,128)(2,1)S(1)} custom-call(s32[4]{0:T(128)S(1)} %bitcast.64, bf16[1536,768]{1,0:T(8,128)(2,1)S(1)} %copy-done.6, bf16[1536,768]{1,0:T(8,128)(2,1)S(1)} %copy-done.6, bf16[1536,768]{1,0:T(8,128)(2,1)S(1)} %copy-done.6, bf16[1536,256]{1,0:T(8,128)(2,1)S(1)} %copy-done.18, ...), custom_call_target="tpu_custom_call" | custom-call | flops 12079595520 | bytes 6291456 | tf_op jit(solution)/shard_map/self_backward/pallas_call | solution.py:494
  528.2 14.2 %self_backward.6.refs_2_ = bf16[1536,768]{1,0:T(8,128)(2,1)S(1)} custom-call(s32[4]{0:T(128)S(1)} %bitcast.65, bf16[1536,768]{1,0:T(8,128)(2,1)S(1)} %copy-done.4, bf16[1536,768]{1,0:T(8,128)(2,1)S(1)} %copy-done.4, bf16[1536,768]{1,0:T(8,128)(2,1)S(1)} %copy-done.4, bf16[1536,256]{1,0:T(8,128)(2,1)S(1)} %copy-done.16, ...), custom_call_target="tpu_custom_call" | custom-call | flops 12079595520 | bytes 6291456 | tf_op jit(solution)/shard_map/self_backward/pallas_call | solution.py:494
  552.2 7.6 collective-permute-done.50
  560.9 7.6 collective-permute-done.49
  571.2 14.2 %self_backward.7.refs_0_ = bf16[1536,768]{1,0:T(8,128)(2,1)S(1)} custom-call(s32[4]{0:T(128)S(1)} %bitcast.66, bf16[1536,768]{1,0:T(8,128)(2,1)S(1)} %convolution_convert_fusion.3.q_ref.k_ref.v_ref, bf16[1536,768]{1,0:T(8,128)(2,1)S(1)} %convolution_convert_fusion.3.q_ref.k_ref.v_ref, bf16[1536,768]{1,0:T(8,128)(2,1)S(1)} %convolution_convert_fusion.3.q_ref.k_ref.v_ref, ...), custom_call_target="tpu_custom_call" | custom-call | flops 12079595520 | bytes 6291456 | tf_op jit(solution)/shard_map/self_backward/pallas_call | solution.py:494
  589.6 10.8 %collective-permute-done.59 = bf16[128,768]{1,0:T(8,128)(2,1)S(1)} collective-permute-done((bf16[128,768]{1,0:T(8,128)(2,1)S(1)}, bf16[128,768]{1,0:T(8,128)(2,1)S(1)}, u32[]{:S(2)}, u32[]{:S(2)}) %collective-permute-start.59) | collective-permute-done | bytes 196640 | tf_op jit(solution)/shard_map/ppermute | solution.py:1030
  602.4 11.9 %collective-permute-done.55 = bf16[128,1024]{1,0:T(8,128)(2,1)S(1)} collective-permute-done((bf16[128,1024]{1,0:T(8,128)(2,1)S(1)}, bf16[128,1024]{1,0:T(8,128)(2,1)S(1)}, u32[]{:S(2)}, u32[]{:S(2)}) %collective-permute-start.55) | collective-permute-done | bytes 262176 | tf_op jit(solution)/shard_map/ppermute | solution.py:1030
  622.6 18.7 %frames_gradient.1 = (f32[1536,1024]{1,0:T(8,128)}, f32[8,1024]{1,0:T(8,128)}) custom-call(bf16[1536,1024]{1,0:T(8,128)(2,1)} %x_ref.1, f32[1536,1024]{1,0:T(8,128)} %get-tuple-element.339.gmid_ref, bf16[1536,768]{1,0:T(8,128)(2,1)} %copy-done.12, bf16[1536,768]{1,0:T(8,128)(2,1)} %copy-done.10, bf16[1536,768]{1,0:T(8,128)(2,1)} %copy-done.11, ...), custom_call_target="tpu_custom_call" | custom-call | flops 9663676416 | bytes 18874368 | tf_op jit(solution)/shard_map/frames_gradient/pallas_call | solution.py:961
  699.0 7.8 collective-permute-done.76
  708.2 8.3 collective-permute-done.82
  736.2 10.7 %collective-permute-done.78 = bf16[128,768]{1,0:T(8,128)(2,1)S(1)} collective-permute-done((bf16[128,768]{1,0:T(8,128)(2,1)S(1)}, bf16[128,768]{1,0:T(8,128)(2,1)S(1)}, u32[]{:S(2)}, u32[]{:S(2)}) %collective-permute-start.78) | collective-permute-done | bytes 196640 | tf_op jit(solution)/shard_map/ppermute | solution.py:1030
  782.5 8.4 %collective-permute-done.80 = bf16[512,768]{1,0:T(8,128)(2,1)S(1)} collective-permute-done((bf16[512,768]{1,0:T(8,128)(2,1)S(1)}, bf16[512,768]{1,0:T(8,128)(2,1)S(1)}, u32[]{:S(2)}, u32[]{:S(2)}) %collective-permute-start.80) | collective-permute-done | bytes 786464 | tf_op jit(solution)/shard_map/ppermute | solution.py:1030
  (618 shorter events, 402.0 us)
Async XLA Ops:
  139.7 46.6 %collective-permute-start.18 = (bf16[1024,512]{1,0:T(8,128)(2,1)}, bf16[1024,512]{1,0:T(8,128)(2,1)}, u32[]{:S(2)}, u32[]{:S(2)}) collective-permute-start(bf16[1024,512]{1,0:T(8,128)(2,1)} %collective-permute-done.16.refs_0_), channel_id=1, source_target_pairs={{0,4},{2,6},{4,0},{6,2},{8,12},{10,14},{12,8},{14,10},{16,20},{18,... | collective-permute-start | bytes 3145736 | tf_op jit(solution)/shard_map/ppermute | solution.py:1030
  141.2 91.8 %collective-permute-start.20 = (bf16[1024,512]{1,0:T(8,128)(2,1)}, bf16[1024,512]{1,0:T(8,128)(2,1)}, u32[]{:S(2)}, u32[]{:S(2)}) collective-permute-start(bf16[1024,512]{1,0:T(8,128)(2,1)} %collective-permute-done.16.refs_0_), channel_id=1, source_target_pairs={{0,2},{2,0},{4,6},{6,4},{8,10},{10,8},{12,14},{14,12},{16,18},{18,... | collective-permute-start | bytes 3145736 | tf_op jit(solution)/shard_map/ppermute | solution.py:1030
  141.4 44.9 %collective-permute-start.17 = (bf16[512,1024]{1,0:T(8,128)(2,1)}, bf16[512,1024]{1,0:T(8,128)(2,1)}, u32[]{:S(2)}, u32[]{:S(2)}) collective-permute-start(bf16[512,1024]{1,0:T(8,128)(2,1)} %constant_dynamic-slice_fusion.1), channel_id=1, source_target_pairs={{0,1},{1,0},{2,3},{3,2},{4,5},{5,4},{6,7},{7,6},{8,9},{9,8},{10,11... | collective-permute-start | bytes 3145736 | tf_op jit(solution)/shard_map/ppermute | solution.py:1027
  186.3 46.8 %collective-permute-start.19 = (bf16[512,1024]{1,0:T(8,128)(2,1)}, bf16[512,1024]{1,0:T(8,128)(2,1)}, u32[]{:S(2)}, u32[]{:S(2)}) collective-permute-start(bf16[512,1024]{1,0:T(8,128)(2,1)} %collective-permute-done.17.refs_2_), channel_id=1, source_target_pairs={{0,4},{2,6},{4,0},{6,2},{8,12},{10,14},{12,8},{14,10},{16,20},{18,... | collective-permute-start | bytes 3145736 | tf_op jit(solution)/shard_map/ppermute | solution.py:1030
  186.9 49.2 %collective-permute-start.22 = (bf16[512,1024]{1,0:T(8,128)(2,1)}, bf16[512,1024]{1,0:T(8,128)(2,1)}, u32[]{:S(2)}, u32[]{:S(2)}) collective-permute-start(bf16[512,1024]{1,0:T(8,128)(2,1)} %collective-permute-done.17.refs_2_), channel_id=1, source_target_pairs={{0,2},{2,0},{4,6},{6,4},{8,10},{10,8},{12,14},{14,12},{16,18},{18,... | collective-permute-start | bytes 3145736 | tf_op jit(solution)/shard_map/ppermute | solution.py:1030
  186.9 46.2 %collective-permute-start.21 = (bf16[1024,512]{1,0:T(8,128)(2,1)}, bf16[1024,512]{1,0:T(8,128)(2,1)}, u32[]{:S(2)}, u32[]{:S(2)}) collective-permute-start(bf16[1024,512]{1,0:T(8,128)(2,1)} %collective-permute-done.18.refs_1_), channel_id=1, source_target_pairs={{0,2},{2,0},{4,6},{6,4},{8,10},{10,8},{12,14},{14,12},{16,18},{18,... | collective-permute-start | bytes 3145736 | tf_op jit(solution)/shard_map/ppermute | solution.py:1030
  236.2 47.8 %collective-permute-start.24 = (bf16[1024,1024]{1,0:T(8,128)(2,1)}, bf16[1024,1024]{1,0:T(8,128)(2,1)}, u32[]{:S(2)}, u32[]{:S(2)}) collective-permute-start(bf16[1024,1024]{1,0:T(8,128)(2,1)} %get-tuple-element.315), channel_id=1, source_target_pairs={{0,2},{2,0},{4,6},{6,4},{8,10},{10,8},{12,14},{14,12},{16,18},{18,... | collective-permute-start | bytes 6291464 | tf_op jit(solution)/shard_map/ppermute | solution.py:1030
  238.0 84.1 %collective-permute-start.28 = (bf16[1024,1024]{1,0:T(8,128)(2,1)}, bf16[1024,1024]{1,0:T(8,128)(2,1)}, u32[]{:S(2)}, u32[]{:S(2)}) collective-permute-start(bf16[1024,1024]{1,0:T(8,128)(2,1)} %get-tuple-element.347), channel_id=1, source_target_pairs={{0,2},{2,0},{4,6},{6,4},{8,10},{10,8},{12,14},{14,12},{16,18},{18,... | collective-permute-start | bytes 6291464 | tf_op jit(solution)/shard_map/ppermute | solution.py:1030
  331.2 37.6 %collective-permute-start.29 = (bf16[1024,512]{1,0:T(8,128)(2,1)}, bf16[1024,512]{1,0:T(8,128)(2,1)}, u32[]{:S(2)}, u32[]{:S(2)}) collective-permute-start(bf16[1024,512]{1,0:T(8,128)(2,1)} %get-tuple-element.348), channel_id=1, source_target_pairs={{0,1},{1,0},{2,3},{3,2},{4,5},{5,4},{6,7},{7,6},{8,9},{9,8},{10,11... | collective-permute-start | bytes 3145736 | tf_op jit(solution)/shard_map/ppermute | solution.py:1027
  381.3 46.4 %collective-permute-start.34 = (bf16[1024,512]{1,0:T(8,128)(2,1)S(1)}, bf16[1024,512]{1,0:T(8,128)(2,1)S(1)}, u32[]{:S(2)}, u32[]{:S(2)}) collective-permute-start(bf16[1024,512]{1,0:T(8,128)(2,1)S(1)} %copy-done.62), channel_id=1, source_target_pairs={{0,1},{1,0},{2,3},{3,2},{4,5},{5,4},{6,7},{7,6},{8,9},{9,8},{10,11... | collective-permute-start | bytes 3145736 | tf_op jit(solution)/shard_map/ppermute | solution.py:1027
  382.3 42.3 %collective-permute-start.33 = (bf16[512,512]{1,0:T(8,128)(2,1)S(1)}, bf16[512,512]{1,0:T(8,128)(2,1)S(1)}, u32[]{:S(2)}, u32[]{:S(2)}) collective-permute-start(bf16[512,512]{1,0:T(8,128)(2,1)S(1)} %get-tuple-element.359), channel_id=1, source_target_pairs={{0,4},{2,6},{4,0},{6,2},{8,12},{10,14},{12,8},{14,10},{16,20},{18,... | collective-permute-start | bytes 1572872 | tf_op jit(solution)/shard_map/ppermute | solution.py:1030
  424.0 37.0 %collective-permute-start.37 = (bf16[1024,768]{1,0:T(8,128)(2,1)}, bf16[1024,768]{1,0:T(8,128)(2,1)}, u32[]{:S(2)}, u32[]{:S(2)}) collective-permute-start(bf16[1024,768]{1,0:T(8,128)(2,1)} %pad_maximum_fusion.7), channel_id=1, source_target_pairs={{0,2},{2,0},{4,6},{6,4},{8,10},{10,8},{12,14},{14,12},{16,18},{18,... | collective-permute-start | bytes 4718600 | tf_op jit(solution)/shard_map/ppermute | solution.py:1030
  475.9 37.4 %collective-permute-start.47 = (bf16[512,768]{1,0:T(8,128)(2,1)}, bf16[512,768]{1,0:T(8,128)(2,1)}, u32[]{:S(2)}, u32[]{:S(2)}) collective-permute-start(bf16[512,768]{1,0:T(8,128)(2,1)} %get-tuple-element.390), channel_id=1, source_target_pairs={{0,4},{2,6},{4,0},{6,2},{8,12},{10,14},{12,8},{14,10},{16,20},{18,... | collective-permute-start | bytes 2359304 | tf_op jit(solution)/shard_map/ppermute | solution.py:1030
  480.4 40.7 %collective-permute-start.43 = (bf16[1024,768]{1,0:T(8,128)(2,1)}, bf16[1024,768]{1,0:T(8,128)(2,1)}, u32[]{:S(2)}, u32[]{:S(2)}) collective-permute-start(bf16[1024,768]{1,0:T(8,128)(2,1)} %convolution_convert_fusion.7), channel_id=1, source_target_pairs={{0,2},{2,0},{4,6},{6,4},{8,10},{10,8},{12,14},{14,12},{16,18},{18,... | collective-permute-start | bytes 4718600 | tf_op jit(solution)/shard_map/ppermute | solution.py:1030
  503.9 167.6 %collective-permute-start.70 = (bf16[256,768]{1,0:T(8,128)(2,1)}, bf16[256,768]{1,0:T(8,128)(2,1)}, u32[]{:S(2)}, u32[]{:S(2)}) collective-permute-start(bf16[256,768]{1,0:T(8,128)(2,1)} %convolution_convert_fusion.14), channel_id=1, source_target_pairs={{0,1},{1,0},{2,3},{3,2},{4,5},{5,4},{6,7},{7,6},{8,9},{9,8},{10,11... | collective-permute-start | bytes 1179656 | tf_op jit(solution)/shard_map/ppermute | solution.py:1027
  550.3 64.9 %collective-permute-start.60 = (bf16[512,768]{1,0:T(8,128)(2,1)}, bf16[512,768]{1,0:T(8,128)(2,1)}, u32[]{:S(2)}, u32[]{:S(2)}) collective-permute-start(bf16[512,768]{1,0:T(8,128)(2,1)} %get-tuple-element.518), channel_id=1, source_target_pairs={{0,1},{1,0},{2,3},{3,2},{4,5},{5,4},{6,7},{7,6},{8,9},{9,8},{10,11... | collective-permute-start | bytes 2359304 | tf_op jit(solution)/shard_map/ppermute | solution.py:1027
  568.6 46.6 %collective-permute-start.61 = (bf16[1024,768]{1,0:T(8,128)(2,1)}, bf16[1024,768]{1,0:T(8,128)(2,1)S(1)}, u32[]{:S(2)}, u32[]{:S(2)}) collective-permute-start(bf16[1024,768]{1,0:T(8,128)(2,1)} %convolution_convert_fusion.5), channel_id=1, source_target_pairs={{0,2},{2,0},{4,6},{6,4},{8,10},{10,8},{12,14},{14,12},{16,18},{18,... | collective-permute-start | bytes 4718600 | tf_op jit(solution)/shard_map/ppermute | solution.py:1030
  618.0 41.9 %collective-permute-start.68 = (bf16[512,768]{1,0:T(8,128)(2,1)}, bf16[512,768]{1,0:T(8,128)(2,1)}, u32[]{:S(2)}, u32[]{:S(2)}) collective-permute-start(bf16[512,768]{1,0:T(8,128)(2,1)} %get-tuple-element.428), channel_id=1, source_target_pairs={{0,4},{2,6},{4,0},{6,2},{8,12},{10,14},{12,8},{14,10},{16,20},{18,... | collective-permute-start | bytes 2359304 | tf_op jit(solution)/shard_map/ppermute | solution.py:1030
  618.5 42.7 %collective-permute-start.66 = (bf16[1024,384]{1,0:T(8,128)(2,1)S(1)}, bf16[1024,384]{1,0:T(8,128)(2,1)S(1)}, u32[]{:S(2)}, u32[]{:S(2)}) collective-permute-start(bf16[1024,384]{1,0:T(8,128)(2,1)S(1)} %copy-done.63), channel_id=1, source_target_pairs={{0,1},{1,0},{2,3},{3,2},{4,5},{5,4},{6,7},{7,6},{8,9},{9,8},{10,11... | collective-permute-start | bytes 2359304 | tf_op jit(solution)/shard_map/ppermute | solution.py:1027
  673.5 44.9 %collective-permute-start.100 = (bf16[512,512]{1,0:T(8,128)(2,1)S(1)}, bf16[512,512]{1,0:T(8,128)(2,1)S(1)}, u32[]{:S(2)}, u32[]{:S(2)}) collective-permute-start(bf16[512,512]{1,0:T(8,128)(2,1)S(1)} %pad_maximum_fusion.28), channel_id=1, source_target_pairs={{0,4},{2,6},{4,0},{6,2},{8,12},{10,14},{12,8},{14,10},{16,20},{18,... | collective-permute-start | bytes 1572872 | tf_op jit(solution)/shard_map/ppermute | solution.py:1030
  674.4 86.1 %collective-permute-start.101 = (bf16[1024,512]{1,0:T(8,128)(2,1)S(1)}, bf16[1024,512]{1,0:T(8,128)(2,1)S(1)}, u32[]{:S(2)}, u32[]{:S(2)}) collective-permute-start(bf16[1024,512]{1,0:T(8,128)(2,1)S(1)} %pad_maximum_fusion.11), channel_id=1, source_target_pairs={{0,2},{2,0},{4,6},{6,4},{8,10},{10,8},{12,14},{14,12},{16,18},{18,... | collective-permute-start | bytes 3145736 | tf_op jit(solution)/shard_map/ppermute | solution.py:1030
  674.4 85.9 %collective-permute-start.98 = (bf16[512,1024]{1,0:T(8,128)(2,1)S(1)}, bf16[512,1024]{1,0:T(8,128)(2,1)S(1)}, u32[]{:S(2)}, u32[]{:S(2)}) collective-permute-start(bf16[512,1024]{1,0:T(8,128)(2,1)S(1)} %pad_maximum_fusion.10), channel_id=1, source_target_pairs={{0,4},{2,6},{4,0},{6,2},{8,12},{10,14},{12,8},{14,10},{16,20},{18,... | collective-permute-start | bytes 3145736 | tf_op jit(solution)/shard_map/ppermute | solution.py:1030
  716.5 54.3 %collective-permute-start.96 = (bf16[512,768]{1,0:T(8,128)(2,1)S(1)}, bf16[512,768]{1,0:T(8,128)(2,1)S(1)}, u32[]{:S(2)}, u32[]{:S(2)}) collective-permute-start(bf16[512,768]{1,0:T(8,128)(2,1)S(1)} %pad_maximum_fusion.18), channel_id=1, source_target_pairs={{0,4},{2,6},{4,0},{6,2},{8,12},{10,14},{12,8},{14,10},{16,20},{18,... | collective-permute-start | bytes 2359304 | tf_op jit(solution)/shard_map/ppermute | solution.py:1030
  770.6 42.8 %collective-permute-start.99 = (bf16[1024,1024]{1,0:T(8,128)(2,1)}, bf16[1024,1024]{1,0:T(8,128)(2,1)}, u32[]{:S(2)}, u32[]{:S(2)}) collective-permute-start(bf16[1024,1024]{1,0:T(8,128)(2,1)} %pad_maximum_fusion.2), channel_id=1, source_target_pairs={{0,2},{2,0},{4,6},{6,4},{8,10},{10,8},{12,14},{14,12},{16,18},{18,... | collective-permute-start | bytes 6291464 | tf_op jit(solution)/shard_map/ppermute | solution.py:1030
  (184 other events, 2068.7 us)

commit v3 on v2

--- a/solution.py
+++ b/solution.py
@@ -767,21 +767,16 @@
     )(cb, tb, e, after, g, middle, q, cctx, lse, *weights)
 
 
-def feed_kernel(
-    idx_ref, fr_hbm, frt_hbm, cot_hbm, o_in, e_in, *refs, own, first, last
-):
+def feed_kernel(idx_ref, fr_ref, frt_ref, cot_ref, o_in, e_in, *refs, own, first, last):
     if own:
         fi_src, fo_src = refs[:2]
         refs = refs[2:]
     else:
         fi_srcs, fo_srcs = refs[:2], refs[2:4]
         refs = refs[4:]
-    (o_out, e_out, gi_ref, go_ref, fr_ref, frt_ref, cot_ref, out_ref, acc_o, acc_e,
-     fi_buf, fo_buf, act_s, gh_s, wsem, isem, asem) = refs
+    o_out, e_out, gi_ref, go_ref, acc_o, acc_e, fi_buf, fo_buf, act_s, gh_s, wsem, asem = refs
     p = pl.program_id(0)
     slot = p % 2
-    rows = 256
-    blocks = fr_hbm.shape[0] // rows
 
     def weights(step, into, act):
         if own:
@@ -795,38 +790,18 @@
                     act(pltpu.make_async_copy(fi_srcs[s], fi_buf.at[into], wsem.at[into, 0]))
                     act(pltpu.make_async_copy(fo_srcs[s], fo_buf.at[into], wsem.at[into, 1]))
 
-    def cut(r):
-        return slice(rows * r, rows * r + rows)
-
-    def row_in(r):
-        return [
-            pltpu.make_async_copy(fr_hbm.at[cut(r), :], fr_ref.at[cut(r), :], isem.at[0, r]),
-            pltpu.make_async_copy(cot_hbm.at[cut(r), :], cot_ref.at[cut(r), :], isem.at[1, r]),
-        ]
-
-    def sums_in(r):
-        loads = [pltpu.make_async_copy(o_in.at[cut(r), :], acc_o.at[cut(r), :], asem.at[0, r])]
-        if not first:
-            loads.append(pltpu.make_async_copy(e_in.at[cut(r), :], acc_e.at[cut(r), :], asem.at[1, r]))
-        return loads
-
-    def sums_out(r):
-        stores = [pltpu.make_async_copy(acc_e.at[cut(r), :], e_out.at[cut(r), :], asem.at[1, r])]
-        source = out_ref if last else acc_o
-        stores.append(pltpu.make_async_copy(source.at[cut(r), :], o_out.at[cut(r), :], asem.at[0, r]))
-        return stores
-
-    turned = pltpu.make_async_copy(frt_hbm, frt_ref, isem.at[2, 0])
+    o_load = pltpu.make_async_copy(o_in, acc_o, asem.at[0])
+    if not first:
+        e_load = pltpu.make_async_copy(e_in, acc_e, asem.at[1])
 
     @pl.when(p == 0)
     def _():
         weights(p, slot, lambda c: c.start())
-        for c in row_in(0) + row_in(1) + sums_in(0):
-            c.start()
-        if first:
+        o_load.start()
+        if not first:
+            e_load.start()
+        else:
             acc_e[...] = jnp.zeros_like(acc_e)
-        for c in row_in(0):
-            c.wait()
 
     weights(p, slot, lambda c: c.wait())
 
@@ -834,59 +809,48 @@
     def _():
         weights(p + 1, 1 - slot, lambda c: c.start())
 
-    fi, fo = fi_buf.at[slot], fo_buf.at[slot]
-
-    def products(r):
-        return dot(fr_ref[cut(r), :], fi[...], 1, 0), dot(cot_ref[cut(r), :], fo[...], 1, 1)
-
-    def whole_pass(arriving):
-        queue = [products(0)]
-        for r in range(blocks):
-            if arriving:
-                for c in (row_in(r + 1) if r + 1 < blocks else []) + sums_in(r):
-                    c.wait()
-                for c in (row_in(r + 2) if r + 2 < blocks else []) + (
-                    sums_in(r + 1) if r + 1 < blocks else []
-                ):
-                    c.start()
-                if r == 2:
-                    turned.start()
-            elif r > 0:
-                for c in sums_out(r - 1):
-                    c.start()
-            if r + 1 < blocks:
-                queue.append(products(r + 1))
-            h, g = queue.pop(0)
-            active, slope = gelu_pair(h)
-            active = active.astype(jnp.bfloat16)
-            gh = (g * slope).astype(jnp.bfloat16)
-            act_s[cut(r), :] = active
-            gh_s[cut(r), :] = gh
-            o_sum = acc_o[cut(r), :] + dot(active, fo[...], 1, 0)
-            if last and not arriving:
-                out_ref[cut(r), :] = o_sum.astype(jnp.bfloat16)
-            else:
-                acc_o[cut(r), :] = o_sum
-            acc_e[cut(r), :] += dot(gh, fi[...], 1, 1)
-        if not arriving:
-            for c in sums_out(blocks - 1):
-                c.start()
-        if arriving:
-            turned.wait()
-        gi_ref[...] = dot(frt_ref[...], gh_s[...], 1, 0).astype(jnp.bfloat16)
-        go_ref[...] = dot(act_s[...], cot_ref[...], 0, 0).astype(jnp.bfloat16)
-        if not arriving:
-            for r in range(blocks):
-                for c in sums_out(r):
-                    c.wait()
-
     @pl.when(p == 0)
     def _():
-        whole_pass(True)
+        o_load.wait()
+        if not first:
+            e_load.wait()
+
+    fi, fo = fi_buf.at[slot], fo_buf.at[slot]
+    rows = 256
+    blocks = fr_ref.shape[0] // rows
+
+    def products(r):
+        sl = slice(rows * r, rows * r + rows)
+        return dot(fr_ref[sl, :], fi[...], 1, 0), dot(cot_ref[sl, :], fo[...], 1, 1)
+
+    ahead = 1
+    queue = [products(r) for r in range(ahead)]
+    for r in range(blocks):
+        if r + ahead < blocks:
+            queue.append(products(r + ahead))
+        h, g = queue.pop(0)
+        sl = slice(rows * r, rows * r + rows)
+        active, slope = gelu_pair(h)
+        active = active.astype(jnp.bfloat16)
+        gh = (g * slope).astype(jnp.bfloat16)
+        act_s[sl, :] = active
+        gh_s[sl, :] = gh
+        acc_o[sl, :] += dot(active, fo[...], 1, 0)
+        acc_e[sl, :] += dot(gh, fi[...], 1, 1)
+    gi_ref[...] = dot(frt_ref[...], gh_s[...], 1, 0).astype(jnp.bfloat16)
+    go_ref[...] = dot(act_s[...], cot_ref[...], 0, 0).astype(jnp.bfloat16)
 
     @pl.when(p == 1)
     def _():
-        whole_pass(False)
+        e_store = pltpu.make_async_copy(acc_e, e_out, asem.at[1])
+        e_store.start()
+        if last:
+            o_out[...] = acc_o[...].astype(jnp.bfloat16)
+        else:
+            o_store = pltpu.make_async_copy(acc_o, o_out, asem.at[0])
+            o_store.start()
+            o_store.wait()
+        e_store.wait()
 
 
 def feed_part(idx, rows, rows_t, cot, o_in, e_in, fis, fos, first, last):
@@ -894,25 +858,21 @@
     own = len(fis) == 1
     bf, f = jnp.bfloat16, jnp.float32
     hbm = pl.BlockSpec(memory_space=pl.ANY)
+    once = lambda shape: pl.BlockSpec(shape, lambda p, idx: (0, 0), pipeline_mode=pl.Buffered(1))
     grad = lambda shape: jax.ShapeDtypeStruct(shape, bf)
-    blocks = n // 256
     return pl.pallas_call(
         functools.partial(feed_kernel, own=own, first=first, last=last),
         grid_spec=pltpu.PrefetchScalarGridSpec(
             num_scalar_prefetch=1,
             grid=(2,),
-            in_specs=[hbm] * (5 + 2 * len(fis)),
+            in_specs=[once((n, d)), once((d, n)), once((n, d))] + [hbm] * (2 + 2 * len(fis)),
             out_specs=[
-                hbm,
+                once((n, d)) if last else hbm,
                 hbm,
                 pl.BlockSpec((d, NB), lambda p, idx: (0, idx[p] % 2)),
                 pl.BlockSpec((NB, d), lambda p, idx: (idx[p] % 2, 0)),
             ],
             scratch_shapes=[
-                pltpu.VMEM((n, d), bf),
-                pltpu.VMEM((d, n), bf),
-                pltpu.VMEM((n, d), bf),
-                pltpu.VMEM((n, d) if last else (16, 128), bf),
                 pltpu.VMEM((n, d), f),
                 pltpu.VMEM((n, d), f),
                 pltpu.VMEM((2, d, NB), bf),
@@ -920,8 +880,7 @@
                 pltpu.VMEM((n, NB), bf),
                 pltpu.VMEM((n, NB), bf),
                 pltpu.SemaphoreType.DMA((2, 2)),
-                pltpu.SemaphoreType.DMA((3, blocks)),
-                pltpu.SemaphoreType.DMA((2, blocks)),
+                pltpu.SemaphoreType.DMA((2,)),
             ],
         ),
         out_shape=[
@@ -970,6 +929,86 @@
     )(x, gmid, *gs, *ws, vec)
 
 
+def pair_at(b):
+    return (b % 2) * 4 + (b // 2) % 2 * 2 + b // 4
+
+
+def spread_feed_kernel(t_ref, in_ref, out_ref):
+    n = in_ref.shape[1] // 2
+    for c in range(2):
+        in_ref[:, n * c : n * c + n] = t_ref[c, :, :n].astype(jnp.float32)
+        out_ref[c] = t_ref[c, :, n:].astype(jnp.float32)
+
+
+def spread_feed(t):
+    _, rows, columns = t.shape
+    n = columns // 2
+    f = jnp.float32
+    return pl.pallas_call(
+        spread_feed_kernel,
+        grid=(8,),
+        in_specs=[pl.BlockSpec((2, rows, columns), lambda b: (pair_at(b), 0, 0))],
+        out_specs=[
+            pl.BlockSpec((rows, 2 * n), lambda b: (b, 0)),
+            pl.BlockSpec((2, rows, n), lambda b: (0, b, 0)),
+        ],
+        out_shape=[
+            jax.ShapeDtypeStruct((8 * rows, 2 * n), f),
+            jax.ShapeDtypeStruct((2, 8 * rows, n), f),
+        ],
+        compiler_params=pltpu.CompilerParams(vmem_limit_bytes=32 << 20),
+        name="spread_feed",
+        cost_estimate=pl.CostEstimate(flops=0, bytes_accessed=6 * t.size, transcendentals=0),
+    )(t)
+
+
+def spread_rest_kernel(t_ref, *refs):
+    cq, co, so, ck, cv, tw, q, k, v, tb = refs
+    n = cq.shape[1] // 2
+    b = pl.program_id(0)
+
+    def both(i):
+        return jnp.concatenate(
+            [t_ref[c, :, n * i : n * i + n].astype(jnp.float32) for c in range(2)], 1
+        )
+
+    for i, ref in ((0, cq), (3, ck), (4, cv), (6, q), (7, k), (8, v)):
+        ref[...] = both(i)
+    co[...] = jnp.transpose(both(1))
+    so[...] = jnp.transpose(both(2))
+
+    @pl.when(b < 6)
+    def _():
+        tw[...] = both(5)
+
+    @pl.when(b == 6)
+    def _():
+        tb[...] = both(5)[0:8]
+
+
+def spread_rest(t, n):
+    rows = t.shape[1]
+    f = jnp.float32
+    wide = pl.BlockSpec((rows, 2 * n), lambda b: (b, 0))
+    turned = pl.BlockSpec((2 * n, rows), lambda b: (0, b))
+    square = jax.ShapeDtypeStruct((8 * rows, 2 * n), f)
+    tall = jax.ShapeDtypeStruct((2 * n, 8 * rows), f)
+    return pl.pallas_call(
+        spread_rest_kernel,
+        grid=(8,),
+        in_specs=[pl.BlockSpec((2,) + t.shape[1:], lambda b: (pair_at(b), 0, 0))],
+        out_specs=[wide, turned, turned, wide, wide, pl.BlockSpec((rows, 2 * n), lambda b: (jnp.minimum(b, 5), 0))]
+        + [wide] * 3
+        + [pl.BlockSpec((8, 2 * n), lambda b: (0, 0))],
+        out_shape=[square, tall, tall, square, square, jax.ShapeDtypeStruct((6 * rows, 2 * n), f)]
+        + [square] * 3
+        + [jax.ShapeDtypeStruct((8, 2 * n), f)],
+        compiler_params=pltpu.CompilerParams(vmem_limit_bytes=32 << 20),
+        name="spread_rest",
+        cost_estimate=pl.CostEstimate(flops=0, bytes_accessed=6 * t.size, transcendentals=0),
+    )(t)
+
+
 class Journey:
     def __init__(self, hops):
         self.hops = hops
@@ -984,6 +1023,7 @@
 
 
 def onward(main, *journeys):
+    journeys = [j for j in journeys if j.result is None]
     main, tied = lax.optimization_barrier((main, [j.pending for j in journeys]))
     for journey, sent in zip(journeys, tied):
         journey.go(sent)
@@ -1053,12 +1093,7 @@
             kept, sent = parts_of(terms, step)
             sent = yield sent
             terms = (kept, over_bit(sent, step))
-        block = add(*terms)
-        for step in reversed(steps):
-            block = yield block
-            block = ordered((me // step) % 2 == 0, block, over_bit(block, step), 0)
-        block = yield block
-        return block, over_core(block)
+        return add(*terms)
 
     def travel_y(own, other):
         other = yield other
@@ -1228,11 +1263,19 @@
         vec,
     )
     small = Journey(travel_small(sums[:4]))
-    (g_c, grad_q, g_s, grad_ctx, grad_k, grad_v) = onward(
-        (g_c, grad_q, g_s, grad_ctx, grad_k, grad_v), j_out[0], j_out[1], small
-    )
-
     side = width
+
+    def split_heads_back(t):
+        oc, tc, od, td = [t[:, side // 2 * n : side // 2 * (n + 1)] for n in range(4)]
+        return ordered(core == 0, oc, od, 1), ordered(core == 0, tc, td, 1)
+
+    dk_own, dk_other = split_heads_back(grad_k)
+    dv_own, dv_other = split_heads_back(grad_v)
+    g_c, text_hop = tie((g_c, jnp.concatenate([dk_other, dv_other], 1)))
+    text_hop = over_y(text_hop)
+    (g_c, grad_q, g_s, grad_ctx) = onward(
+        (g_c, grad_q, g_s, grad_ctx), j_out[0], j_out[1], small
+    )
 
     def both(big, small):
         out = []
@@ -1253,18 +1296,29 @@
         oc, tc, od, td = [t[:, side // 2 * n : side // 2 * (n + 1)] for n in range(4)]
         return ordered(core == 0, oc, od, 1), ordered(core == 0, tc, td, 1)
 
-    dk_own, dk_other = split_heads_back(grad_k)
-    dv_own, dv_other = split_heads_back(grad_v)
-    came = over_y(jnp.concatenate([dk_other, dv_other], 1))
-    dk = ordered(half == 0, dk_own, came[:, :width], 0)
-    dv = ordered(half == 0, dv_own, came[:, width:], 0)
+    grad_ctx, c_send, text_hop = tie((grad_ctx, c_send, text_hop))
+    c_got = over_core(c_send)
+    dk = ordered(half == 0, dk_own, text_hop[:, :width], 0)
+    dv = ordered(half == 0, dv_own, text_hop[:, width:], 0)
     grad_text = against(dk, cross_key) + against(dv, cross_value)
-    mine = piece(grad_text, half, width, 1)
-    grad_text = (
-        mine + over_y(piece(grad_text, 1 - half, width, 1).astype(bf16)).astype(f32)
-    ).astype(bf16)
+    text_mine = piece(grad_text, half, width, 1)
+    text_hop = piece(grad_text, 1 - half, width, 1).astype(bf16)
+    grad_ctx, text_mine, text_hop = tie((grad_ctx, text_mine, text_hop))
+    text_hop = over_y(text_hop)
+    grad_ctx = onward(grad_ctx, j_in, *j_out, small)
+
+    grads, parts = [None] * 4, [None] * 4
+
+    def back(n, main):
+        grads[n] = group_backward(clip_bounds, qkv[n], ctx[n], main, log[n], n)
+        parts[n] = outer_sum(self_rows, grads[n]).astype(bf16)
+        main, parts[n] = tie((main, parts[n]))
+        return main
+
+    main = back(3, grad_ctx)
+    main, c_got, text_hop = tie((main, c_got, text_hop))
+    grad_text = (text_mine + text_hop.astype(f32)).astype(bf16)
     text_part = against(grad_text, text_weight).astype(bf16)
-    text_grad = text_part.astype(f32) + over_y(text_part).astype(f32)
     tall = text_full.shape[1] - text_states.shape[1]
     text_wide = jnp.concatenate(
         [
@@ -1285,21 +1339,6 @@
         ).astype(bf16)
         for w in (core, 1 - core)
     ]
-
-    grad_ctx, c_send, text_send = tie((grad_ctx, c_send, text_send))
-    c_got, text_got = over_core((c_send, text_send))
-    grad_ctx = onward(grad_ctx, j_in, *j_out, small)
-
-    grads, parts = [None] * 4, [None] * 4
-
-    def back(n, main):
-        grads[n] = group_backward(clip_bounds, qkv[n], ctx[n], main, log[n], n)
-        parts[n] = outer_sum(self_rows, grads[n]).astype(bf16)
-        main, parts[n] = tie((main, parts[n]))
-        return main
-
-    main = back(3, grad_ctx)
-    main, c_got, text_got = tie((main, c_got, text_got))
     c_cut = c_keep[0].shape[1] // 2
     j_wide = [
         Journey(
@@ -1307,26 +1346,33 @@
         )
         for sl in (slice(0, c_cut), slice(c_cut, None))
     ]
+    main, parts[3], text_send = tie((main, parts[3], text_send))
+    td_got, text_got = over_core(parts[3]), over_core(text_send)
+    main = onward(main, j_in, *j_out, j_wide[0], small)
+    main = back(1, main)
+    main, td_got, text_got = tie((main, td_got, text_got))
     j_text = Journey(travel((text_keep, text_got), steps))
-    main, parts[3] = tie((main, parts[3]))
-    td_got = over_core(parts[3])
-    main = onward(main, j_in, *j_out, j_wide[0], j_text, small)
-    main = back(1, main)
-    main, td_got = tie((main, td_got))
     e_cut = parts[1].shape[0] // 2
     other = add(parts[1], td_got)
     main, other = tie((main, other))
     came_1 = over_y(other[:e_cut])
     main = onward(main, j_in, *j_out, j_text, small)
+
+    def gathered(blocks):
+        return lax.all_gather(jnp.concatenate(blocks, 1), "dp", axis=0, tiled=False)
+
     main = back(2, main)
-    main, parts[2], came_1 = tie((main, parts[2], came_1))
+    main, parts[2], came_1, text_part = tie((main, parts[2], came_1, text_part))
     od_got = over_core(parts[2])
-    came_2 = over_y(other[e_cut:])
-    main = onward(main, j_in, *j_out, j_wide[0], j_text)
+    came_2, text_came = over_y(other[e_cut:]), over_y(text_part)
+    main = onward(main, j_wide[0], j_text)
+    main, blocks = tie((main, [j.result for j in (j_in, *j_out)]))
+    feed_sum = gathered(blocks)
     main = back(0, main)
-    main, came_1, came_2, od_got = tie((main, came_1, came_2, od_got))
+    main, came_1, came_2, od_got, text_came = tie((main, came_1, came_2, od_got, text_came))
+    text_grad = text_part.astype(f32) + text_came.astype(f32)
     j_self = Journey(travel((parts[0], od_got, jnp.concatenate([came_1, came_2])), steps))
-    grads = onward(grads, j_in, *j_out, j_wide[0], j_wide[1], j_text, j_self)
+    grads = onward(grads, j_wide[0], j_wide[1], j_text, j_self)
     frames_grad, self_sums = final_grads(frames, g_middle, grads, qkv_w, vec)
     last = Journey(travel_small(self_sums[:2]))
     everything = [j_in, *j_out, *j_wide, j_text, j_self, small, last]
@@ -1335,39 +1381,32 @@
         while journey.result is None:
             journey.go(journey.pending)
     early, late = small.result, last.result
-    everything = None
-
-    def full(result, at, size, axis):
-        mine, theirs = [t[:, at : at + size] for t in result]
-        return ordered(core == 0, mine, theirs, axis).astype(f32)
-
-    n = side // 2
-    wide_sum = [jnp.concatenate([j.result[t] for j in j_wide], 1) for t in range(2)]
-    text_sum, self_sum = j_text.result, j_self.result
-    out_sum = [jnp.concatenate([j.result[t] for j in j_out], 1) for t in range(2)]
-    text_rows_grad = full(text_sum, 2 * n, n, 1)
+    rest_sum = gathered([j.result for j in (*j_wide, j_text, j_self)])
+
+    feed_in_grad, feed_out_grad = spread_feed(feed_sum)
+    cq_g, co_g, so_g, ck_g, cv_g, text_g, q_g, k_g, v_g, bias_g = spread_rest(rest_sum, side // 2)
     return (
         output,
         frames_grad,
         text_grad,
         late[0],
         late[1],
-        full(self_sum, 0, n, 1),
-        full(self_sum, n, n, 1),
-        full(self_sum, 2 * n, n, 1),
-        full(wide_sum, 2 * n, n, 1).T,
+        q_g,
+        k_g,
+        v_g,
+        so_g,
         early[2],
         early[3],
-        full(wide_sum, 0, n, 1),
-        full(text_sum, 0, n, 1),
-        full(text_sum, n, n, 1),
-        full(wide_sum, n, n, 1).T,
-        text_rows_grad[: text_states.shape[1]],
-        text_rows_grad[text_states.shape[1]],
+        cq_g,
+        ck_g,
+        cv_g,
+        co_g,
+        text_g,
+        bias_g[0],
         early[0],
         early[1],
-        full(j_in.result, 0, 2 * NB, 1),
-        ordered(core == 0, *out_sum, 0).astype(f32),
+        feed_in_grad,
+        feed_out_grad.reshape(feed_out.shape),
     )
 
 

time: 832 us -> 743 us (0.89)
  other arithmetic: 109 us -> 66.9 us
  starting transfers between devices: 90.5 us -> 57 us
  waiting for transfers between devices: 187 us -> 164 us
  between operations: 3.36 us -> 16.4 us
    ppermute x82 -> x54, waiting for transfers between devices: 146 us -> 83.8 us  [over_bit(): lax.ppermute(a, 'dp', [(i, i ^ step) for i in range(dp)])]
    all_gather x0 -> x2, waiting for transfers between devices: none -> 53.3 us  [gathered(): return lax.all_gather(jnp.concatenate(blocks, 1), 'dp', axis=0, tiled=False)]
    ppermute x82 -> x54, starting transfers between devices: 67.7 us -> 35.3 us  [over_bit(): lax.ppermute(a, 'dp', [(i, i ^ step) for i in range(dp)])]
    pallas_call x4, Pallas kernels: 167 us -> 145 us  [feed_part(): pl.pallas_call(functools.partial(feed_kernel, own=own, first=first, last=...]
    convert_element_type x10 -> x1, other arithmetic: 18.9 us -> 1.02 us  [row_body(): grad_text = (text_mine + text_hop.astype(f32)).astype(bf16)]
    ppermute x21, waiting for transfers between devices: 41.1 us -> 26.9 us  [over_y(): return jax.tree.map(lambda a: lax.ppermute(a, 'mp', swap), t)]
    pallas_call x0 -> x2, Pallas kernels: none -> 13.1 us  [the longest x1 6.93 us: spread_rest(): pl.pallas_call(spread_rest_kernel, grid=(8,), in_specs=[pl.BlockSpec((2,)...]
    select_n x35 -> x8, other arithmetic: 14.7 us -> 3.48 us  [ordered(): jnp.where(mine_first, mine, theirs)]
  transfers between devices with their start and end apart: 103 -> 77, of which waited for: 33 -> 26; matrix products, arithmetic and copies ran while one was open for 21% -> 18% of each run, Pallas kernels for 41% -> 43%
where the time goes in v3:
time: 743 us; the launch traced here: 739 us
  Pallas kernels  328 us (44%)
  waiting for transfers between devices  164 us (22%)
  other arithmetic  66.9 us (9%)
  starting transfers between devices  57 us (8%)
  local copies, waits for them, and re-layouts  56.4 us (8%)
  matrix products  50.2 us (7%)
  between operations  16.4 us (2%)
    pallas_call x4, Pallas kernels, feed_part(): pl.pallas_call(functools.partial(feed_kernel, own=own, first=first, last=...  145 us
    ppermute x54, waiting for transfers between devices, over_bit(): lax.ppermute(a, 'dp', [(i, i ^ step) for i in range(dp)])  83.8 us
    pallas_call x4, Pallas kernels, group_backward(): pl.pallas_call(self_bwd_kernel, grid=(pairs,), in_specs=[pl.BlockSpec(mem...  57.4 us
    all_gather x2, waiting for transfers between devices, gathered(): return lax.all_gather(jnp.concatenate(blocks, 1), 'dp', axis=0, tiled=False)  53.3 us
    convert_element_type x33, other arithmetic, add(): return reduce(jnp.add, [t.astype(f32) for t in ts]).astype(bf16)  42.1 us
    pallas_call x1, Pallas kernels, mid_backward(): pl.pallas_call(functools.partial(mid_backward_kernel, len(cos)), grid=(n...  35.3 us
    ppermute x54, starting transfers between devices, over_bit(): lax.ppermute(a, 'dp', [(i, i ^ step) for i in range(dp)])  35.3 us
    dot_general x16, matrix products, outer_sum(): lax.dot_general(left_side, right_side, (((0,), (0,)), ((), ())), preferre...  31.4 us
  transfers between devices with their start and end apart: 77, of which 26 were waited for; matrix products, arithmetic and copies ran while one was open for 18% of the time, Pallas kernels for 43%

profile of v3, /device:TPU:0, one launch (start us, length us, event | category | flops | bytes accessed | tf_op | source)
XLA Modules:
  0.0 738.9 jit_solution(5098986889110493363)
XLA Ops:
  58.0 7.7 %self_forward.4 = (bf16[1536,256]{1,0:T(8,128)(2,1)S(1)}, f32[2,2,1536]{2,1,0:T(2,128)S(1)}) custom-call(s32[4]{0:T(128)S(1)} %bitcast.58, bf16[1536,768]{1,0:T(8,128)(2,1)S(1)} %convolution_convert_fusion.3.q_ref.k_ref.v_ref, bf16[1536,768]{1,0:T(8,128)(2,1)S(1)} %convolution_convert_fusion.3.q_ref.k_ref.v_ref, ...), custom_call_target="tpu_custom_call" | custom-call | flops 4831838208 | bytes 3145728 | tf_op jit(solution)/shard_map/self_forward/pallas_call | solution.py:481
  69.2 7.9 %self_forward.5 = (bf16[1536,256]{1,0:T(8,128)(2,1)S(1)}, f32[2,2,1536]{2,1,0:T(2,128)S(1)}) custom-call(s32[4]{0:T(128)S(1)} %bitcast.59, bf16[1536,768]{1,0:T(8,128)(2,1)S(1)} %copy-done.5, bf16[1536,768]{1,0:T(8,128)(2,1)S(1)} %copy-done.5, bf16[1536,768]{1,0:T(8,128)(2,1)S(1)} %copy-done.5), custom_call_target="tpu_custom_call" | custom-call | flops 4831838208 | bytes 3145728 | tf_op jit(solution)/shard_map/self_forward/pallas_call | solution.py:481
  88.8 7.7 %self_forward.6 = (bf16[1536,256]{1,0:T(8,128)(2,1)S(1)}, f32[2,2,1536]{2,1,0:T(2,128)S(1)}) custom-call(s32[4]{0:T(128)S(1)} %bitcast.60, bf16[1536,768]{1,0:T(8,128)(2,1)S(1)} %convolution_convert_fusion.q_ref.k_ref.v_ref, bf16[1536,768]{1,0:T(8,128)(2,1)S(1)} %convolution_convert_fusion.q_ref.k_ref.v_ref, ...), custom_call_target="tpu_custom_call" | custom-call | flops 4831838208 | bytes 3145728 | tf_op jit(solution)/shard_map/self_forward/pallas_call | solution.py:481
  109.2 7.9 %self_forward.7 = (bf16[1536,256]{1,0:T(8,128)(2,1)S(1)}, f32[2,2,1536]{2,1,0:T(2,128)S(1)}) custom-call(s32[4]{0:T(128)S(1)} %bitcast.61, bf16[1536,768]{1,0:T(8,128)(2,1)S(1)} %convolution_convert_fusion.1.q_ref.k_ref.v_ref, bf16[1536,768]{1,0:T(8,128)(2,1)S(1)} %convolution_convert_fusion.1.q_ref.k_ref.v_ref, ...), custom_call_target="tpu_custom_call" | custom-call | flops 4831838208 | bytes 3145728 | tf_op jit(solution)/shard_map/self_forward/pallas_call | solution.py:481
  119.2 27.0 %mid_forward.1 = (f32[1536,1024]{1,0:T(8,128)}, bf16[1536,1024]{1,0:T(8,128)(2,1)}, bf16[1536,1024]{1,0:T(8,128)(2,1)}, bf16[1536,1024]{1,0:T(8,128)(2,1)}, f32[...) custom-call(s32[4]{0:T(128)} %bitcast.62, s32[4]{0:T(128)} %bitcast.81, ...), custom_call_target="tpu_custom_call" | custom-call | flops 19327352832 | bytes 31457280 | tf_op jit(solution)/shard_map/mid_forward/pallas_call | solution.py:633
  148.8 35.1 %feed_first.1 = (f32[1536,1024]{1,0:T(8,128)}, f32[1536,1024]{1,0:T(8,128)}, bf16[1024,1024]{1,0:T(8,128)(2,1)}, bf16[1024,1024]{1,0:T(8,128)(2,1)}) custom-call(s32[2]{0:T(128)} %pad_add_fusion.2.idx_ref, bf16[1536,1024]{1,0:T(8,128)(2,1)} %get-tuple-element.299.fr_ref, bf16[1024,1536]{1,0:T(8,128)(2,1)} %get-tuple-element.300.frt_ref, ...), custom_call_target="tpu_custom_call" | custom-call | flops 19327352832 | bytes 50331648 | tf_op jit(solution)/shard_map/feed_first/pallas_call | solution.py:863
  185.0 36.6 %feed_more.2 = (f32[1536,1024]{1,0:T(8,128)}, f32[1536,1024]{1,0:T(8,128)}, bf16[1024,1024]{1,0:T(8,128)(2,1)}, bf16[1024,1024]{1,0:T(8,128)(2,1)}) custom-call(s32[2]{0:T(128)} %get-tuple-element.570.idx_ref, bf16[1536,1024]{1,0:T(8,128)(2,1)} %get-tuple-element.299.fr_ref, bf16[1024,1536]{1,0:T(8,128)(2,1)} %get-tuple-element.300.frt_ref, ...), custom_call_target="tpu_custom_call" | custom-call | flops 19327352832 | bytes 50331648 | tf_op jit(solution)/shard_map/feed_more/pallas_call | solution.py:863
  228.2 36.8 %feed_more.3 = (f32[1536,1024]{1,0:T(8,128)}, f32[1536,1024]{1,0:T(8,128)}, bf16[1024,1024]{1,0:T(8,128)(2,1)}, bf16[1024,1024]{1,0:T(8,128)(2,1)}) custom-call(s32[2]{0:T(128)} %get-tuple-element.569.idx_ref, bf16[1536,1024]{1,0:T(8,128)(2,1)} %get-tuple-element.299.fr_ref, bf16[1024,1536]{1,0:T(8,128)(2,1)} %get-tuple-element.300.frt_ref, ...), custom_call_target="tpu_custom_call" | custom-call | flops 19327352832 | bytes 50331648 | tf_op jit(solution)/shard_map/feed_more/pallas_call | solution.py:863
  271.5 36.4 %feed_last.1 = (bf16[1536,1024]{1,0:T(8,128)(2,1)}, f32[1536,1024]{1,0:T(8,128)}, bf16[1024,1024]{1,0:T(8,128)(2,1)}, bf16[1024,1024]{1,0:T(8,128)(2,1)}) custom-call(s32[2]{0:T(128)} %get-tuple-element.569.idx_ref, bf16[1536,1024]{1,0:T(8,128)(2,1)} %get-tuple-element.299.fr_ref, bf16[1024,1536]{1,0:T(8,128)(2,1)} %get-tuple-element.300.frt_ref, ...), custom_call_target="tpu_custom_call" | custom-call | flops 19327352832 | bytes 50331648 | tf_op jit(solution)/shard_map/feed_last/pallas_call | solution.py:863
  318.1 35.3 %mid_backward.1 = (bf16[1536,1024]{1,0:T(8,128)(2,1)}, bf16[1536,1024]{1,0:T(8,128)(2,1)}, f32[1536,1024]{1,0:T(8,128)}, bf16[1536,1024]{1,0:T(8,128)(2,1)}, bf1...) custom-call(s32[4]{0:T(128)} %bitcast.63, s32[4]{0:T(128)} %bitcast.82, ...), custom_call_target="tpu_custom_call" | custom-call | flops 32212254720 | bytes 36175872 | tf_op jit(solution)/shard_map/mid_backward/pallas_call | solution.py:752
  397.7 10.0 %collective-permute-done.33 = bf16[1024,512]{1,0:T(8,128)(2,1)S(1)} collective-permute-done((bf16[1024,512]{1,0:T(8,128)(2,1)S(1)}, bf16[1024,512]{1,0:T(8,128)(2,1)S(1)}, u32[]{:S(2)}, u32[]{:S(2)}) %collective-permute-start.33) | collective-permute-done | bytes 1048608 | tf_op jit(solution)/shard_map/ppermute | solution.py:1067
  411.7 14.4 %self_backward.4.refs_3_ = bf16[1536,768]{1,0:T(8,128)(2,1)S(1)} custom-call(s32[4]{0:T(128)S(1)} %bitcast.64, bf16[1536,768]{1,0:T(8,128)(2,1)S(1)} %copy-done.10, bf16[1536,768]{1,0:T(8,128)(2,1)S(1)} %copy-done.10, bf16[1536,768]{1,0:T(8,128)(2,1)S(1)} %copy-done.10, bf16[1536,256]{1,0:T(8,128)(2,1)S(1)} %copy-done.19, ...), custom_call_target="tpu_custom_call" | custom-call | flops 12079595520 | bytes 6291456 | tf_op jit(solution)/shard_map/self_backward/pallas_call | solution.py:494
  461.9 14.6 %self_backward.5.refs_1_ = bf16[1536,768]{1,0:T(8,128)(2,1)S(1)} custom-call(s32[4]{0:T(128)S(1)} %bitcast.65, bf16[1536,768]{1,0:T(8,128)(2,1)S(1)} %copy-done.8, bf16[1536,768]{1,0:T(8,128)(2,1)S(1)} %copy-done.8, bf16[1536,768]{1,0:T(8,128)(2,1)S(1)} %copy-done.8, bf16[1536,256]{1,0:T(8,128)(2,1)S(1)} %copy-done.17, ...), custom_call_target="tpu_custom_call" | custom-call | flops 12079595520 | bytes 6291456 | tf_op jit(solution)/shard_map/self_backward/pallas_call | solution.py:494
  487.4 6.8 collective-permute-done.48
  506.0 14.2 %self_backward.6.refs_2_ = bf16[1536,768]{1,0:T(8,128)(2,1)S(1)} custom-call(s32[4]{0:T(128)S(1)} %bitcast.66, bf16[1536,768]{1,0:T(8,128)(2,1)S(1)} %copy-done.6, bf16[1536,768]{1,0:T(8,128)(2,1)S(1)} %copy-done.6, bf16[1536,768]{1,0:T(8,128)(2,1)S(1)} %copy-done.6, bf16[1536,256]{1,0:T(8,128)(2,1)S(1)} %copy-done.15, ...), custom_call_target="tpu_custom_call" | custom-call | flops 12079595520 | bytes 6291456 | tf_op jit(solution)/shard_map/self_backward/pallas_call | solution.py:494
  535.9 14.3 %self_backward.7.refs_0_ = bf16[1536,768]{1,0:T(8,128)(2,1)S(1)} custom-call(s32[4]{0:T(128)S(1)} %bitcast.67, bf16[1536,768]{1,0:T(8,128)(2,1)S(1)} %convolution_convert_fusion.3.q_ref.k_ref.v_ref, bf16[1536,768]{1,0:T(8,128)(2,1)S(1)} %convolution_convert_fusion.3.q_ref.k_ref.v_ref, bf16[1536,768]{1,0:T(8,128)(2,1)S(1)} %convolution_convert_fusion.3.q_ref.k_ref.v_ref, ...), custom_call_target="tpu_custom_call" | custom-call | flops 12079595520 | bytes 6291456 | tf_op jit(solution)/shard_map/self_backward/pallas_call | solution.py:494
  553.0 8.8 %collective-permute-done.54 = bf16[256,768]{1,0:T(8,128)(2,1)S(1)} collective-permute-done((bf16[256,768]{1,0:T(8,128)(2,1)S(1)}, bf16[256,768]{1,0:T(8,128)(2,1)S(1)}, u32[]{:S(2)}, u32[]{:S(2)}) %collective-permute-start.54) | collective-permute-done | bytes 393248 | tf_op jit(solution)/shard_map/ppermute | solution.py:1070
  565.3 19.0 %frames_gradient.1 = (f32[1536,1024]{1,0:T(8,128)}, f32[8,1024]{1,0:T(8,128)}) custom-call(bf16[1536,1024]{1,0:T(8,128)(2,1)} %x_ref.1, f32[1536,1024]{1,0:T(8,128)} %get-tuple-element.350.gmid_ref, bf16[1536,768]{1,0:T(8,128)(2,1)} %copy-done.23, bf16[1536,768]{1,0:T(8,128)(2,1)} %copy-done.21, bf16[1536,768]{1,0:T(8,128)(2,1)} %copy-done.22, ...), custom_call_target="tpu_custom_call" | custom-call | flops 9663676416 | bytes 18874368 | tf_op jit(solution)/shard_map/frames_gradient/pallas_call | solution.py:920
  587.1 12.0 %collective-permute-done.60 = bf16[512,768]{1,0:T(8,128)(2,1)S(1)} collective-permute-done((bf16[512,768]{1,0:T(8,128)(2,1)S(1)}, bf16[512,768]{1,0:T(8,128)(2,1)S(1)}, u32[]{:S(2)}, u32[]{:S(2)}) %collective-permute-start.60) | collective-permute-done | bytes 786464 | tf_op jit(solution)/shard_map/ppermute | solution.py:1070
  602.0 11.8 %collective-permute-done.68 = bf16[512,384]{0,1:T(8,128)(2,1)S(1)} collective-permute-done((bf16[512,384]{0,1:T(8,128)(2,1)S(1)}, bf16[512,384]{0,1:T(8,128)(2,1)S(1)}, u32[]{:S(2)}, u32[]{:S(2)}) %collective-permute-start.68) | collective-permute-done | bytes 393248 | tf_op jit(solution)/shard_map/ppermute | solution.py:1070
  614.6 10.5 %collective-permute-done.72 = bf16[256,768]{1,0:T(8,128)(2,1)S(1)} collective-permute-done((bf16[256,768]{1,0:T(8,128)(2,1)S(1)}, bf16[256,768]{1,0:T(8,128)(2,1)S(1)}, u32[]{:S(2)}, u32[]{:S(2)}) %collective-permute-start.72) | collective-permute-done | bytes 393248 | tf_op jit(solution)/shard_map/ppermute | solution.py:1070
  626.0 6.9 collective-permute-done.69
  667.3 53.3 %all-gather.5.cloned.1.call-done = bf16[2048,2304]{1,0:T(8,128)(2,1)} async-done(((bf16[128,2304]{1,0:T(8,128)(2,1)}), bf16[2048,2304]{1,0:T(8,128)(2,1)}) %all-gather.5.cloned.1.call-update) | async-done | bytes 9437200 | tf_op jit(solution)/shard_map/all_gather | solution.py:1362
  724.3 6.9 spread_rest.1
  (533 shorter events, 280.6 us)
Async XLA Ops:
  7.2 650.5 %all-gather.7.cloned.1.call-start = ((), (), s32[]{:S(2)}) async-start(), calls=%async_computation.1 | async-start | bytes 8912896 | tf_op jit(solution)/shard_map/all_gather | solution.py:1362
  14.6 36.2 %collective-permute-start.1 = (bf16[256,768]{1,0:T(8,128)(2,1)}, bf16[256,768]{1,0:T(8,128)(2,1)}, u32[]{:S(2)}, u32[]{:S(2)}) collective-permute-start(bf16[256,768]{1,0:T(8,128)(2,1)} %get-tuple-element.244), channel_id=1, source_target_pairs={{0,1},{1,0},{2,3},{3,2},{4,5},{5,4},{6,7},{7,6},{8,9},{9,8},{10,11... | collective-permute-start | bytes 1179656 | tf_op jit(solution)/shard_map/ppermute | solution.py:1067
  17.6 33.2 %collective-permute-start = (bf16[256,512]{1,0:T(8,128)(2,1)}, bf16[256,512]{1,0:T(8,128)(2,1)}, u32[]{:S(2)}, u32[]{:S(2)}) collective-permute-start(bf16[256,512]{1,0:T(8,128)(2,1)} %fusion.40), channel_id=1, source_target_pairs={{0,1},{1,0},{2,3},{3,2},{4,5},{5,4},{6,7},{7,6},{8,9},{9,8},{10,11... | collective-permute-start | bytes 786440 | tf_op jit(solution)/shard_map/ppermute | solution.py:1067
  146.2 37.7 %collective-permute-start.18 = (bf16[1024,512]{1,0:T(8,128)(2,1)}, bf16[1024,512]{1,0:T(8,128)(2,1)}, u32[]{:S(2)}, u32[]{:S(2)}) collective-permute-start(bf16[1024,512]{1,0:T(8,128)(2,1)} %collective-permute-done.16.refs_0_), channel_id=1, source_target_pairs={{0,4},{2,6},{4,0},{6,2},{8,12},{10,14},{12,8},{14,10},{16,20},{18,... | collective-permute-start | bytes 3145736 | tf_op jit(solution)/shard_map/ppermute | solution.py:1070
  147.7 73.8 %collective-permute-start.20 = (bf16[1024,512]{1,0:T(8,128)(2,1)}, bf16[1024,512]{1,0:T(8,128)(2,1)}, u32[]{:S(2)}, u32[]{:S(2)}) collective-permute-start(bf16[1024,512]{1,0:T(8,128)(2,1)} %collective-permute-done.16.refs_0_), channel_id=1, source_target_pairs={{0,2},{2,0},{4,6},{6,4},{8,10},{10,8},{12,14},{14,12},{16,18},{18,... | collective-permute-start | bytes 3145736 | tf_op jit(solution)/shard_map/ppermute | solution.py:1070
  147.8 36.0 %collective-permute-start.17 = (bf16[512,1024]{1,0:T(8,128)(2,1)}, bf16[512,1024]{1,0:T(8,128)(2,1)}, u32[]{:S(2)}, u32[]{:S(2)}) collective-permute-start(bf16[512,1024]{1,0:T(8,128)(2,1)} %constant_dynamic-slice_fusion.2), channel_id=1, source_target_pairs={{0,1},{1,0},{2,3},{3,2},{4,5},{5,4},{6,7},{7,6},{8,9},{9,8},{10,11... | collective-permute-start | bytes 3145736 | tf_op jit(solution)/shard_map/ppermute | solution.py:1067
  183.9 37.7 %collective-permute-start.19 = (bf16[512,1024]{1,0:T(8,128)(2,1)}, bf16[512,1024]{1,0:T(8,128)(2,1)}, u32[]{:S(2)}, u32[]{:S(2)}) collective-permute-start(bf16[512,1024]{1,0:T(8,128)(2,1)} %collective-permute-done.17.refs_2_), channel_id=1, source_target_pairs={{0,4},{2,6},{4,0},{6,2},{8,12},{10,14},{12,8},{14,10},{16,20},{18,... | collective-permute-start | bytes 3145736 | tf_op jit(solution)/shard_map/ppermute | solution.py:1070
  184.5 37.4 %collective-permute-start.22 = (bf16[512,1024]{1,0:T(8,128)(2,1)}, bf16[512,1024]{1,0:T(8,128)(2,1)}, u32[]{:S(2)}, u32[]{:S(2)}) collective-permute-start(bf16[512,1024]{1,0:T(8,128)(2,1)} %collective-permute-done.17.refs_2_), channel_id=1, source_target_pairs={{0,2},{2,0},{4,6},{6,4},{8,10},{10,8},{12,14},{14,12},{16,18},{18,... | collective-permute-start | bytes 3145736 | tf_op jit(solution)/shard_map/ppermute | solution.py:1070
  184.5 37.1 %collective-permute-start.21 = (bf16[1024,512]{1,0:T(8,128)(2,1)}, bf16[1024,512]{1,0:T(8,128)(2,1)}, u32[]{:S(2)}, u32[]{:S(2)}) collective-permute-start(bf16[1024,512]{1,0:T(8,128)(2,1)} %collective-permute-done.18.refs_1_), channel_id=1, source_target_pairs={{0,2},{2,0},{4,6},{6,4},{8,10},{10,8},{12,14},{14,12},{16,18},{18,... | collective-permute-start | bytes 3145736 | tf_op jit(solution)/shard_map/ppermute | solution.py:1070
  224.7 40.4 %collective-permute-start.24 = (bf16[1024,1024]{1,0:T(8,128)(2,1)}, bf16[1024,1024]{1,0:T(8,128)(2,1)}, u32[]{:S(2)}, u32[]{:S(2)}) collective-permute-start(bf16[1024,1024]{1,0:T(8,128)(2,1)} %get-tuple-element.326), channel_id=1, source_target_pairs={{0,2},{2,0},{4,6},{6,4},{8,10},{10,8},{12,14},{14,12},{16,18},{18,... | collective-permute-start | bytes 6291464 | tf_op jit(solution)/shard_map/ppermute | solution.py:1070
  227.8 80.1 %collective-permute-start.28 = (bf16[1024,1024]{1,0:T(8,128)(2,1)}, bf16[1024,1024]{1,0:T(8,128)(2,1)}, u32[]{:S(2)}, u32[]{:S(2)}) collective-permute-start(bf16[1024,1024]{1,0:T(8,128)(2,1)} %get-tuple-element.359), channel_id=1, source_target_pairs={{0,2},{2,0},{4,6},{6,4},{8,10},{10,8},{12,14},{14,12},{16,18},{18,... | collective-permute-start | bytes 6291464 | tf_op jit(solution)/shard_map/ppermute | solution.py:1070
  269.6 41.2 %collective-permute-start.27 = (bf16[512,1024]{1,0:T(8,128)(2,1)}, bf16[512,1024]{1,0:T(8,128)(2,1)}, u32[]{:S(2)}, u32[]{:S(2)}) collective-permute-start(bf16[512,1024]{1,0:T(8,128)(2,1)} %get-tuple-element.339), channel_id=1, source_target_pairs={{0,4},{2,6},{4,0},{6,2},{8,12},{10,14},{12,8},{14,10},{16,20},{18,... | collective-permute-start | bytes 3145736 | tf_op jit(solution)/shard_map/ppermute | solution.py:1070
  271.0 39.7 %collective-permute-start.25 = (bf16[1024,1024]{1,0:T(8,128)(2,1)}, bf16[1024,1024]{1,0:T(8,128)(2,1)}, u32[]{:S(2)}, u32[]{:S(2)}) collective-permute-start(bf16[1024,1024]{1,0:T(8,128)(2,1)} %get-tuple-element.337), channel_id=1, source_target_pairs={{0,2},{2,0},{4,6},{6,4},{8,10},{10,8},{12,14},{14,12},{16,18},{18,... | collective-permute-start | bytes 6291464 | tf_op jit(solution)/shard_map/ppermute | solution.py:1070
  271.0 39.7 %collective-permute-start.26 = (bf16[1024,1024]{1,0:T(8,128)(2,1)}, bf16[1024,1024]{1,0:T(8,128)(2,1)}, u32[]{:S(2)}, u32[]{:S(2)}) collective-permute-start(bf16[1024,1024]{1,0:T(8,128)(2,1)} %get-tuple-element.338), channel_id=1, source_target_pairs={{0,2},{2,0},{4,6},{6,4},{8,10},{10,8},{12,14},{14,12},{16,18},{18,... | collective-permute-start | bytes 6291464 | tf_op jit(solution)/shard_map/ppermute | solution.py:1070
  317.0 40.7 %collective-permute-start.29 = (bf16[1024,512]{1,0:T(8,128)(2,1)}, bf16[1024,512]{1,0:T(8,128)(2,1)}, u32[]{:S(2)}, u32[]{:S(2)}) collective-permute-start(bf16[1024,512]{1,0:T(8,128)(2,1)} %get-tuple-element.360), channel_id=1, source_target_pairs={{0,1},{1,0},{2,3},{3,2},{4,5},{5,4},{6,7},{7,6},{8,9},{9,8},{10,11... | collective-permute-start | bytes 3145736 | tf_op jit(solution)/shard_map/ppermute | solution.py:1067
  356.2 36.0 %collective-permute-start.31 = (bf16[512,1024]{1,0:T(8,128)(2,1)}, bf16[512,1024]{1,0:T(8,128)(2,1)S(1)}, u32[]{:S(2)}, u32[]{:S(2)}) collective-permute-start(bf16[512,1024]{1,0:T(8,128)(2,1)} %add_convert_fusion.5), channel_id=1, source_target_pairs={{0,4},{2,6},{4,0},{6,2},{8,12},{10,14},{12,8},{14,10},{16,20},{18,... | collective-permute-start | bytes 3145736 | tf_op jit(solution)/shard_map/ppermute | solution.py:1070
  387.2 46.3 %collective-permute-start.37 = (bf16[256,512]{1,0:T(8,128)(2,1)}, bf16[256,512]{1,0:T(8,128)(2,1)}, u32[]{:S(2)}, u32[]{:S(2)}) collective-permute-start(bf16[256,512]{1,0:T(8,128)(2,1)} %dynamic-slice_convert_fusion), channel_id=1, source_target_pairs={{0,1},{1,0},{2,3},{3,2},{4,5},{5,4},{6,7},{7,6},{8,9},{9,8},{10,11... | collective-permute-start | bytes 786440 | tf_op jit(solution)/shard_map/ppermute | solution.py:1067
  392.2 41.4 %collective-permute-start.35 = (bf16[1024,768]{0,1:T(8,128)(2,1)}, bf16[1024,768]{0,1:T(8,128)(2,1)}, u32[]{:S(2)}, u32[]{:S(2)}) collective-permute-start(bf16[1024,768]{0,1:T(8,128)(2,1)} %pad_maximum_fusion.3), channel_id=1, source_target_pairs={{0,2},{2,0},{4,6},{6,4},{8,10},{10,8},{12,14},{14,12},{16,18},{18,... | collective-permute-start | bytes 4718600 | tf_op jit(solution)/shard_map/ppermute | solution.py:1070
  395.9 37.7 %collective-permute-start.36 = (bf16[1024,768]{0,1:T(8,128)(2,1)}, bf16[1024,768]{0,1:T(8,128)(2,1)}, u32[]{:S(2)}, u32[]{:S(2)}) collective-permute-start(bf16[1024,768]{0,1:T(8,128)(2,1)} %pad_maximum_fusion.4), channel_id=1, source_target_pairs={{0,2},{2,0},{4,6},{6,4},{8,10},{10,8},{12,14},{14,12},{16,18},{18,... | collective-permute-start | bytes 4718600 | tf_op jit(solution)/shard_map/ppermute | solution.py:1070
  436.2 59.5 %collective-permute-start.42 = (bf16[1024,768]{1,0:T(8,128)(2,1)}, bf16[1024,768]{1,0:T(8,128)(2,1)}, u32[]{:S(2)}, u32[]{:S(2)}) collective-permute-start(bf16[1024,768]{1,0:T(8,128)(2,1)} %convolution_convert_fusion.7), channel_id=1, source_target_pairs={{0,2},{2,0},{4,6},{6,4},{8,10},{10,8},{12,14},{14,12},{16,18},{18,... | collective-permute-start | bytes 4718600 | tf_op jit(solution)/shard_map/ppermute | solution.py:1070
  436.3 59.5 %collective-permute-start.43 = (bf16[1024,768]{1,0:T(8,128)(2,1)}, bf16[1024,768]{1,0:T(8,128)(2,1)}, u32[]{:S(2)}, u32[]{:S(2)}) collective-permute-start(bf16[1024,768]{1,0:T(8,128)(2,1)} %pad_maximum_fusion.5), channel_id=1, source_target_pairs={{0,2},{2,0},{4,6},{6,4},{8,10},{10,8},{12,14},{14,12},{16,18},{18,... | collective-permute-start | bytes 4718600 | tf_op jit(solution)/shard_map/ppermute | solution.py:1070
  528.3 192.3 %all-gather.5.cloned.1.call-start = ((), (), s32[]{:S(2)}) async-start(), calls=%async_computation | async-start | bytes 10027008 | tf_op jit(solution)/shard_map/all_gather | solution.py:1362
  563.4 35.7 %collective-permute-start.60 = (bf16[512,768]{1,0:T(8,128)(2,1)S(1)}, bf16[512,768]{1,0:T(8,128)(2,1)S(1)}, u32[]{:S(2)}, u32[]{:S(2)}) collective-permute-start(bf16[512,768]{1,0:T(8,128)(2,1)S(1)} %get-tuple-element.437), channel_id=1, source_target_pairs={{0,4},{2,6},{4,0},{6,2},{8,12},{10,14},{12,8},{14,10},{16,20},{18,... | collective-permute-start | bytes 2359304 | tf_op jit(solution)/shard_map/ppermute | solution.py:1070
  564.3 35.0 %collective-permute-start.59 = (bf16[1024,384]{0,1:T(8,128)(2,1)S(1)}, bf16[1024,384]{0,1:T(8,128)(2,1)S(1)}, u32[]{:S(2)}, u32[]{:S(2)}) collective-permute-start(bf16[1024,384]{0,1:T(8,128)(2,1)S(1)} %copy-done.64), channel_id=1, source_target_pairs={{0,1},{1,0},{2,3},{3,2},{4,5},{5,4},{6,7},{7,6},{8,9},{9,8},{10,11... | collective-permute-start | bytes 2359304 | tf_op jit(solution)/shard_map/ppermute | solution.py:1067
  (169 other events, 1747.0 us)
Sparse Core Ops, SparseCore 0:
  528.5 103.3 all-gather.6
  639.7 80.8 all-gather.4

commit v4 on v3

--- a/solution.py
+++ b/solution.py
@@ -1286,6 +1286,7 @@
 
     ctx_all = [jnp.concatenate(ctx[:2], 1), jnp.concatenate(ctx[2:], 1)]
     wide = [both(cross_rows, grad_q), both(g_c, cross_ctx)]
+    wide = onward(wide, j_in, *j_out, small)
     so_parts = [outer_sum(g_s, t).astype(bf16) for t in ctx_all]
     wide.append([(t[:, : side // 2], t[:, side // 2 :]) for t in so_parts])
     c_keep, c_send = [
@@ -1305,18 +1306,20 @@
     text_hop = piece(grad_text, 1 - half, width, 1).astype(bf16)
     grad_ctx, text_mine, text_hop = tie((grad_ctx, text_mine, text_hop))
     text_hop = over_y(text_hop)
-    grad_ctx = onward(grad_ctx, j_in, *j_out, small)
 
     grads, parts = [None] * 4, [None] * 4
 
-    def back(n, main):
+    def kernel(n, main):
         grads[n] = group_backward(clip_bounds, qkv[n], ctx[n], main, log[n], n)
+
+    def finish(n, main):
         parts[n] = outer_sum(self_rows, grads[n]).astype(bf16)
         main, parts[n] = tie((main, parts[n]))
         return main
 
-    main = back(3, grad_ctx)
-    main, c_got, text_hop = tie((main, c_got, text_hop))
+    main = grad_ctx
+    kernel(3, main)
+    grads[3], c_got, text_hop = tie((grads[3], c_got, text_hop))
     grad_text = (text_mine + text_hop.astype(f32)).astype(bf16)
     text_part = against(grad_text, text_weight).astype(bf16)
     tall = text_full.shape[1] - text_states.shape[1]
@@ -1346,33 +1349,40 @@
         )
         for sl in (slice(0, c_cut), slice(c_cut, None))
     ]
+    grads[3] = onward(grads[3], j_in, *j_out, j_wide[0], small)
+    main = finish(3, main)
     main, parts[3], text_send = tie((main, parts[3], text_send))
     td_got, text_got = over_core(parts[3]), over_core(text_send)
-    main = onward(main, j_in, *j_out, j_wide[0], small)
-    main = back(1, main)
-    main, td_got, text_got = tie((main, td_got, text_got))
+    kernel(1, main)
+    grads[1], td_got, text_got = tie((grads[1], td_got, text_got))
     j_text = Journey(travel((text_keep, text_got), steps))
+    grads[1] = onward(grads[1], j_in, *j_out, j_text, small)
+    main = finish(1, main)
     e_cut = parts[1].shape[0] // 2
     other = add(parts[1], td_got)
     main, other = tie((main, other))
     came_1 = over_y(other[:e_cut])
-    main = onward(main, j_in, *j_out, j_text, small)
-
     def gathered(blocks):
         return lax.all_gather(jnp.concatenate(blocks, 1), "dp", axis=0, tiled=False)
 
-    main = back(2, main)
-    main, parts[2], came_1, text_part = tie((main, parts[2], came_1, text_part))
+    kernel(2, main)
+    grads[2], came_1, text_part, blocks = tie(
+        (grads[2], came_1, text_part, [j.result for j in (j_in, *j_out)])
+    )
+    feed_sum = gathered(blocks)
+    grads[2] = onward(grads[2], j_wide[0], j_text)
+    main = finish(2, main)
     od_got = over_core(parts[2])
     came_2, text_came = over_y(other[e_cut:]), over_y(text_part)
-    main = onward(main, j_wide[0], j_text)
-    main, blocks = tie((main, [j.result for j in (j_in, *j_out)]))
-    feed_sum = gathered(blocks)
-    main = back(0, main)
-    main, came_1, came_2, od_got, text_came = tie((main, came_1, came_2, od_got, text_came))
+    kernel(0, main)
+    grads[0], came_1, came_2, od_got, text_came = tie(
+        (grads[0], came_1, came_2, od_got, text_came)
+    )
+    grads[0] = onward(grads[0], *j_wide, j_text)
+    main = finish(0, main)
     text_grad = text_part.astype(f32) + text_came.astype(f32)
     j_self = Journey(travel((parts[0], od_got, jnp.concatenate([came_1, came_2])), steps))
-    grads = onward(grads, j_wide[0], j_wide[1], j_text, j_self)
+    grads = onward(grads, j_self)
     frames_grad, self_sums = final_grads(frames, g_middle, grads, qkv_w, vec)
     last = Journey(travel_small(self_sums[:2]))
     everything = [j_in, *j_out, *j_wide, j_text, j_self, small, last]

time: 743 us -> 733 us (0.987)
  waiting for transfers between devices: 164 us -> 148 us
  starting transfers between devices: 57 us -> 71.8 us
  other arithmetic: 66.9 us -> 57.6 us
    ppermute x54, starting transfers between devices: 35.3 us -> 49.4 us  [over_bit(): lax.ppermute(a, 'dp', [(i, i ^ step) for i in range(dp)])]
    ppermute x54, waiting for transfers between devices: 83.8 us -> 73.5 us  [over_bit(): lax.ppermute(a, 'dp', [(i, i ^ step) for i in range(dp)])]
    unnamed x235 -> x215, local copies, waits for them, and re-layouts: 19.2 us -> 22.6 us
  transfers between devices with their start and end apart: 77 -> 77, of which waited for: 26 -> 28; matrix products, arithmetic and copies ran while one was open for 18% -> 17% of each run, Pallas kernels for 43% -> 44%
where the time goes in v4:
time: 733 us; the launch traced here: 729 us
  Pallas kernels  328 us (45%)
  waiting for transfers between devices  148 us (20%)
  starting transfers between devices  71.8 us (10%)
  other arithmetic  57.6 us (8%)
  local copies, waits for them, and re-layouts  56.9 us (8%)
  matrix products  51 us (7%)
  between operations  16.3 us (2%)
    pallas_call x4, Pallas kernels, feed_part(): pl.pallas_call(functools.partial(feed_kernel, own=own, first=first, last=...  145 us
    ppermute x54, waiting for transfers between devices, over_bit(): lax.ppermute(a, 'dp', [(i, i ^ step) for i in range(dp)])  73.5 us
    pallas_call x4, Pallas kernels, group_backward(): pl.pallas_call(self_bwd_kernel, grid=(pairs,), in_specs=[pl.BlockSpec(mem...  57.4 us
    all_gather x2, waiting for transfers between devices, gathered(): return lax.all_gather(jnp.concatenate(blocks, 1), 'dp', axis=0, tiled=False)  52.4 us
    ppermute x54, starting transfers between devices, over_bit(): lax.ppermute(a, 'dp', [(i, i ^ step) for i in range(dp)])  49.4 us
    convert_element_type x33, other arithmetic, add(): return reduce(jnp.add, [t.astype(f32) for t in ts]).astype(bf16)  36.6 us
    pallas_call x1, Pallas kernels, mid_backward(): pl.pallas_call(functools.partial(mid_backward_kernel, len(cos)), grid=(n...  35.3 us
    dot_general x16, matrix products, outer_sum(): lax.dot_general(left_side, right_side, (((0,), (0,)), ((), ())), preferre...  32 us
  transfers between devices with their start and end apart: 77, of which 28 were waited for; matrix products, arithmetic and copies ran while one was open for 17% of the time, Pallas kernels for 44%

profile of v4, /device:TPU:0, one launch (start us, length us, event | category | flops | bytes accessed | tf_op | source)
XLA Modules:
  0.0 729.0 jit_solution(11324285095641871896)
XLA Ops:
  34.3 6.4 convolution_convert_fusion.2.q_ref.k_ref.v_ref
  57.4 7.7 %self_forward.4 = (bf16[1536,256]{1,0:T(8,128)(2,1)S(1)}, f32[2,2,1536]{2,1,0:T(2,128)S(1)}) custom-call(s32[4]{0:T(128)S(1)} %bitcast.58, bf16[1536,768]{1,0:T(8,128)(2,1)S(1)} %convolution_convert_fusion.3.q_ref.k_ref.v_ref, bf16[1536,768]{1,0:T(8,128)(2,1)S(1)} %convolution_convert_fusion.3.q_ref.k_ref.v_ref, ...), custom_call_target="tpu_custom_call" | custom-call | flops 4831838208 | bytes 3145728 | tf_op jit(solution)/shard_map/self_forward/pallas_call | solution.py:481
  68.7 7.9 %self_forward.5 = (bf16[1536,256]{1,0:T(8,128)(2,1)S(1)}, f32[2,2,1536]{2,1,0:T(2,128)S(1)}) custom-call(s32[4]{0:T(128)S(1)} %bitcast.59, bf16[1536,768]{1,0:T(8,128)(2,1)S(1)} %copy-done.5, bf16[1536,768]{1,0:T(8,128)(2,1)S(1)} %copy-done.5, bf16[1536,768]{1,0:T(8,128)(2,1)S(1)} %copy-done.5), custom_call_target="tpu_custom_call" | custom-call | flops 4831838208 | bytes 3145728 | tf_op jit(solution)/shard_map/self_forward/pallas_call | solution.py:481
  88.2 7.7 %self_forward.6 = (bf16[1536,256]{1,0:T(8,128)(2,1)S(1)}, f32[2,2,1536]{2,1,0:T(2,128)S(1)}) custom-call(s32[4]{0:T(128)S(1)} %bitcast.60, bf16[1536,768]{1,0:T(8,128)(2,1)S(1)} %convolution_convert_fusion.q_ref.k_ref.v_ref, bf16[1536,768]{1,0:T(8,128)(2,1)S(1)} %convolution_convert_fusion.q_ref.k_ref.v_ref, ...), custom_call_target="tpu_custom_call" | custom-call | flops 4831838208 | bytes 3145728 | tf_op jit(solution)/shard_map/self_forward/pallas_call | solution.py:481
  108.6 7.9 %self_forward.7 = (bf16[1536,256]{1,0:T(8,128)(2,1)S(1)}, f32[2,2,1536]{2,1,0:T(2,128)S(1)}) custom-call(s32[4]{0:T(128)S(1)} %bitcast.61, bf16[1536,768]{1,0:T(8,128)(2,1)S(1)} %convolution_convert_fusion.1.q_ref.k_ref.v_ref, bf16[1536,768]{1,0:T(8,128)(2,1)S(1)} %convolution_convert_fusion.1.q_ref.k_ref.v_ref, ...), custom_call_target="tpu_custom_call" | custom-call | flops 4831838208 | bytes 3145728 | tf_op jit(solution)/shard_map/self_forward/pallas_call | solution.py:481
  118.6 27.0 %mid_forward.1 = (f32[1536,1024]{1,0:T(8,128)}, bf16[1536,1024]{1,0:T(8,128)(2,1)}, bf16[1536,1024]{1,0:T(8,128)(2,1)}, bf16[1536,1024]{1,0:T(8,128)(2,1)}, f32[...) custom-call(s32[4]{0:T(128)} %bitcast.62, s32[4]{0:T(128)} %bitcast.81, ...), custom_call_target="tpu_custom_call" | custom-call | flops 19327352832 | bytes 31457280 | tf_op jit(solution)/shard_map/mid_forward/pallas_call | solution.py:633
  148.2 35.1 %feed_first.1 = (f32[1536,1024]{1,0:T(8,128)}, f32[1536,1024]{1,0:T(8,128)}, bf16[1024,1024]{1,0:T(8,128)(2,1)}, bf16[1024,1024]{1,0:T(8,128)(2,1)}) custom-call(s32[2]{0:T(128)} %pad_add_fusion.2.idx_ref, bf16[1536,1024]{1,0:T(8,128)(2,1)} %get-tuple-element.306.fr_ref, bf16[1024,1536]{1,0:T(8,128)(2,1)} %get-tuple-element.307.frt_ref, ...), custom_call_target="tpu_custom_call" | custom-call | flops 19327352832 | bytes 50331648 | tf_op jit(solution)/shard_map/feed_first/pallas_call | solution.py:863
  184.4 36.6 %feed_more.2 = (f32[1536,1024]{1,0:T(8,128)}, f32[1536,1024]{1,0:T(8,128)}, bf16[1024,1024]{1,0:T(8,128)(2,1)}, bf16[1024,1024]{1,0:T(8,128)(2,1)}) custom-call(s32[2]{0:T(128)} %get-tuple-element.584.idx_ref, bf16[1536,1024]{1,0:T(8,128)(2,1)} %get-tuple-element.306.fr_ref, bf16[1024,1536]{1,0:T(8,128)(2,1)} %get-tuple-element.307.frt_ref, ...), custom_call_target="tpu_custom_call" | custom-call | flops 19327352832 | bytes 50331648 | tf_op jit(solution)/shard_map/feed_more/pallas_call | solution.py:863
  227.5 36.8 %feed_more.3 = (f32[1536,1024]{1,0:T(8,128)}, f32[1536,1024]{1,0:T(8,128)}, bf16[1024,1024]{1,0:T(8,128)(2,1)}, bf16[1024,1024]{1,0:T(8,128)(2,1)}) custom-call(s32[2]{0:T(128)} %get-tuple-element.583.idx_ref, bf16[1536,1024]{1,0:T(8,128)(2,1)} %get-tuple-element.306.fr_ref, bf16[1024,1536]{1,0:T(8,128)(2,1)} %get-tuple-element.307.frt_ref, ...), custom_call_target="tpu_custom_call" | custom-call | flops 19327352832 | bytes 50331648 | tf_op jit(solution)/shard_map/feed_more/pallas_call | solution.py:863
  270.9 36.4 %feed_last.1 = (bf16[1536,1024]{1,0:T(8,128)(2,1)}, f32[1536,1024]{1,0:T(8,128)}, bf16[1024,1024]{1,0:T(8,128)(2,1)}, bf16[1024,1024]{1,0:T(8,128)(2,1)}) custom-call(s32[2]{0:T(128)} %get-tuple-element.583.idx_ref, bf16[1536,1024]{1,0:T(8,128)(2,1)} %get-tuple-element.306.fr_ref, bf16[1024,1536]{1,0:T(8,128)(2,1)} %get-tuple-element.307.frt_ref, ...), custom_call_target="tpu_custom_call" | custom-call | flops 19327352832 | bytes 50331648 | tf_op jit(solution)/shard_map/feed_last/pallas_call | solution.py:863
  317.6 35.3 %mid_backward.1 = (bf16[1536,1024]{1,0:T(8,128)(2,1)}, bf16[1536,1024]{1,0:T(8,128)(2,1)}, f32[1536,1024]{1,0:T(8,128)}, bf16[1536,1024]{1,0:T(8,128)(2,1)}, bf1...) custom-call(s32[4]{0:T(128)} %bitcast.63, s32[4]{0:T(128)} %bitcast.82, ...), custom_call_target="tpu_custom_call" | custom-call | flops 32212254720 | bytes 36175872 | tf_op jit(solution)/shard_map/mid_backward/pallas_call | solution.py:752
  406.1 14.2 %self_backward.4.refs_3_ = bf16[1536,768]{1,0:T(8,128)(2,1)S(1)} custom-call(s32[4]{0:T(128)S(1)} %bitcast.64, bf16[1536,768]{1,0:T(8,128)(2,1)S(1)} %copy-done.10, bf16[1536,768]{1,0:T(8,128)(2,1)S(1)} %copy-done.10, bf16[1536,768]{1,0:T(8,128)(2,1)S(1)} %copy-done.10, bf16[1536,256]{1,0:T(8,128)(2,1)S(1)} %copy-done.24, ...), custom_call_target="tpu_custom_call" | custom-call | flops 12079595520 | bytes 6291456 | tf_op jit(solution)/shard_map/self_backward/pallas_call | solution.py:494
  449.9 14.6 %self_backward.5.refs_1_ = bf16[1536,768]{1,0:T(8,128)(2,1)S(1)} custom-call(s32[4]{0:T(128)S(1)} %bitcast.65, bf16[1536,768]{1,0:T(8,128)(2,1)S(1)} %copy-done.8, bf16[1536,768]{1,0:T(8,128)(2,1)S(1)} %copy-done.8, bf16[1536,768]{1,0:T(8,128)(2,1)S(1)} %copy-done.8, bf16[1536,256]{1,0:T(8,128)(2,1)S(1)} %copy-done.22, ...), custom_call_target="tpu_custom_call" | custom-call | flops 12079595520 | bytes 6291456 | tf_op jit(solution)/shard_map/self_backward/pallas_call | solution.py:494
  486.6 14.2 %self_backward.6.refs_2_ = bf16[1536,768]{1,0:T(8,128)(2,1)S(1)} custom-call(s32[4]{0:T(128)S(1)} %bitcast.66, bf16[1536,768]{1,0:T(8,128)(2,1)S(1)} %copy-done.6, bf16[1536,768]{1,0:T(8,128)(2,1)S(1)} %copy-done.6, bf16[1536,768]{1,0:T(8,128)(2,1)S(1)} %copy-done.6, bf16[1536,256]{1,0:T(8,128)(2,1)S(1)} %copy-done.20, ...), custom_call_target="tpu_custom_call" | custom-call | flops 12079595520 | bytes 6291456 | tf_op jit(solution)/shard_map/self_backward/pallas_call | solution.py:494
  509.5 11.2 %collective-permute-done.51 = bf16[1024,384]{1,0:T(8,128)(2,1)S(1)} collective-permute-done((bf16[1024,384]{1,0:T(8,128)(2,1)}, bf16[1024,384]{1,0:T(8,128)(2,1)S(1)}, u32[]{:S(2)}, u32[]{:S(2)}) %collective-permute-start.51) | collective-permute-done | bytes 786464 | tf_op jit(solution)/shard_map/ppermute | solution.py:1067
  543.3 14.4 %self_backward.7.refs_0_ = bf16[1536,768]{1,0:T(8,128)(2,1)S(1)} custom-call(s32[4]{0:T(128)S(1)} %bitcast.67, bf16[1536,768]{1,0:T(8,128)(2,1)S(1)} %convolution_convert_fusion.3.q_ref.k_ref.v_ref, bf16[1536,768]{1,0:T(8,128)(2,1)S(1)} %convolution_convert_fusion.3.q_ref.k_ref.v_ref, bf16[1536,768]{1,0:T(8,128)(2,1)S(1)} %convolution_convert_fusion.3.q_ref.k_ref.v_ref, ...), custom_call_target="tpu_custom_call" | custom-call | flops 12079595520 | bytes 6291456 | tf_op jit(solution)/shard_map/self_backward/pallas_call | solution.py:494
  557.7 7.6 %collective-permute-done.57 = bf16[256,768]{1,0:T(8,128)(2,1)S(1)} collective-permute-done((bf16[256,768]{1,0:T(8,128)(2,1)}, bf16[256,768]{1,0:T(8,128)(2,1)S(1)}, u32[]{:S(2)}, u32[]{:S(2)}) %collective-permute-start.57) | collective-permute-done | bytes 393248 | tf_op jit(solution)/shard_map/ppermute | solution.py:1070
  574.7 18.8 %frames_gradient.1 = (f32[1536,1024]{1,0:T(8,128)}, f32[8,1024]{1,0:T(8,128)}) custom-call(bf16[1536,1024]{1,0:T(8,128)(2,1)} %x_ref.1, f32[1536,1024]{1,0:T(8,128)} %get-tuple-element.357.gmid_ref, bf16[1536,768]{1,0:T(8,128)(2,1)} %copy-done.15, bf16[1536,768]{1,0:T(8,128)(2,1)} %copy-done.12, bf16[1536,768]{1,0:T(8,128)(2,1)} %copy-done.13, ...), custom_call_target="tpu_custom_call" | custom-call | flops 9663676416 | bytes 18874368 | tf_op jit(solution)/shard_map/frames_gradient/pallas_call | solution.py:920
  599.9 5.6 collective-permute-done.71
  609.8 7.7 %collective-permute-done.72 = bf16[256,768]{1,0:T(8,128)(2,1)S(1)} collective-permute-done((bf16[256,768]{1,0:T(8,128)(2,1)S(1)}, bf16[256,768]{1,0:T(8,128)(2,1)S(1)}, u32[]{:S(2)}, u32[]{:S(2)}) %collective-permute-start.72) | collective-permute-done | bytes 393248 | tf_op jit(solution)/shard_map/ppermute | solution.py:1070
  620.7 7.7 %collective-permute-done.73 = bf16[128,768]{1,0:T(8,128)(2,1)S(1)} collective-permute-done((bf16[128,768]{1,0:T(8,128)(2,1)S(1)}, bf16[128,768]{1,0:T(8,128)(2,1)S(1)}, u32[]{:S(2)}, u32[]{:S(2)}) %collective-permute-start.73) | collective-permute-done | bytes 196640 | tf_op jit(solution)/shard_map/ppermute | solution.py:1070
  652.1 6.2 spread_feed.1
  658.3 52.4 %all-gather.5.cloned.1.call-done = bf16[2048,2304]{1,0:T(8,128)(2,1)} async-done(((bf16[128,2304]{1,0:T(8,128)(2,1)}), bf16[2048,2304]{1,0:T(8,128)(2,1)}) %all-gather.5.cloned.1.call-update) | async-done | bytes 9437200 | tf_op jit(solution)/shard_map/all_gather | solution.py:1366
  714.4 6.9 spread_rest.1
  (511 shorter events, 286.5 us)
Async XLA Ops:
  7.2 641.4 %all-gather.7.cloned.1.call-start = ((), (), s32[]{:S(2)}) async-start(), calls=%async_computation.1 | async-start | bytes 8912896 | tf_op jit(solution)/shard_map/all_gather | solution.py:1366
  14.0 36.2 %collective-permute-start.1 = (bf16[256,768]{1,0:T(8,128)(2,1)}, bf16[256,768]{1,0:T(8,128)(2,1)}, u32[]{:S(2)}, u32[]{:S(2)}) collective-permute-start(bf16[256,768]{1,0:T(8,128)(2,1)} %get-tuple-element.251), channel_id=1, source_target_pairs={{0,1},{1,0},{2,3},{3,2},{4,5},{5,4},{6,7},{7,6},{8,9},{9,8},{10,11... | collective-permute-start | bytes 1179656 | tf_op jit(solution)/shard_map/ppermute | solution.py:1067
  17.0 33.2 %collective-permute-start = (bf16[256,512]{1,0:T(8,128)(2,1)}, bf16[256,512]{1,0:T(8,128)(2,1)}, u32[]{:S(2)}, u32[]{:S(2)}) collective-permute-start(bf16[256,512]{1,0:T(8,128)(2,1)} %fusion.40), channel_id=1, source_target_pairs={{0,1},{1,0},{2,3},{3,2},{4,5},{5,4},{6,7},{7,6},{8,9},{9,8},{10,11... | collective-permute-start | bytes 786440 | tf_op jit(solution)/shard_map/ppermute | solution.py:1067
  117.4 28.1 %collective-permute-start.16 = (bf16[1024,512]{1,0:T(8,128)(2,1)S(1)}, bf16[1024,512]{1,0:T(8,128)(2,1)}, u32[]{:S(2)}, u32[]{:S(2)}) collective-permute-start(bf16[1024,512]{1,0:T(8,128)(2,1)S(1)} %copy-done.58), channel_id=1, source_target_pairs={{0,1},{1,0},{2,3},{3,2},{4,5},{5,4},{6,7},{7,6},{8,9},{9,8},{10,11... | collective-permute-start | bytes 3145736 | tf_op jit(solution)/shard_map/ppermute | solution.py:1067
  145.6 37.7 %collective-permute-start.18 = (bf16[1024,512]{1,0:T(8,128)(2,1)}, bf16[1024,512]{1,0:T(8,128)(2,1)}, u32[]{:S(2)}, u32[]{:S(2)}) collective-permute-start(bf16[1024,512]{1,0:T(8,128)(2,1)} %collective-permute-done.16.refs_0_), channel_id=1, source_target_pairs={{0,4},{2,6},{4,0},{6,2},{8,12},{10,14},{12,8},{14,10},{16,20},{18,... | collective-permute-start | bytes 3145736 | tf_op jit(solution)/shard_map/ppermute | solution.py:1070
  147.1 73.8 %collective-permute-start.20 = (bf16[1024,512]{1,0:T(8,128)(2,1)}, bf16[1024,512]{1,0:T(8,128)(2,1)}, u32[]{:S(2)}, u32[]{:S(2)}) collective-permute-start(bf16[1024,512]{1,0:T(8,128)(2,1)} %collective-permute-done.16.refs_0_), channel_id=1, source_target_pairs={{0,2},{2,0},{4,6},{6,4},{8,10},{10,8},{12,14},{14,12},{16,18},{18,... | collective-permute-start | bytes 3145736 | tf_op jit(solution)/shard_map/ppermute | solution.py:1070
  147.3 35.9 %collective-permute-start.17 = (bf16[512,1024]{1,0:T(8,128)(2,1)}, bf16[512,1024]{1,0:T(8,128)(2,1)}, u32[]{:S(2)}, u32[]{:S(2)}) collective-permute-start(bf16[512,1024]{1,0:T(8,128)(2,1)} %constant_dynamic-slice_fusion.2), channel_id=1, source_target_pairs={{0,1},{1,0},{2,3},{3,2},{4,5},{5,4},{6,7},{7,6},{8,9},{9,8},{10,11... | collective-permute-start | bytes 3145736 | tf_op jit(solution)/shard_map/ppermute | solution.py:1067
  183.3 37.7 %collective-permute-start.19 = (bf16[512,1024]{1,0:T(8,128)(2,1)}, bf16[512,1024]{1,0:T(8,128)(2,1)}, u32[]{:S(2)}, u32[]{:S(2)}) collective-permute-start(bf16[512,1024]{1,0:T(8,128)(2,1)} %collective-permute-done.17.refs_2_), channel_id=1, source_target_pairs={{0,4},{2,6},{4,0},{6,2},{8,12},{10,14},{12,8},{14,10},{16,20},{18,... | collective-permute-start | bytes 3145736 | tf_op jit(solution)/shard_map/ppermute | solution.py:1070
  183.9 37.4 %collective-permute-start.22 = (bf16[512,1024]{1,0:T(8,128)(2,1)}, bf16[512,1024]{1,0:T(8,128)(2,1)}, u32[]{:S(2)}, u32[]{:S(2)}) collective-permute-start(bf16[512,1024]{1,0:T(8,128)(2,1)} %collective-permute-done.17.refs_2_), channel_id=1, source_target_pairs={{0,2},{2,0},{4,6},{6,4},{8,10},{10,8},{12,14},{14,12},{16,18},{18,... | collective-permute-start | bytes 3145736 | tf_op jit(solution)/shard_map/ppermute | solution.py:1070
  183.9 37.1 %collective-permute-start.21 = (bf16[1024,512]{1,0:T(8,128)(2,1)}, bf16[1024,512]{1,0:T(8,128)(2,1)}, u32[]{:S(2)}, u32[]{:S(2)}) collective-permute-start(bf16[1024,512]{1,0:T(8,128)(2,1)} %collective-permute-done.18.refs_1_), channel_id=1, source_target_pairs={{0,2},{2,0},{4,6},{6,4},{8,10},{10,8},{12,14},{14,12},{16,18},{18,... | collective-permute-start | bytes 3145736 | tf_op jit(solution)/shard_map/ppermute | solution.py:1070
  224.1 40.3 %collective-permute-start.24 = (bf16[1024,1024]{1,0:T(8,128)(2,1)}, bf16[1024,1024]{1,0:T(8,128)(2,1)}, u32[]{:S(2)}, u32[]{:S(2)}) collective-permute-start(bf16[1024,1024]{1,0:T(8,128)(2,1)} %get-tuple-element.333), channel_id=1, source_target_pairs={{0,2},{2,0},{4,6},{6,4},{8,10},{10,8},{12,14},{14,12},{16,18},{18,... | collective-permute-start | bytes 6291464 | tf_op jit(solution)/shard_map/ppermute | solution.py:1070
  227.2 80.2 %collective-permute-start.28 = (bf16[1024,1024]{1,0:T(8,128)(2,1)}, bf16[1024,1024]{1,0:T(8,128)(2,1)}, u32[]{:S(2)}, u32[]{:S(2)}) collective-permute-start(bf16[1024,1024]{1,0:T(8,128)(2,1)} %get-tuple-element.366), channel_id=1, source_target_pairs={{0,2},{2,0},{4,6},{6,4},{8,10},{10,8},{12,14},{14,12},{16,18},{18,... | collective-permute-start | bytes 6291464 | tf_op jit(solution)/shard_map/ppermute | solution.py:1070
  269.0 41.2 %collective-permute-start.27 = (bf16[512,1024]{1,0:T(8,128)(2,1)}, bf16[512,1024]{1,0:T(8,128)(2,1)}, u32[]{:S(2)}, u32[]{:S(2)}) collective-permute-start(bf16[512,1024]{1,0:T(8,128)(2,1)} %get-tuple-element.346), channel_id=1, source_target_pairs={{0,4},{2,6},{4,0},{6,2},{8,12},{10,14},{12,8},{14,10},{16,20},{18,... | collective-permute-start | bytes 3145736 | tf_op jit(solution)/shard_map/ppermute | solution.py:1070
  270.4 39.7 %collective-permute-start.25 = (bf16[1024,1024]{1,0:T(8,128)(2,1)}, bf16[1024,1024]{1,0:T(8,128)(2,1)}, u32[]{:S(2)}, u32[]{:S(2)}) collective-permute-start(bf16[1024,1024]{1,0:T(8,128)(2,1)} %get-tuple-element.344), channel_id=1, source_target_pairs={{0,2},{2,0},{4,6},{6,4},{8,10},{10,8},{12,14},{14,12},{16,18},{18,... | collective-permute-start | bytes 6291464 | tf_op jit(solution)/shard_map/ppermute | solution.py:1070
  270.4 39.7 %collective-permute-start.26 = (bf16[1024,1024]{1,0:T(8,128)(2,1)}, bf16[1024,1024]{1,0:T(8,128)(2,1)}, u32[]{:S(2)}, u32[]{:S(2)}) collective-permute-start(bf16[1024,1024]{1,0:T(8,128)(2,1)} %get-tuple-element.345), channel_id=1, source_target_pairs={{0,2},{2,0},{4,6},{6,4},{8,10},{10,8},{12,14},{14,12},{16,18},{18,... | collective-permute-start | bytes 6291464 | tf_op jit(solution)/shard_map/ppermute | solution.py:1070
  316.4 40.7 %collective-permute-start.29 = (bf16[1024,512]{1,0:T(8,128)(2,1)}, bf16[1024,512]{1,0:T(8,128)(2,1)}, u32[]{:S(2)}, u32[]{:S(2)}) collective-permute-start(bf16[1024,512]{1,0:T(8,128)(2,1)} %get-tuple-element.367), channel_id=1, source_target_pairs={{0,1},{1,0},{2,3},{3,2},{4,5},{5,4},{6,7},{7,6},{8,9},{9,8},{10,11... | collective-permute-start | bytes 3145736 | tf_op jit(solution)/shard_map/ppermute | solution.py:1067
  356.2 44.3 %collective-permute-start.34 = (bf16[128,1024]{1,0:T(8,128)(2,1)S(1)}, bf16[128,1024]{1,0:T(8,128)(2,1)S(1)}, u32[]{:S(2)}, u32[]{:S(2)}) collective-permute-start(bf16[128,1024]{1,0:T(8,128)(2,1)S(1)} %pad_maximum_fusion.22), channel_id=1, source_target_pairs={{0,1},{1,0},{2,3},{3,2},{4,5},{5,4},{6,7},{7,6},{8,9},{9,8},{10,11... | collective-permute-start | bytes 786440 | tf_op jit(solution)/shard_map/ppermute | solution.py:1067
  403.2 33.5 %collective-permute-start.35 = (bf16[1024,768]{1,0:T(8,128)(2,1)}, bf16[1024,768]{1,0:T(8,128)(2,1)S(1)}, u32[]{:S(2)}, u32[]{:S(2)}) collective-permute-start(bf16[1024,768]{1,0:T(8,128)(2,1)} %pad_maximum_fusion.3), channel_id=1, source_target_pairs={{0,2},{2,0},{4,6},{6,4},{8,10},{10,8},{12,14},{14,12},{16,18},{18,... | collective-permute-start | bytes 4718600 | tf_op jit(solution)/shard_map/ppermute | solution.py:1070
  403.2 33.5 %collective-permute-start.36 = (bf16[1024,768]{1,0:T(8,128)(2,1)}, bf16[1024,768]{1,0:T(8,128)(2,1)}, u32[]{:S(2)}, u32[]{:S(2)}) collective-permute-start(bf16[1024,768]{1,0:T(8,128)(2,1)} %pad_maximum_fusion.4), channel_id=1, source_target_pairs={{0,2},{2,0},{4,6},{6,4},{8,10},{10,8},{12,14},{14,12},{16,18},{18,... | collective-permute-start | bytes 4718600 | tf_op jit(solution)/shard_map/ppermute | solution.py:1070
  403.8 27.8 %collective-permute-start.40 = (bf16[512,512]{1,0:T(8,128)(2,1)}, bf16[512,512]{1,0:T(8,128)(2,1)S(1)}, u32[]{:S(2)}, u32[]{:S(2)}) collective-permute-start(bf16[512,512]{1,0:T(8,128)(2,1)} %get-tuple-element.395), channel_id=1, source_target_pairs={{0,4},{2,6},{4,0},{6,2},{8,12},{10,14},{12,8},{14,10},{16,20},{18,... | collective-permute-start | bytes 1572872 | tf_op jit(solution)/shard_map/ppermute | solution.py:1070
  447.3 28.2 %collective-permute-start.42 = (bf16[1024,768]{1,0:T(8,128)(2,1)}, bf16[1024,768]{1,0:T(8,128)(2,1)}, u32[]{:S(2)}, u32[]{:S(2)}) collective-permute-start(bf16[1024,768]{1,0:T(8,128)(2,1)} %convolution_convert_fusion.7), channel_id=1, source_target_pairs={{0,2},{2,0},{4,6},{6,4},{8,10},{10,8},{12,14},{14,12},{16,18},{18,... | collective-permute-start | bytes 4718600 | tf_op jit(solution)/shard_map/ppermute | solution.py:1070
  447.4 28.1 %collective-permute-start.43 = (bf16[1024,768]{1,0:T(8,128)(2,1)S(1)}, bf16[1024,768]{1,0:T(8,128)(2,1)S(1)}, u32[]{:S(2)}, u32[]{:S(2)}) collective-permute-start(bf16[1024,768]{1,0:T(8,128)(2,1)S(1)} %pad_maximum_fusion.5), channel_id=1, source_target_pairs={{0,2},{2,0},{4,6},{6,4},{8,10},{10,8},{12,14},{14,12},{16,18},{18,... | collective-permute-start | bytes 4718600 | tf_op jit(solution)/shard_map/ppermute | solution.py:1070
  505.2 205.6 %all-gather.5.cloned.1.call-start = ((), (), s32[]{:S(2)}) async-start(), calls=%async_computation | async-start | bytes 10027008 | tf_op jit(solution)/shard_map/all_gather | solution.py:1366
  532.0 34.6 %collective-permute-start.54 = (bf16[1024,768]{1,0:T(8,128)(2,1)}, bf16[1024,768]{1,0:T(8,128)(2,1)S(1)}, u32[]{:S(2)}, u32[]{:S(2)}) collective-permute-start(bf16[1024,768]{1,0:T(8,128)(2,1)} %convolution_convert_fusion.5), channel_id=1, source_target_pairs={{0,2},{2,0},{4,6},{6,4},{8,10},{10,8},{12,14},{14,12},{16,18},{18,... | collective-permute-start | bytes 4718600 | tf_op jit(solution)/shard_map/ppermute | solution.py:1070
  (159 other events, 1625.1 us)
Sparse Core Ops, SparseCore 0:
  505.3 88.0 all-gather.6
  630.5 80.2 all-gather.4

commit v5 on v4

--- a/solution.py
+++ b/solution.py
@@ -1373,20 +1373,19 @@
     grads[2] = onward(grads[2], j_wide[0], j_text)
     main = finish(2, main)
     od_got = over_core(parts[2])
-    came_2, text_came = over_y(other[e_cut:]), over_y(text_part)
+    came_2 = over_y(other[e_cut:])
     kernel(0, main)
-    grads[0], came_1, came_2, od_got, text_came = tie(
-        (grads[0], came_1, came_2, od_got, text_came)
-    )
+    grads[0], came_1, came_2, od_got = tie((grads[0], came_1, came_2, od_got))
     grads[0] = onward(grads[0], *j_wide, j_text)
     main = finish(0, main)
-    text_grad = text_part.astype(f32) + text_came.astype(f32)
     j_self = Journey(travel((parts[0], od_got, jnp.concatenate([came_1, came_2])), steps))
     grads = onward(grads, j_self)
     frames_grad, self_sums = final_grads(frames, g_middle, grads, qkv_w, vec)
     last = Journey(travel_small(self_sums[:2]))
     everything = [j_in, *j_out, *j_wide, j_text, j_self, small, last]
     frames_grad = onward(frames_grad, *[j for j in everything if j.result is None])
+    frames_grad, text_part = tie((frames_grad, text_part))
+    text_grad = text_part.astype(f32) + over_y(text_part).astype(f32)
     for journey in everything:
         while journey.result is None:
             journey.go(journey.pending)

time: 733 us -> 728 us (level)
  waiting for transfers between devices: 148 us -> 140 us
    unnamed x215 -> x209, local copies, waits for them, and re-layouts: 22.6 us -> 22.5 us
  transfers between devices with their start and end apart: 77 -> 77, of which waited for: 28 -> 26; matrix products, arithmetic and copies ran while one was open for 17% -> 17% of each run, Pallas kernels for 44% -> 44%
where the time goes in v5:
time: 728 us; the launch traced here: 724 us
  Pallas kernels  328 us (45%)
  waiting for transfers between devices  140 us (19%)
  starting transfers between devices  75.3 us (10%)
  local copies, waits for them, and re-layouts  56.8 us (8%)
  other arithmetic  56.8 us (8%)
  matrix products  51 us (7%)
  between operations  16.3 us (2%)
    pallas_call x4, Pallas kernels, feed_part(): pl.pallas_call(functools.partial(feed_kernel, own=own, first=first, last=...  145 us
    ppermute x54, waiting for transfers between devices, over_bit(): lax.ppermute(a, 'dp', [(i, i ^ step) for i in range(dp)])  69.2 us
    pallas_call x4, Pallas kernels, group_backward(): pl.pallas_call(self_bwd_kernel, grid=(pairs,), in_specs=[pl.BlockSpec(mem...  57.5 us
    all_gather x2, waiting for transfers between devices, gathered(): return lax.all_gather(jnp.concatenate(blocks, 1), 'dp', axis=0, tiled=False)  51.8 us
    ppermute x54, starting transfers between devices, over_bit(): lax.ppermute(a, 'dp', [(i, i ^ step) for i in range(dp)])  51.4 us
    convert_element_type x33, other arithmetic, add(): return reduce(jnp.add, [t.astype(f32) for t in ts]).astype(bf16)  35.8 us
    pallas_call x1, Pallas kernels, mid_backward(): pl.pallas_call(functools.partial(mid_backward_kernel, len(cos)), grid=(n...  35.3 us
    dot_general x16, matrix products, outer_sum(): lax.dot_general(left_side, right_side, (((0,), (0,)), ((), ())), preferre...  32 us
  transfers between devices with their start and end apart: 77, of which 26 were waited for; matrix products, arithmetic and copies ran while one was open for 17% of the time, Pallas kernels for 44%

profile of v5, /device:TPU:0, one launch (start us, length us, event | category | flops | bytes accessed | tf_op | source)
XLA Modules:
  0.0 724.1 jit_solution(15098230963739375070)
XLA Ops:
  34.3 6.4 convolution_convert_fusion.2.q_ref.k_ref.v_ref
  57.5 7.7 %self_forward.4 = (bf16[1536,256]{1,0:T(8,128)(2,1)S(1)}, f32[2,2,1536]{2,1,0:T(2,128)S(1)}) custom-call(s32[4]{0:T(128)S(1)} %bitcast.58, bf16[1536,768]{1,0:T(8,128)(2,1)S(1)} %convolution_convert_fusion.3.q_ref.k_ref.v_ref, bf16[1536,768]{1,0:T(8,128)(2,1)S(1)} %convolution_convert_fusion.3.q_ref.k_ref.v_ref, ...), custom_call_target="tpu_custom_call" | custom-call | flops 4831838208 | bytes 3145728 | tf_op jit(solution)/shard_map/self_forward/pallas_call | solution.py:481
  68.7 7.9 %self_forward.5 = (bf16[1536,256]{1,0:T(8,128)(2,1)S(1)}, f32[2,2,1536]{2,1,0:T(2,128)S(1)}) custom-call(s32[4]{0:T(128)S(1)} %bitcast.59, bf16[1536,768]{1,0:T(8,128)(2,1)S(1)} %copy-done.5, bf16[1536,768]{1,0:T(8,128)(2,1)S(1)} %copy-done.5, bf16[1536,768]{1,0:T(8,128)(2,1)S(1)} %copy-done.5), custom_call_target="tpu_custom_call" | custom-call | flops 4831838208 | bytes 3145728 | tf_op jit(solution)/shard_map/self_forward/pallas_call | solution.py:481
  88.3 7.7 %self_forward.6 = (bf16[1536,256]{1,0:T(8,128)(2,1)S(1)}, f32[2,2,1536]{2,1,0:T(2,128)S(1)}) custom-call(s32[4]{0:T(128)S(1)} %bitcast.60, bf16[1536,768]{1,0:T(8,128)(2,1)S(1)} %convolution_convert_fusion.q_ref.k_ref.v_ref, bf16[1536,768]{1,0:T(8,128)(2,1)S(1)} %convolution_convert_fusion.q_ref.k_ref.v_ref, ...), custom_call_target="tpu_custom_call" | custom-call | flops 4831838208 | bytes 3145728 | tf_op jit(solution)/shard_map/self_forward/pallas_call | solution.py:481
  108.6 7.9 %self_forward.7 = (bf16[1536,256]{1,0:T(8,128)(2,1)S(1)}, f32[2,2,1536]{2,1,0:T(2,128)S(1)}) custom-call(s32[4]{0:T(128)S(1)} %bitcast.61, bf16[1536,768]{1,0:T(8,128)(2,1)S(1)} %convolution_convert_fusion.1.q_ref.k_ref.v_ref, bf16[1536,768]{1,0:T(8,128)(2,1)S(1)} %convolution_convert_fusion.1.q_ref.k_ref.v_ref, ...), custom_call_target="tpu_custom_call" | custom-call | flops 4831838208 | bytes 3145728 | tf_op jit(solution)/shard_map/self_forward/pallas_call | solution.py:481
  118.7 27.0 %mid_forward.1 = (f32[1536,1024]{1,0:T(8,128)}, bf16[1536,1024]{1,0:T(8,128)(2,1)}, bf16[1536,1024]{1,0:T(8,128)(2,1)}, bf16[1536,1024]{1,0:T(8,128)(2,1)}, f32[...) custom-call(s32[4]{0:T(128)} %bitcast.62, s32[4]{0:T(128)} %bitcast.81, ...), custom_call_target="tpu_custom_call" | custom-call | flops 19327352832 | bytes 31457280 | tf_op jit(solution)/shard_map/mid_forward/pallas_call | solution.py:633
  148.2 35.1 %feed_first.1 = (f32[1536,1024]{1,0:T(8,128)}, f32[1536,1024]{1,0:T(8,128)}, bf16[1024,1024]{1,0:T(8,128)(2,1)}, bf16[1024,1024]{1,0:T(8,128)(2,1)}) custom-call(s32[2]{0:T(128)} %pad_add_fusion.2.idx_ref, bf16[1536,1024]{1,0:T(8,128)(2,1)} %get-tuple-element.307.fr_ref, bf16[1024,1536]{1,0:T(8,128)(2,1)} %get-tuple-element.308.frt_ref, ...), custom_call_target="tpu_custom_call" | custom-call | flops 19327352832 | bytes 50331648 | tf_op jit(solution)/shard_map/feed_first/pallas_call | solution.py:863
  184.5 36.5 %feed_more.2 = (f32[1536,1024]{1,0:T(8,128)}, f32[1536,1024]{1,0:T(8,128)}, bf16[1024,1024]{1,0:T(8,128)(2,1)}, bf16[1024,1024]{1,0:T(8,128)(2,1)}) custom-call(s32[2]{0:T(128)} %get-tuple-element.586.idx_ref, bf16[1536,1024]{1,0:T(8,128)(2,1)} %get-tuple-element.307.fr_ref, bf16[1024,1536]{1,0:T(8,128)(2,1)} %get-tuple-element.308.frt_ref, ...), custom_call_target="tpu_custom_call" | custom-call | flops 19327352832 | bytes 50331648 | tf_op jit(solution)/shard_map/feed_more/pallas_call | solution.py:863
  227.6 36.8 %feed_more.3 = (f32[1536,1024]{1,0:T(8,128)}, f32[1536,1024]{1,0:T(8,128)}, bf16[1024,1024]{1,0:T(8,128)(2,1)}, bf16[1024,1024]{1,0:T(8,128)(2,1)}) custom-call(s32[2]{0:T(128)} %get-tuple-element.585.idx_ref, bf16[1536,1024]{1,0:T(8,128)(2,1)} %get-tuple-element.307.fr_ref, bf16[1024,1536]{1,0:T(8,128)(2,1)} %get-tuple-element.308.frt_ref, ...), custom_call_target="tpu_custom_call" | custom-call | flops 19327352832 | bytes 50331648 | tf_op jit(solution)/shard_map/feed_more/pallas_call | solution.py:863
  271.0 36.4 %feed_last.1 = (bf16[1536,1024]{1,0:T(8,128)(2,1)}, f32[1536,1024]{1,0:T(8,128)}, bf16[1024,1024]{1,0:T(8,128)(2,1)}, bf16[1024,1024]{1,0:T(8,128)(2,1)}) custom-call(s32[2]{0:T(128)} %get-tuple-element.585.idx_ref, bf16[1536,1024]{1,0:T(8,128)(2,1)} %get-tuple-element.307.fr_ref, bf16[1024,1536]{1,0:T(8,128)(2,1)} %get-tuple-element.308.frt_ref, ...), custom_call_target="tpu_custom_call" | custom-call | flops 19327352832 | bytes 50331648 | tf_op jit(solution)/shard_map/feed_last/pallas_call | solution.py:863
  317.6 35.3 %mid_backward.1 = (bf16[1536,1024]{1,0:T(8,128)(2,1)}, bf16[1536,1024]{1,0:T(8,128)(2,1)}, f32[1536,1024]{1,0:T(8,128)}, bf16[1536,1024]{1,0:T(8,128)(2,1)}, bf1...) custom-call(s32[4]{0:T(128)} %bitcast.63, s32[4]{0:T(128)} %bitcast.82, ...), custom_call_target="tpu_custom_call" | custom-call | flops 32212254720 | bytes 36175872 | tf_op jit(solution)/shard_map/mid_backward/pallas_call | solution.py:752
  406.2 14.2 %self_backward.4.refs_3_ = bf16[1536,768]{1,0:T(8,128)(2,1)S(1)} custom-call(s32[4]{0:T(128)S(1)} %bitcast.64, bf16[1536,768]{1,0:T(8,128)(2,1)S(1)} %copy-done.10, bf16[1536,768]{1,0:T(8,128)(2,1)S(1)} %copy-done.10, bf16[1536,768]{1,0:T(8,128)(2,1)S(1)} %copy-done.10, bf16[1536,256]{1,0:T(8,128)(2,1)S(1)} %copy-done.24, ...), custom_call_target="tpu_custom_call" | custom-call | flops 12079595520 | bytes 6291456 | tf_op jit(solution)/shard_map/self_backward/pallas_call | solution.py:494
  449.9 14.6 %self_backward.5.refs_1_ = bf16[1536,768]{1,0:T(8,128)(2,1)S(1)} custom-call(s32[4]{0:T(128)S(1)} %bitcast.65, bf16[1536,768]{1,0:T(8,128)(2,1)S(1)} %copy-done.8, bf16[1536,768]{1,0:T(8,128)(2,1)S(1)} %copy-done.8, bf16[1536,768]{1,0:T(8,128)(2,1)S(1)} %copy-done.8, bf16[1536,256]{1,0:T(8,128)(2,1)S(1)} %copy-done.22, ...), custom_call_target="tpu_custom_call" | custom-call | flops 12079595520 | bytes 6291456 | tf_op jit(solution)/shard_map/self_backward/pallas_call | solution.py:494
  486.7 14.2 %self_backward.6.refs_2_ = bf16[1536,768]{1,0:T(8,128)(2,1)S(1)} custom-call(s32[4]{0:T(128)S(1)} %bitcast.66, bf16[1536,768]{1,0:T(8,128)(2,1)S(1)} %copy-done.6, bf16[1536,768]{1,0:T(8,128)(2,1)S(1)} %copy-done.6, bf16[1536,768]{1,0:T(8,128)(2,1)S(1)} %copy-done.6, bf16[1536,256]{1,0:T(8,128)(2,1)S(1)} %copy-done.20, ...), custom_call_target="tpu_custom_call" | custom-call | flops 12079595520 | bytes 6291456 | tf_op jit(solution)/shard_map/self_backward/pallas_call | solution.py:494
  509.6 11.2 %collective-permute-done.51 = bf16[1024,384]{1,0:T(8,128)(2,1)S(1)} collective-permute-done((bf16[1024,384]{1,0:T(8,128)(2,1)}, bf16[1024,384]{1,0:T(8,128)(2,1)S(1)}, u32[]{:S(2)}, u32[]{:S(2)}) %collective-permute-start.51) | collective-permute-done | bytes 786464 | tf_op jit(solution)/shard_map/ppermute | solution.py:1067
  521.1 6.2 collective-permute-done.52
  542.5 14.5 %self_backward.7.refs_0_ = bf16[1536,768]{1,0:T(8,128)(2,1)S(1)} custom-call(s32[4]{0:T(128)S(1)} %bitcast.67, bf16[1536,768]{1,0:T(8,128)(2,1)S(1)} %convolution_convert_fusion.3.q_ref.k_ref.v_ref, bf16[1536,768]{1,0:T(8,128)(2,1)S(1)} %convolution_convert_fusion.3.q_ref.k_ref.v_ref, bf16[1536,768]{1,0:T(8,128)(2,1)S(1)} %convolution_convert_fusion.3.q_ref.k_ref.v_ref, ...), custom_call_target="tpu_custom_call" | custom-call | flops 12079595520 | bytes 6291456 | tf_op jit(solution)/shard_map/self_backward/pallas_call | solution.py:494
  557.0 8.2 %collective-permute-done.56 = bf16[256,768]{1,0:T(8,128)(2,1)S(1)} collective-permute-done((bf16[256,768]{1,0:T(8,128)(2,1)}, bf16[256,768]{1,0:T(8,128)(2,1)S(1)}, u32[]{:S(2)}, u32[]{:S(2)}) %collective-permute-start.56) | collective-permute-done | bytes 393248 | tf_op jit(solution)/shard_map/ppermute | solution.py:1070
  573.0 18.6 %frames_gradient.1 = (f32[1536,1024]{1,0:T(8,128)}, f32[8,1024]{1,0:T(8,128)}) custom-call(bf16[1536,1024]{1,0:T(8,128)(2,1)} %x_ref.1, f32[1536,1024]{1,0:T(8,128)} %get-tuple-element.358.gmid_ref, bf16[1536,768]{1,0:T(8,128)(2,1)} %copy-done.15, bf16[1536,768]{1,0:T(8,128)(2,1)} %copy-done.12, bf16[1536,768]{1,0:T(8,128)(2,1)} %copy-done.13, ...), custom_call_target="tpu_custom_call" | custom-call | flops 9663676416 | bytes 18874368 | tf_op jit(solution)/shard_map/frames_gradient/pallas_call | solution.py:920
  592.4 6.0 collective-permute-start.71
  599.6 7.6 %collective-permute-done.71 = bf16[128,768]{1,0:T(8,128)(2,1)S(1)} collective-permute-done((bf16[128,768]{1,0:T(8,128)(2,1)S(1)}, bf16[128,768]{1,0:T(8,128)(2,1)S(1)}, u32[]{:S(2)}, u32[]{:S(2)}) %collective-permute-start.71) | collective-permute-done | bytes 196640 | tf_op jit(solution)/shard_map/ppermute | solution.py:1070
  647.8 6.2 spread_feed.1
  654.0 51.8 %all-gather.5.cloned.1.call-done = bf16[2048,2304]{1,0:T(8,128)(2,1)} async-done(((bf16[128,2304]{1,0:T(8,128)(2,1)}), bf16[2048,2304]{1,0:T(8,128)(2,1)}) %all-gather.5.cloned.1.call-update) | async-done | bytes 9437200 | tf_op jit(solution)/shard_map/all_gather | solution.py:1366
  709.5 6.9 spread_rest.1
  (505 shorter events, 282.8 us)
Async XLA Ops:
  7.2 637.1 %all-gather.7.cloned.1.call-start = ((), (), s32[]{:S(2)}) async-start(), calls=%async_computation.1 | async-start | bytes 8912896 | tf_op jit(solution)/shard_map/all_gather | solution.py:1366
  14.1 36.2 %collective-permute-start.1 = (bf16[256,768]{1,0:T(8,128)(2,1)}, bf16[256,768]{1,0:T(8,128)(2,1)}, u32[]{:S(2)}, u32[]{:S(2)}) collective-permute-start(bf16[256,768]{1,0:T(8,128)(2,1)} %get-tuple-element.252), channel_id=1, source_target_pairs={{0,1},{1,0},{2,3},{3,2},{4,5},{5,4},{6,7},{7,6},{8,9},{9,8},{10,11... | collective-permute-start | bytes 1179656 | tf_op jit(solution)/shard_map/ppermute | solution.py:1067
  17.0 33.2 %collective-permute-start = (bf16[256,512]{1,0:T(8,128)(2,1)}, bf16[256,512]{1,0:T(8,128)(2,1)}, u32[]{:S(2)}, u32[]{:S(2)}) collective-permute-start(bf16[256,512]{1,0:T(8,128)(2,1)} %fusion.40), channel_id=1, source_target_pairs={{0,1},{1,0},{2,3},{3,2},{4,5},{5,4},{6,7},{7,6},{8,9},{9,8},{10,11... | collective-permute-start | bytes 786440 | tf_op jit(solution)/shard_map/ppermute | solution.py:1067
  117.5 28.1 %collective-permute-start.16 = (bf16[1024,512]{1,0:T(8,128)(2,1)S(1)}, bf16[1024,512]{1,0:T(8,128)(2,1)}, u32[]{:S(2)}, u32[]{:S(2)}) collective-permute-start(bf16[1024,512]{1,0:T(8,128)(2,1)S(1)} %copy-done.57), channel_id=1, source_target_pairs={{0,1},{1,0},{2,3},{3,2},{4,5},{5,4},{6,7},{7,6},{8,9},{9,8},{10,11... | collective-permute-start | bytes 3145736 | tf_op jit(solution)/shard_map/ppermute | solution.py:1067
  145.7 37.6 %collective-permute-start.18 = (bf16[1024,512]{1,0:T(8,128)(2,1)}, bf16[1024,512]{1,0:T(8,128)(2,1)}, u32[]{:S(2)}, u32[]{:S(2)}) collective-permute-start(bf16[1024,512]{1,0:T(8,128)(2,1)} %collective-permute-done.16.refs_0_), channel_id=1, source_target_pairs={{0,4},{2,6},{4,0},{6,2},{8,12},{10,14},{12,8},{14,10},{16,20},{18,... | collective-permute-start | bytes 3145736 | tf_op jit(solution)/shard_map/ppermute | solution.py:1070
  147.2 73.8 %collective-permute-start.20 = (bf16[1024,512]{1,0:T(8,128)(2,1)}, bf16[1024,512]{1,0:T(8,128)(2,1)}, u32[]{:S(2)}, u32[]{:S(2)}) collective-permute-start(bf16[1024,512]{1,0:T(8,128)(2,1)} %collective-permute-done.16.refs_0_), channel_id=1, source_target_pairs={{0,2},{2,0},{4,6},{6,4},{8,10},{10,8},{12,14},{14,12},{16,18},{18,... | collective-permute-start | bytes 3145736 | tf_op jit(solution)/shard_map/ppermute | solution.py:1070
  147.4 35.9 %collective-permute-start.17 = (bf16[512,1024]{1,0:T(8,128)(2,1)}, bf16[512,1024]{1,0:T(8,128)(2,1)}, u32[]{:S(2)}, u32[]{:S(2)}) collective-permute-start(bf16[512,1024]{1,0:T(8,128)(2,1)} %constant_dynamic-slice_fusion.2), channel_id=1, source_target_pairs={{0,1},{1,0},{2,3},{3,2},{4,5},{5,4},{6,7},{7,6},{8,9},{9,8},{10,11... | collective-permute-start | bytes 3145736 | tf_op jit(solution)/shard_map/ppermute | solution.py:1067
  183.3 37.7 %collective-permute-start.19 = (bf16[512,1024]{1,0:T(8,128)(2,1)}, bf16[512,1024]{1,0:T(8,128)(2,1)}, u32[]{:S(2)}, u32[]{:S(2)}) collective-permute-start(bf16[512,1024]{1,0:T(8,128)(2,1)} %collective-permute-done.17.refs_2_), channel_id=1, source_target_pairs={{0,4},{2,6},{4,0},{6,2},{8,12},{10,14},{12,8},{14,10},{16,20},{18,... | collective-permute-start | bytes 3145736 | tf_op jit(solution)/shard_map/ppermute | solution.py:1070
  184.0 37.3 %collective-permute-start.22 = (bf16[512,1024]{1,0:T(8,128)(2,1)}, bf16[512,1024]{1,0:T(8,128)(2,1)}, u32[]{:S(2)}, u32[]{:S(2)}) collective-permute-start(bf16[512,1024]{1,0:T(8,128)(2,1)} %collective-permute-done.17.refs_2_), channel_id=1, source_target_pairs={{0,2},{2,0},{4,6},{6,4},{8,10},{10,8},{12,14},{14,12},{16,18},{18,... | collective-permute-start | bytes 3145736 | tf_op jit(solution)/shard_map/ppermute | solution.py:1070
  184.0 37.1 %collective-permute-start.21 = (bf16[1024,512]{1,0:T(8,128)(2,1)}, bf16[1024,512]{1,0:T(8,128)(2,1)}, u32[]{:S(2)}, u32[]{:S(2)}) collective-permute-start(bf16[1024,512]{1,0:T(8,128)(2,1)} %collective-permute-done.18.refs_1_), channel_id=1, source_target_pairs={{0,2},{2,0},{4,6},{6,4},{8,10},{10,8},{12,14},{14,12},{16,18},{18,... | collective-permute-start | bytes 3145736 | tf_op jit(solution)/shard_map/ppermute | solution.py:1070
  224.1 40.3 %collective-permute-start.24 = (bf16[1024,1024]{1,0:T(8,128)(2,1)}, bf16[1024,1024]{1,0:T(8,128)(2,1)}, u32[]{:S(2)}, u32[]{:S(2)}) collective-permute-start(bf16[1024,1024]{1,0:T(8,128)(2,1)} %get-tuple-element.334), channel_id=1, source_target_pairs={{0,2},{2,0},{4,6},{6,4},{8,10},{10,8},{12,14},{14,12},{16,18},{18,... | collective-permute-start | bytes 6291464 | tf_op jit(solution)/shard_map/ppermute | solution.py:1070
  227.2 80.2 %collective-permute-start.28 = (bf16[1024,1024]{1,0:T(8,128)(2,1)}, bf16[1024,1024]{1,0:T(8,128)(2,1)}, u32[]{:S(2)}, u32[]{:S(2)}) collective-permute-start(bf16[1024,1024]{1,0:T(8,128)(2,1)} %get-tuple-element.367), channel_id=1, source_target_pairs={{0,2},{2,0},{4,6},{6,4},{8,10},{10,8},{12,14},{14,12},{16,18},{18,... | collective-permute-start | bytes 6291464 | tf_op jit(solution)/shard_map/ppermute | solution.py:1070
  269.0 41.2 %collective-permute-start.27 = (bf16[512,1024]{1,0:T(8,128)(2,1)}, bf16[512,1024]{1,0:T(8,128)(2,1)}, u32[]{:S(2)}, u32[]{:S(2)}) collective-permute-start(bf16[512,1024]{1,0:T(8,128)(2,1)} %get-tuple-element.347), channel_id=1, source_target_pairs={{0,4},{2,6},{4,0},{6,2},{8,12},{10,14},{12,8},{14,10},{16,20},{18,... | collective-permute-start | bytes 3145736 | tf_op jit(solution)/shard_map/ppermute | solution.py:1070
  270.5 39.7 %collective-permute-start.25 = (bf16[1024,1024]{1,0:T(8,128)(2,1)}, bf16[1024,1024]{1,0:T(8,128)(2,1)}, u32[]{:S(2)}, u32[]{:S(2)}) collective-permute-start(bf16[1024,1024]{1,0:T(8,128)(2,1)} %get-tuple-element.345), channel_id=1, source_target_pairs={{0,2},{2,0},{4,6},{6,4},{8,10},{10,8},{12,14},{14,12},{16,18},{18,... | collective-permute-start | bytes 6291464 | tf_op jit(solution)/shard_map/ppermute | solution.py:1070
  270.5 39.7 %collective-permute-start.26 = (bf16[1024,1024]{1,0:T(8,128)(2,1)}, bf16[1024,1024]{1,0:T(8,128)(2,1)}, u32[]{:S(2)}, u32[]{:S(2)}) collective-permute-start(bf16[1024,1024]{1,0:T(8,128)(2,1)} %get-tuple-element.346), channel_id=1, source_target_pairs={{0,2},{2,0},{4,6},{6,4},{8,10},{10,8},{12,14},{14,12},{16,18},{18,... | collective-permute-start | bytes 6291464 | tf_op jit(solution)/shard_map/ppermute | solution.py:1070
  316.4 40.7 %collective-permute-start.29 = (bf16[1024,512]{1,0:T(8,128)(2,1)}, bf16[1024,512]{1,0:T(8,128)(2,1)}, u32[]{:S(2)}, u32[]{:S(2)}) collective-permute-start(bf16[1024,512]{1,0:T(8,128)(2,1)} %get-tuple-element.368), channel_id=1, source_target_pairs={{0,1},{1,0},{2,3},{3,2},{4,5},{5,4},{6,7},{7,6},{8,9},{9,8},{10,11... | collective-permute-start | bytes 3145736 | tf_op jit(solution)/shard_map/ppermute | solution.py:1067
  356.3 44.3 %collective-permute-start.34 = (bf16[128,1024]{1,0:T(8,128)(2,1)S(1)}, bf16[128,1024]{1,0:T(8,128)(2,1)S(1)}, u32[]{:S(2)}, u32[]{:S(2)}) collective-permute-start(bf16[128,1024]{1,0:T(8,128)(2,1)S(1)} %pad_maximum_fusion.22), channel_id=1, source_target_pairs={{0,1},{1,0},{2,3},{3,2},{4,5},{5,4},{6,7},{7,6},{8,9},{9,8},{10,11... | collective-permute-start | bytes 786440 | tf_op jit(solution)/shard_map/ppermute | solution.py:1067
  403.3 33.5 %collective-permute-start.35 = (bf16[1024,768]{1,0:T(8,128)(2,1)}, bf16[1024,768]{1,0:T(8,128)(2,1)S(1)}, u32[]{:S(2)}, u32[]{:S(2)}) collective-permute-start(bf16[1024,768]{1,0:T(8,128)(2,1)} %pad_maximum_fusion.3), channel_id=1, source_target_pairs={{0,2},{2,0},{4,6},{6,4},{8,10},{10,8},{12,14},{14,12},{16,18},{18,... | collective-permute-start | bytes 4718600 | tf_op jit(solution)/shard_map/ppermute | solution.py:1070
  403.3 33.5 %collective-permute-start.36 = (bf16[1024,768]{1,0:T(8,128)(2,1)}, bf16[1024,768]{1,0:T(8,128)(2,1)}, u32[]{:S(2)}, u32[]{:S(2)}) collective-permute-start(bf16[1024,768]{1,0:T(8,128)(2,1)} %pad_maximum_fusion.4), channel_id=1, source_target_pairs={{0,2},{2,0},{4,6},{6,4},{8,10},{10,8},{12,14},{14,12},{16,18},{18,... | collective-permute-start | bytes 4718600 | tf_op jit(solution)/shard_map/ppermute | solution.py:1070
  447.3 28.2 %collective-permute-start.42 = (bf16[1024,768]{1,0:T(8,128)(2,1)}, bf16[1024,768]{1,0:T(8,128)(2,1)}, u32[]{:S(2)}, u32[]{:S(2)}) collective-permute-start(bf16[1024,768]{1,0:T(8,128)(2,1)} %convolution_convert_fusion.7), channel_id=1, source_target_pairs={{0,2},{2,0},{4,6},{6,4},{8,10},{10,8},{12,14},{14,12},{16,18},{18,... | collective-permute-start | bytes 4718600 | tf_op jit(solution)/shard_map/ppermute | solution.py:1070
  447.4 28.1 %collective-permute-start.43 = (bf16[1024,768]{1,0:T(8,128)(2,1)S(1)}, bf16[1024,768]{1,0:T(8,128)(2,1)S(1)}, u32[]{:S(2)}, u32[]{:S(2)}) collective-permute-start(bf16[1024,768]{1,0:T(8,128)(2,1)S(1)} %pad_maximum_fusion.5), channel_id=1, source_target_pairs={{0,2},{2,0},{4,6},{6,4},{8,10},{10,8},{12,14},{14,12},{16,18},{18,... | collective-permute-start | bytes 4718600 | tf_op jit(solution)/shard_map/ppermute | solution.py:1070
  505.2 200.6 %all-gather.5.cloned.1.call-start = ((), (), s32[]{:S(2)}) async-start(), calls=%async_computation | async-start | bytes 10027008 | tf_op jit(solution)/shard_map/all_gather | solution.py:1366
  532.1 33.2 %collective-permute-start.54 = (bf16[1024,768]{1,0:T(8,128)(2,1)}, bf16[1024,768]{1,0:T(8,128)(2,1)S(1)}, u32[]{:S(2)}, u32[]{:S(2)}) collective-permute-start(bf16[1024,768]{1,0:T(8,128)(2,1)} %convolution_convert_fusion.5), channel_id=1, source_target_pairs={{0,2},{2,0},{4,6},{6,4},{8,10},{10,8},{12,14},{14,12},{16,18},{18,... | collective-permute-start | bytes 4718600 | tf_op jit(solution)/shard_map/ppermute | solution.py:1070
  570.5 28.0 %collective-permute-start.59 = (bf16[512,768]{1,0:T(8,128)(2,1)S(1)}, bf16[512,768]{1,0:T(8,128)(2,1)S(1)}, u32[]{:S(2)}, u32[]{:S(2)}) collective-permute-start(bf16[512,768]{1,0:T(8,128)(2,1)S(1)} %get-tuple-element.451), channel_id=1, source_target_pairs={{0,4},{2,6},{4,0},{6,2},{8,12},{10,14},{12,8},{14,10},{16,20},{18,... | collective-permute-start | bytes 2359304 | tf_op jit(solution)/shard_map/ppermute | solution.py:1070
  (156 other events, 1574.3 us)
Sparse Core Ops, SparseCore 0:
  505.4 87.6 all-gather.6
  624.8 80.9 all-gather.4
